TPU v7x, 512 devices: a whole 4x4x16 slice. The times are simulated.
512 devices in a mesh: dp: 4 (over x), in: 32 (over z, core), out: 4 (over y).
Axes of the slice: x: 4, y: 4, z: 16, core: 2. Of those that a mesh axis runs over, the one named last changes fastest.
Arguments:
- tokens: bfloat16 [512, 8192], P('dp', 'in'), may hold values from -6 to 6
- cotangent: bfloat16 [512, 8192], P('dp', 'in'), may hold values from -3 to 3
- first_blocks: bfloat16 [32, 4, 5, 256, 256], P('in', 'out'), may hold values from -0.15625 to 0.15625
- second_blocks: bfloat16 [32, 4, 5, 256, 256], P('in', 'out'), may hold values from -0.078125 to 0.078125
- first_left: bfloat16 [8192, 512], P('in'), may hold values from -0.0625 to 0.0625
- first_right: bfloat16 [512, 4, 8192], P(None, 'out', 'in'), may hold values from -0.25 to 0.25
- second_left: bfloat16 [4, 8192, 512], P('out', 'in'), may hold values from -0.03125 to 0.03125
- second_right: bfloat16 [512, 8192], P(None, 'in'), may hold values from -0.25 to 0.25
- strides: int32 [4], replicated, may hold values from 1 to 16, as said below
Outputs:
- output: bfloat16 [512, 8192], P('dp', 'in')
- input_grad: bfloat16 [512, 8192], P('dp', 'in')
- first_blocks_grad: float32 [32, 4, 5, 256, 256], P('in', 'out', None, 'dp')
- second_blocks_grad: float32 [32, 4, 5, 256, 256], P('in', 'out', None, 'dp')
- first_left_grad: float32 [8192, 512], P('in', 'dp')
- first_right_grad: float32 [512, 4, 8192], P('dp', 'out', 'in')
- second_left_grad: float32 [4, 8192, 512], P('out', 'in', 'dp')
- second_right_grad: float32 [512, 8192], P('dp', 'in')
Inputs may be any that keep to these rules, and one draw needn't show every extreme that they name: strides holds 4 distinct powers of two below 32; 16 is always among them.
All inputs are finite; a program needn't handle non-finite values.
Results may differ from a plain program's by a relative error of at most 0.013.
Values may be sent and summed in bfloat16 or wider, within the bound.
No kernel may reach another device: no remote copies, remote signals or barrier semaphores. Data moves between devices by JAX's collectives and lax.ppermute only.
A program may use at most 64 MiB of HBM per device.

v0:
```python
import jax
import jax.numpy as jnp
from jax import lax
from jax.sharding import PartitionSpec as P

root_half = 0.7071067811865476
gauss_norm = 0.3989422804014327


def swapped(block, axis, distance):
    count = lax.axis_size(axis)
    route = []
    for low in range(count):
        high = low | 1 << distance
        if high != low and high < count:
            route += [(low, high), (high, low)]
    return lax.ppermute(block, axis, route)


def normal_cdf(values):
    return 0.5 * (1.0 + lax.erf(values * root_half))


def sum_partners(partials, stride_all, cross_bits):
    block_rows = partials.shape[3]
    positions = jnp.arange(block_rows, dtype=jnp.int32)
    summed = jnp.zeros(partials.shape[1:], jnp.float32)
    for stride_index in range(partials.shape[0]):
        stride_now = stride_all[stride_index]
        shifted = jnp.take(
            partials[stride_index], jnp.bitwise_xor(positions, stride_now % block_rows), axis=2
        )
        summed = summed + jnp.where(stride_now < block_rows, shifted, 0.0)
    for bit_index in range(cross_bits):
        selected = stride_all == block_rows << bit_index
        outgoing = jnp.sum(jnp.where(selected[:, None, None, None, None], partials, 0.0), axis=0)
        summed = summed + swapped(outgoing, "in", bit_index)
    return summed


def fetch_blocks(blocks, stride_all):
    block_rows = blocks.shape[2]
    positions = jnp.arange(block_rows, dtype=jnp.int32)
    picked = []
    gathered = lax.all_gather(blocks, "in", axis=2, tiled=True)
    offset = lax.axis_index("in") * block_rows
    for stride_index in range(stride_all.shape[0]):
        target = jnp.bitwise_xor(offset + positions, stride_all[stride_index])
        picked.append(jnp.take(gathered, target, axis=2))
    return jnp.stack(picked)


def per_device(
    tokens,
    cotangent,
    first_blocks,
    second_blocks,
    first_left,
    first_right,
    second_left,
    second_right,
    strides,
):
    token_count = tokens.shape[0]
    local_rows = first_blocks.shape[0]
    local_periods = first_blocks.shape[1]
    block_size = first_blocks.shape[3]
    width_here = local_rows * block_size
    cross_bits = lax.axis_size("in").bit_length() - 1
    stride_all = jnp.concatenate([jnp.zeros((1,), jnp.int32), strides])
    x_blocks = tokens.reshape(token_count, local_rows, block_size)
    dy_blocks = cotangent.reshape(token_count, local_rows, block_size)
    four_shape = (token_count, local_periods, local_rows, block_size)
    latent_in = lax.psum(
        jnp.dot(tokens, first_left, preferred_element_type=jnp.float32), "in"
    ).astype(jnp.bfloat16)
    first_terms = jnp.einsum(
        "tlb,lpkbc->ktplc", x_blocks, first_blocks, preferred_element_type=jnp.float32
    )
    low_rank = jnp.einsum("tr,rpf->tpf", latent_in, first_right, preferred_element_type=jnp.float32)
    pre_act = sum_partners(first_terms, stride_all, cross_bits) + low_rank.reshape(four_shape)
    cumul = normal_cdf(pre_act)
    hidden = (pre_act * cumul).astype(jnp.bfloat16)
    hidden_flat = hidden.reshape(token_count, local_periods, width_here)
    latent_part = jnp.einsum(
        "tpf,pfr->tr", hidden_flat, second_left, preferred_element_type=jnp.float32
    )
    latent_out = lax.psum(latent_part, ("in", "out")).astype(jnp.bfloat16)
    hidden_near = fetch_blocks(hidden, stride_all)
    block_out = jnp.einsum(
        "ktplb,lpkbc->tlc", hidden_near, second_blocks, preferred_element_type=jnp.float32
    ).reshape(token_count, width_here)
    output = (
        lax.psum(block_out, "out")
        + jnp.dot(latent_out, second_right, preferred_element_type=jnp.float32)
    ).astype(jnp.bfloat16)
    cot_part = jnp.einsum("tc,rc->tr", cotangent, second_right, preferred_element_type=jnp.float32)
    cot_latent = lax.psum(cot_part, "in").astype(jnp.bfloat16)
    second_terms = jnp.einsum(
        "tlc,lpkbc->ktplb", dy_blocks, second_blocks, preferred_element_type=jnp.float32
    )
    back_rank = jnp.einsum(
        "tr,pfr->tpf", cot_latent, second_left, preferred_element_type=jnp.float32
    )
    hidden_grad = sum_partners(second_terms, stride_all, cross_bits) + back_rank.reshape(four_shape)
    slope = cumul + pre_act * jnp.exp(-0.5 * pre_act * pre_act) * gauss_norm
    pre_grad = (hidden_grad * slope).astype(jnp.bfloat16)
    grad_flat = pre_grad.reshape(token_count, local_periods, width_here)
    second_blocks_part = jnp.einsum(
        "ktplb,tlc->lpkbc", hidden_near, dy_blocks, preferred_element_type=jnp.float32
    )
    second_left_part = jnp.einsum(
        "tpf,tr->pfr", hidden_flat, cot_latent, preferred_element_type=jnp.float32
    )
    second_right_part = jnp.einsum(
        "tr,tc->rc", latent_out, cotangent, preferred_element_type=jnp.float32
    )
    hid_part = jnp.einsum("tpf,rpf->tr", grad_flat, first_right, preferred_element_type=jnp.float32)
    hid_latent = lax.psum(hid_part, ("in", "out")).astype(jnp.bfloat16)
    grad_near = fetch_blocks(pre_grad, stride_all)
    block_in = jnp.einsum(
        "ktplc,lpkbc->tlb", grad_near, first_blocks, preferred_element_type=jnp.float32
    ).reshape(token_count, width_here)
    rank_in = jnp.einsum("tr,br->tb", hid_latent, first_left, preferred_element_type=jnp.float32)
    input_grad = (lax.psum(block_in, "out") + rank_in).astype(jnp.bfloat16)
    first_blocks_part = jnp.einsum(
        "tlb,ktplc->lpkbc", x_blocks, grad_near, preferred_element_type=jnp.float32
    )
    first_left_part = jnp.einsum(
        "tb,tr->br", tokens, hid_latent, preferred_element_type=jnp.float32
    )
    first_right_part = jnp.einsum(
        "tr,tpf->rpf", latent_in, grad_flat, preferred_element_type=jnp.float32
    )
    block_done = (
        lax.psum_scatter(
            first_blocks_part.astype(jnp.bfloat16), "dp", scatter_dimension=3, tiled=True
        ).astype(jnp.float32),
        lax.psum_scatter(
            second_blocks_part.astype(jnp.bfloat16), "dp", scatter_dimension=3, tiled=True
        ).astype(jnp.float32),
    )
    factor_done = (
        lax.psum_scatter(first_left_part, "dp", scatter_dimension=1, tiled=True),
        lax.psum_scatter(first_right_part, "dp", scatter_dimension=0, tiled=True),
        lax.psum_scatter(second_left_part, "dp", scatter_dimension=2, tiled=True),
        lax.psum_scatter(second_right_part, "dp", scatter_dimension=0, tiled=True),
    )
    grads = (
        block_done[0],
        block_done[1],
        factor_done[0],
        factor_done[1],
        factor_done[2],
        factor_done[3],
    )
    return (output, input_grad) + tuple(grads)


def solution(mesh):
    in_specs = (
        P("dp", "in"),
        P("dp", "in"),
        P("in", "out", None, None, None),
        P("in", "out", None, None, None),
        P("in", None),
        P(None, "out", "in"),
        P("out", "in", None),
        P(None, "in"),
        P(),
    )
    out_specs = (
        P("dp", "in"),
        P("dp", "in"),
        P("in", "out", None, "dp", None),
        P("in", "out", None, "dp", None),
        P("in", "dp"),
        P("dp", "out", "in"),
        P("out", "in", "dp"),
        P("dp", "in"),
    )
    return jax.shard_map(
        per_device, mesh=mesh, in_specs=in_specs, out_specs=out_specs, check_vma=False
    )
```

profile of v0, /device:TPU:1, one launch (start us, length us, event | category | flops | bytes accessed | tf_op | source)
XLA Modules:
  0.0 864.2 jit_solution(6426506591114025849)
XLA Ops:
  8.1 0.8 broadcast_compare_fusion.3
  8.9 1.4 fusion.4
  10.4 3.6 fusion.7
  14.0 16.4 %collective-permute-start.4 = (f32[128,1,1,256]{0,3,2,1:T(8,128)}, f32[128,1,1,256]{0,3,2,1:T(8,128)S(1)}, u32[]{:S(2)}, u32[]{:S(2)}) collective-permute-start(f32[128,1,1,256]{0,3,2,1:T(8,128)} %bitcast.21), channel_id=1, source_target_pairs={{0,64},{64,0},{4,68},{68,4},{8,72},{72,8},{12,76},{76,12},{16,80},... | collective-permute-start | bytes 393224 | tf_op jit(solution)/shard_map/ppermute | solution.py:17
  30.4 4.0 collective-permute-start.3
  34.4 3.1 collective-permute-start.2
  37.5 2.6 collective-permute-start.1
  40.2 3.7 collective-permute-start
  44.4 92.5 %all-reduce.8 = (bf16[128,512]{1,0:T(8,128)(2,1)S(1)}, bf16[128,512]{1,0:T(8,128)(2,1)S(1)}) all-reduce(f32[128,512]{1,0:T(8,128)S(1)} %fusion.80, f32[128,512]{1,0:T(8,128)S(1)} %fusion.81), channel_id=1, replica_groups=mesh['dp'=4,'in'=32,'out'=4] {'in'}, use_global_device_ids=true, to_apply=%region_5.6 | all-reduce | flops 131072 | bytes 786432 | tf_op jit(solution)/shard_map/psum | solution.py:74
  140.1 7.8 collective-permute-start.9
  148.0 6.2 collective-permute-start.8
  154.2 1.9 collective-permute-start.7
  156.2 3.2 collective-permute-start.6
  159.4 4.8 collective-permute-start.5
  164.2 1.7 multiply_convert_fusion
  165.9 9.5 %collective-permute-done.8 = f32[128,1,1,256]{0,3,2,1:T(8,128)S(1)} collective-permute-done((f32[128,1,1,256]{0,3,2,1:T(8,128)}, f32[128,1,1,256]{0,3,2,1:T(8,128)S(1)}, u32[]{:S(2)}, u32[]{:S(2)}) %collective-permute-start.8) | collective-permute-done | bytes 131104 | tf_op jit(solution)/shard_map/ppermute | solution.py:17
  175.6 0.7 copy.58
  177.7 491.8 %all-reduce.9 = (bf16[128,512]{1,0:T(8,128)(2,1)S(1)}, bf16[128,512]{1,0:T(8,128)(2,1)S(1)}) all-reduce(f32[128,512]{1,0:T(8,128)S(1)} %fusion.20, f32[128,512]{1,0:T(8,128)S(1)} %fusion.22), channel_id=1, replica_groups=mesh['dp'=4,'in'=32,'out'=4] {'in','out'}, use_global_device_ids=true, to_apply=%region_7.9 | all-reduce | flops 131072 | bytes 786432 | tf_op jit(solution)/shard_map/psum | solution.py:88
  669.5 1.0 convolution_bitcast_fusion.2
  673.1 1.1 convolution_bitcast_fusion.1
  674.3 0.9 bitcast_dynamic-update-slice_fusion.4
  675.2 0.9 bitcast_dynamic-update-slice_fusion.8
  676.1 0.9 bitcast_dynamic-update-slice_fusion.3
  676.9 0.9 bitcast_dynamic-update-slice_fusion.7
  677.8 0.9 bitcast_dynamic-update-slice_fusion.2
  678.7 0.9 bitcast_dynamic-update-slice_fusion.6
  679.5 0.9 bitcast_dynamic-update-slice_fusion.1
  680.4 0.9 bitcast_dynamic-update-slice_fusion.5
  681.3 0.9 bitcast_dynamic-update-slice_fusion
  682.1 0.9 convolution_bitcast_fusion.5
  683.0 1.0 convolution_bitcast_fusion.3
  684.5 1.7 copy.65
  686.3 1.2 fusion.1
  687.6 1.0 convolution_bitcast_fusion
  688.7 1.1 fusion.82
  689.8 4.9 reduce-scatter.11.cloned.1.call-done
  694.7 1.7 copy.68
  696.4 30.1 %reduce-scatter.13.cloned.1.call-done = f32[128,1,256]{2,0,1:T(8,128)} async-done(((f32[512,1,256]{2,0,1:T(8,128)}), f32[128,1,256]{2,0,1:T(8,128)}) %reduce-scatter.13.cloned.1.call-update) | async-done | bytes 131088 | tf_op jit(solution)/shard_map/reduce_scatter | solution.py:145
  726.4 1.7 copy.69
  728.1 8.0 all-reduce.7.cloned.1.call-done
  736.1 1.7 fusion.2
  737.8 1.8 fusion.3
  739.6 20.7 %reduce-scatter.7.cloned.1.call-done = bf16[1,1,5,64,256]{4,2,1,0,3:T(8,128)(2,1)} async-done(((bf16[1,1,5,256,256]{4,2,1,0,3:T(8,128)(2,1)}), bf16[1,1,5,64,256]{4,2,1,0,3:T(8,128)(2,1)}) %reduce-scatter.7.cloned.1.call-update) | async-done | bytes 163856 | tf_op jit(solution)/shard_map/reduce_scatter | solution.py:136
  760.3 1.7 copy.67
  762.0 30.6 %reduce-scatter.9.cloned.1.call-done = bf16[1,1,5,64,256]{4,3,2,1,0:T(8,128)(2,1)} async-done(((bf16[1,1,5,256,256]{4,3,2,1,0:T(8,128)(2,1)}), bf16[1,1,5,64,256]{4,3,2,1,0:T(8,128)(2,1)}) %reduce-scatter.9.cloned.1.call-update) | async-done | bytes 163856 | tf_op jit(solution)/shard_map/reduce_scatter | solution.py:139
  792.6 1.7 convert_element_type.67
  794.2 30.1 %reduce-scatter.15.cloned.1.call-done = f32[1,256,128]{2,1,0:T(8,128)} async-done(((f32[1,256,512]{2,1,0:T(8,128)}), f32[1,256,128]{2,1,0:T(8,128)}) %reduce-scatter.15.cloned.1.call-update) | async-done | bytes 131088 | tf_op jit(solution)/shard_map/reduce_scatter | solution.py:146
  824.4 32.7 %reduce-scatter.17.cloned.1.call-done = f32[128,256]{1,0:T(8,128)} async-done(((f32[512,256]{1,0:T(8,128)}), f32[128,256]{1,0:T(8,128)}) %reduce-scatter.17.cloned.1.call-update) | async-done | bytes 131088 | tf_op jit(solution)/shard_map/reduce_scatter | solution.py:147
  (58 shorter events, 3.5 us)
Async XLA Ops:
  8.0 2.3 copy-start
  8.0 666.3 %all-gather.5.cloned.1.call-start = ((), (), s32[]{:S(2)}) async-start(), calls=%async_computation.7 | async-start | bytes 2162688 | tf_op jit(solution)/shard_map/all_gather | solution.py:45
  10.3 33.6 %copy-start.3 = (bf16[256,512]{1,0:T(8,128)(2,1)S(1)}, bf16[256,512]{1,0:T(8,128)(2,1)}, u32[]{:S(2)}) copy-start(bf16[256,512]{1,0:T(8,128)(2,1)} %param.15) | copy-start | bytes 786436
  10.3 33.6 %copy-start.7 = (bf16[128,256]{1,0:T(8,128)(2,1)S(1)}, bf16[128,256]{1,0:T(8,128)(2,1)}, u32[]{:S(2)}) copy-start(bf16[128,256]{1,0:T(8,128)(2,1)} %param.11) | copy-start | bytes 196612
  10.3 33.8 %copy-start.2 = (bf16[512,256]{1,0:T(8,128)(2,1)S(1)}, bf16[512,256]{1,0:T(8,128)(2,1)}, u32[]{:S(2)}) copy-start(bf16[512,256]{1,0:T(8,128)(2,1)} %param.18) | copy-start | bytes 786436
  10.3 33.8 %copy-start.6 = (bf16[128,256]{1,0:T(8,128)(2,1)S(1)}, bf16[128,256]{1,0:T(8,128)(2,1)}, u32[]{:S(2)}) copy-start(bf16[128,256]{1,0:T(8,128)(2,1)} %param.12) | copy-start | bytes 196612
  10.3 126.6 %copy-start.9 = (s32[4]{0:T(128)S(1)}, s32[4]{0:T(128)}, u32[]{:S(2)}) copy-start(s32[4]{0:T(128)} %param.19) | copy-start | bytes 52
  10.3 153.8 %copy-start.5 = (bf16[512,1,256]{2,0,1:T(8,128)(2,1)S(1)}, bf16[512,1,256]{2,0,1:T(8,128)(2,1)}, u32[]{:S(2)}) copy-start(bf16[512,1,256]{2,0,1:T(8,128)(2,1)} %param.16) | copy-start | bytes 786436
  14.0 161.4 %copy-start.4 = (bf16[1,256,512]{2,1,0:T(8,128)(2,1)S(1)}, bf16[1,256,512]{2,1,0:T(8,128)(2,1)}, u32[]{:S(2)}) copy-start(bf16[1,256,512]{2,1,0:T(8,128)(2,1)} %param.17) | copy-start | bytes 786436
  14.0 126.1 %collective-permute-start.4 = (f32[128,1,1,256]{0,3,2,1:T(8,128)}, f32[128,1,1,256]{0,3,2,1:T(8,128)S(1)}, u32[]{:S(2)}, u32[]{:S(2)}) collective-permute-start(f32[128,1,1,256]{0,3,2,1:T(8,128)} %bitcast.21), channel_id=1, source_target_pairs={{0,64},{64,0},{4,68},{68,4},{8,72},{72,8},{12,76},{76,12},{16,80},... | collective-permute-start | bytes 393224 | tf_op jit(solution)/shard_map/ppermute | solution.py:17
  30.4 117.5 %collective-permute-start.3 = (f32[128,1,1,256]{0,3,2,1:T(8,128)}, f32[128,1,1,256]{0,3,2,1:T(8,128)}, u32[]{:S(2)}, u32[]{:S(2)}) collective-permute-start(f32[128,1,1,256]{0,3,2,1:T(8,128)} %bitcast.20), channel_id=1, source_target_pairs={{0,32},{32,0},{4,36},{36,4},{8,40},{40,8},{12,44},{44,12},{16,48},... | collective-permute-start | bytes 393224 | tf_op jit(solution)/shard_map/ppermute | solution.py:17
  34.4 119.8 %collective-permute-start.2 = (f32[128,1,1,256]{0,3,2,1:T(8,128)}, f32[128,1,1,256]{0,3,2,1:T(8,128)}, u32[]{:S(2)}, u32[]{:S(2)}) collective-permute-start(f32[128,1,1,256]{0,3,2,1:T(8,128)} %bitcast.19), channel_id=1, source_target_pairs={{0,16},{16,0},{4,20},{20,4},{8,24},{24,8},{12,28},{28,12},{32,48},... | collective-permute-start | bytes 393224 | tf_op jit(solution)/shard_map/ppermute | solution.py:17
  37.5 118.6 %collective-permute-start.1 = (f32[128,1,1,256]{0,3,2,1:T(8,128)}, f32[128,1,1,256]{0,3,2,1:T(8,128)}, u32[]{:S(2)}, u32[]{:S(2)}) collective-permute-start(f32[128,1,1,256]{0,3,2,1:T(8,128)} %bitcast.18), channel_id=1, source_target_pairs={{0,8},{8,0},{4,12},{12,4},{16,24},{24,16},{20,28},{28,20},{32,40},... | collective-permute-start | bytes 393224 | tf_op jit(solution)/shard_map/ppermute | solution.py:17
  40.2 119.2 %collective-permute-start = (f32[128,1,1,256]{0,3,2,1:T(8,128)}, f32[128,1,1,256]{0,3,2,1:T(8,128)}, u32[]{:S(2)}, u32[]{:S(2)}) collective-permute-start(f32[128,1,1,256]{0,3,2,1:T(8,128)} %bitcast.17), channel_id=1, source_target_pairs={{0,4},{4,0},{8,12},{12,8},{16,20},{20,16},{24,28},{28,24},{32,36},... | collective-permute-start | bytes 393224 | tf_op jit(solution)/shard_map/ppermute | solution.py:17
  140.1 14.1 %copy-start.8 = (f32[128,1,1,256]{0,3,2,1:T(8,128)}, f32[128,1,1,256]{0,3,2,1:T(8,128)S(1)}, u32[]{:S(2)}) copy-start(f32[128,1,1,256]{0,3,2,1:T(8,128)S(1)} %collective-permute-done.4) | copy-start | bytes 393220
  140.1 25.8 %collective-permute-start.9 = (f32[128,1,1,256]{0,3,2,1:T(8,128)}, f32[128,1,1,256]{0,3,2,1:T(8,128)S(1)}, u32[]{:S(2)}, u32[]{:S(2)}) collective-permute-start(f32[128,1,1,256]{0,3,2,1:T(8,128)} %bitcast.259), channel_id=1, source_target_pairs={{0,64},{64,0},{4,68},{68,4},{8,72},{72,8},{12,76},{76,12},{16,80},... | collective-permute-start | bytes 393224 | tf_op jit(solution)/shard_map/ppermute | solution.py:17
  148.0 27.4 %collective-permute-start.8 = (f32[128,1,1,256]{0,3,2,1:T(8,128)}, f32[128,1,1,256]{0,3,2,1:T(8,128)S(1)}, u32[]{:S(2)}, u32[]{:S(2)}) collective-permute-start(f32[128,1,1,256]{0,3,2,1:T(8,128)} %bitcast.258), channel_id=1, source_target_pairs={{0,32},{32,0},{4,36},{36,4},{8,40},{40,8},{12,44},{44,12},{16,48},... | collective-permute-start | bytes 393224 | tf_op jit(solution)/shard_map/ppermute | solution.py:17
  154.2 21.1 %collective-permute-start.7 = (f32[128,1,1,256]{0,3,2,1:T(8,128)}, f32[128,1,1,256]{0,3,2,1:T(8,128)S(1)}, u32[]{:S(2)}, u32[]{:S(2)}) collective-permute-start(f32[128,1,1,256]{0,3,2,1:T(8,128)} %bitcast.257), channel_id=1, source_target_pairs={{0,16},{16,0},{4,20},{20,4},{8,24},{24,8},{12,28},{28,12},{32,48},... | collective-permute-start | bytes 393224 | tf_op jit(solution)/shard_map/ppermute | solution.py:17
  156.2 19.2 %collective-permute-start.6 = (f32[128,1,1,256]{0,3,2,1:T(8,128)}, f32[128,1,1,256]{0,3,2,1:T(8,128)S(1)}, u32[]{:S(2)}, u32[]{:S(2)}) collective-permute-start(f32[128,1,1,256]{0,3,2,1:T(8,128)} %bitcast.256), channel_id=1, source_target_pairs={{0,8},{8,0},{4,12},{12,4},{16,24},{24,16},{20,28},{28,20},{32,40},... | collective-permute-start | bytes 393224 | tf_op jit(solution)/shard_map/ppermute | solution.py:17
  159.4 16.0 %collective-permute-start.5 = (f32[128,1,1,256]{0,3,2,1:T(8,128)}, f32[128,1,1,256]{0,3,2,1:T(8,128)S(1)}, u32[]{:S(2)}, u32[]{:S(2)}) collective-permute-start(f32[128,1,1,256]{0,3,2,1:T(8,128)} %bitcast.255), channel_id=1, source_target_pairs={{0,4},{4,0},{8,12},{12,8},{16,20},{20,16},{24,28},{28,24},{32,36},... | collective-permute-start | bytes 393224 | tf_op jit(solution)/shard_map/ppermute | solution.py:17
  176.4 497.9 %all-gather.3.cloned.1.call-start = ((), (), s32[]{:S(2)}) async-start(), calls=%async_computation.6 | async-start | bytes 2162688 | tf_op jit(solution)/shard_map/all_gather | solution.py:45
  177.2 517.5 %reduce-scatter.11.cloned.1.call-start = ((), (), s32[]{:S(2)}) async-start(), calls=%async_computation.10 | async-start | bytes 655360 | tf_op jit(solution)/shard_map/reduce_scatter | solution.py:144
  177.7 504.4 %copy-start.1 = (bf16[1,1,5,256,256]{4,3,2,1,0:T(8,128)(2,1)S(1)}, bf16[1,1,5,256,256]{4,3,2,1,0:T(8,128)(2,1)}, u32[]{:S(2)}) copy-start(bf16[1,1,5,256,256]{4,3,2,1,0:T(8,128)(2,1)} %param.14) | copy-start | bytes 1966084
  670.5 55.9 %reduce-scatter.13.cloned.1.call-start = ((), (), s32[]{:S(2)}) async-start(), calls=%async_computation.11 | async-start | bytes 655360 | tf_op jit(solution)/shard_map/reduce_scatter | solution.py:145
  674.2 61.9 %all-reduce.7.cloned.1.call-start = ((), (), s32[]{:S(2)}) async-start(), calls=%async_computation.14 | async-start | bytes 524288 | tf_op jit(solution)/shard_map/psum | solution.py:94
  684.1 76.2 %reduce-scatter.7.cloned.1.call-start = ((), (), s32[]{:S(2)}) async-start(), calls=%async_computation.8 | async-start | bytes 1310720 | tf_op jit(solution)/shard_map/reduce_scatter | solution.py:136
  686.3 106.3 %reduce-scatter.9.cloned.1.call-start = ((), (), s32[]{:S(2)}) async-start(), calls=%async_computation.9 | async-start | bytes 819200 | tf_op jit(solution)/shard_map/reduce_scatter | solution.py:139
  687.6 136.8 %reduce-scatter.15.cloned.1.call-start = ((), (), s32[]{:S(2)}) async-start(), calls=%async_computation.12 | async-start | bytes 655360 | tf_op jit(solution)/shard_map/reduce_scatter | solution.py:146
  688.6 168.5 %reduce-scatter.17.cloned.1.call-start = ((), (), s32[]{:S(2)}) async-start(), calls=%async_computation.13 | async-start | bytes 655360 | tf_op jit(solution)/shard_map/reduce_scatter | solution.py:147
Sparse Core Ops, SparseCore 0:
  176.5 69.2 all-gather.4
  248.5 68.8 all-gather.2
  684.2 51.8 all-reduce.6
Sparse Core Ops, SparseCore 1:
  670.6 24.0 reduce-scatter.10
  697.6 28.8 reduce-scatter.12
  729.4 30.9 reduce-scatter.6
  763.2 29.4 reduce-scatter.8
  796.0 28.3 reduce-scatter.14
  827.8 29.3 reduce-scatter.16
where the time goes:
time: 866 us; the launch traced here: 864 us
  blocking collectives  584 us (67%)
  waiting for transfers between devices  167 us (19%)
  starting transfers between devices  54.2 us (6%)
  between operations  20.7 us (2%)
  matrix products  18.9 us (2%)
  other arithmetic  10.2 us (1%)
  local copies, waits for them, and re-layouts  9.01 us (1%)
    psum x1, blocking collectives, per_device(): latent_out = lax.psum(latent_part, ('in', 'out')).astype(jnp.bfloat16)  492 us
    psum x1, blocking collectives, per_device(): lax.psum(jnp.dot(tokens, first_left, preferred_element_type=jnp.float32),...  92.5 us
    ppermute x10, starting transfers between devices, swapped(): return lax.ppermute(block, axis, route)  53.9 us
    reduce_scatter x1, waiting for transfers between devices, per_device(): lax.psum_scatter(second_right_part, 'dp', scatter_dimension=0, tiled=True)  32.7 us
    reduce_scatter x1, waiting for transfers between devices, per_device(): lax.psum_scatter(second_blocks_part.astype(jnp.bfloat16), 'dp', scatter_d...  30.6 us
    reduce_scatter x1, waiting for transfers between devices, per_device(): lax.psum_scatter(second_left_part, 'dp', scatter_dimension=2, tiled=True)  30.1 us
    reduce_scatter x1, waiting for transfers between devices, per_device(): lax.psum_scatter(first_right_part, 'dp', scatter_dimension=0, tiled=True)  30.1 us
    reduce_scatter x1, waiting for transfers between devices, per_device(): lax.psum_scatter(first_blocks_part.astype(jnp.bfloat16), 'dp', scatter_di...  20.7 us
  transfers between devices with their start and end apart: 19, of which 8 were waited for; matrix products, arithmetic and copies ran while one was open for 4% of the time, Pallas kernels for 0%

commit v1 on v0

v1 whole, which is shorter than its diff:
```python
import jax
import jax.numpy as jnp
from jax import lax
from jax.sharding import PartitionSpec as P

root_half = 0.7071067811865476
gauss_norm = 0.3989422804014327
f32 = jnp.float32
bf16 = jnp.bfloat16
BITS = 5


def normal_cdf(values):
    return 0.5 * (1.0 + lax.erf(values * root_half))


def swap_bit(block, bit):
    count = lax.axis_size("in")
    return lax.ppermute(block, "in", [(i, i ^ (1 << bit)) for i in range(count)])


def ring(block, axis, distance):
    count = lax.axis_size(axis)
    return lax.ppermute(block, axis, [(i, (i + distance) % count) for i in range(count)])


def dot(a, b, ca, cb):
    return lax.dot_general(a, b, (((ca,), (cb,)), ((), ())), preferred_element_type=f32)


def pick(stack, index):
    return lax.dynamic_index_in_dim(stack, index, 0, keepdims=False)


def sum_rows(partial, axes):
    group, width = partial.shape
    sent = partial.astype(bf16).reshape(group, width // 128, 128)
    got = lax.all_to_all(sent, axes, 0, 0, tiled=True)
    return jnp.sum(got.astype(f32), axis=0).astype(bf16)


def spread_rows(row, axes, group):
    sent = jnp.broadcast_to(row[None], (group,) + row.shape)
    got = lax.all_to_all(sent, axes, 0, 0, tiled=True)
    return got.reshape(group, row.shape[0] * row.shape[1])


def scatter_dp(parts):
    me = lax.axis_index("dp")
    count = lax.axis_size("dp")
    sent = parts.astype(bf16)
    total = pick(sent, me).astype(f32)
    for distance in range(1, count):
        got = ring(pick(sent, (me + distance) % count), "dp", distance)
        total = total + got.astype(f32)
    return total


def per_device(
    tokens,
    cotangent,
    first_blocks,
    second_blocks,
    first_left,
    first_right,
    second_left,
    second_right,
    strides,
):
    count = tokens.shape[0]
    size = tokens.shape[1]
    rank = first_left.shape[1]
    n_in = lax.axis_size("in")
    n_out = lax.axis_size("out")
    n_dp = lax.axis_size("dp")
    p = lax.axis_index("out")
    w1 = first_blocks[0, 0]
    w2 = second_blocks[0, 0]
    right1 = first_right[:, 0]
    left2 = second_left[0]
    all_axes = ("out", "in")
    group = n_in * n_out
    kcount = w1.shape[0]
    powers = jnp.left_shift(1, jnp.arange(BITS, dtype=jnp.int32))
    match = strides[None, :] == powers[:, None]
    present = jnp.any(match, axis=1)
    k_of_bit = jnp.argmax(match, axis=1) + 1
    bit_of_k = jnp.argmax(match, axis=0)

    first = jnp.einsum("tb,kbc->ktc", tokens, w1, preferred_element_type=f32)
    second = jnp.einsum("tc,kbc->ktb", cotangent, w2, preferred_element_type=f32)
    both = jnp.stack([first, second], axis=1).astype(bf16)
    arrived = [swap_bit(pick(both, k_of_bit[b]), b) for b in range(BITS)]

    share = count // n_out
    x_share = lax.dynamic_slice_in_dim(tokens, p * share, share, 0)
    dy_share = lax.dynamic_slice_in_dim(cotangent, p * share, share, 0)
    part = jnp.concatenate([dot(x_share, first_left, 1, 0), dot(dy_share, second_right, 1, 1)], axis=1)
    latent = spread_rows(sum_rows(part, "in"), all_axes, group)
    a, e = latent[:, :rank], latent[:, rank:]

    z = first[0] + dot(a, right1, 1, 0)
    g = second[0] + dot(e, left2, 1, 1)
    for b in range(BITS):
        got = arrived[b].astype(f32)
        z = z + jnp.where(present[b], got[0], 0.0)
        g = g + jnp.where(present[b], got[1], 0.0)
    cumul = normal_cdf(z)
    h = (z * cumul).astype(bf16)
    slope = cumul + z * jnp.exp(-0.5 * z * z) * gauss_norm
    dz = (g * slope).astype(bf16)

    hd = jnp.stack([h, dz])
    near_bits = jnp.stack([swap_bit(hd, b) for b in range(BITS)])
    near = [hd] + [pick(near_bits, bit_of_k[k]) for k in range(kcount - 1)]

    part = jnp.concatenate([dot(h, left2, 1, 0), dot(dz, right1, 1, 1)], axis=1)
    row = sum_rows(part, all_axes)

    hn = jnp.stack([n[0] for n in near])
    dn = jnp.stack([n[1] for n in near])
    block_out = jnp.einsum("ktb,kbc->tc", hn, w2, preferred_element_type=f32)
    block_in = jnp.einsum("ktc,kbc->tb", dn, w1, preferred_element_type=f32)
    blocks = jnp.stack([block_out, block_in])
    blocks_sent = blocks.astype(bf16)
    for distance in range(1, n_out):
        blocks = blocks + ring(blocks_sent, "out", distance).astype(f32)

    grad1 = jnp.einsum("tb,ktc->kbc", tokens, dn, preferred_element_type=f32)
    grad2 = jnp.einsum("ktb,tc->kbc", hn, cotangent, preferred_element_type=f32)

    def by_dp(grad):
        rows = size // n_dp
        cut = grad.reshape(kcount, n_dp, rows, size)
        return jnp.swapaxes(cut, 0, 1).reshape(n_dp, kcount * rows, size)

    right1_part = dot(a, dz, 0, 0).reshape(n_dp, rank // n_dp, size)
    left2_part = dot(e, h, 0, 0).reshape(n_dp, rank // n_dp, size)
    done = scatter_dp(jnp.concatenate([by_dp(grad1), by_dp(grad2), right1_part, left2_part], axis=1))
    rows = kcount * size // n_dp
    first_blocks_grad = done[:rows].reshape(1, 1, kcount, size // n_dp, size)
    second_blocks_grad = done[rows : 2 * rows].reshape(1, 1, kcount, size // n_dp, size)
    first_right_grad = done[2 * rows : 2 * rows + rank // n_dp][:, None]
    second_left_grad = done[2 * rows + rank // n_dp :].T[None]

    latent = spread_rows(row, all_axes, group)
    c, f = latent[:, :rank], latent[:, rank:]
    output = (blocks[0] + dot(c, second_right, 1, 0)).astype(bf16)
    input_grad = (blocks[1] + dot(f, first_left, 1, 1)).astype(bf16)
    left1_part = dot(f, tokens, 0, 0).reshape(n_dp, rank // n_dp, size)
    right2_part = dot(c, cotangent, 0, 0).reshape(n_dp, rank // n_dp, size)
    sent = jnp.concatenate([left1_part, right2_part], axis=1).astype(bf16)
    got = lax.all_to_all(sent, "dp", 0, 0, tiled=True)
    late = jnp.sum(got.astype(f32), axis=0)
    first_left_grad = late[: rank // n_dp].T
    second_right_grad = late[rank // n_dp :]
    return (
        output,
        input_grad,
        first_blocks_grad,
        second_blocks_grad,
        first_left_grad,
        first_right_grad,
        second_left_grad,
        second_right_grad,
    )


def solution(mesh):
    in_specs = (
        P("dp", "in"),
        P("dp", "in"),
        P("in", "out", None, None, None),
        P("in", "out", None, None, None),
        P("in", None),
        P(None, "out", "in"),
        P("out", "in", None),
        P(None, "in"),
        P(),
    )
    out_specs = (
        P("dp", "in"),
        P("dp", "in"),
        P("in", "out", None, "dp", None),
        P("in", "out", None, "dp", None),
        P("in", "dp"),
        P("dp", "out", "in"),
        P("out", "in", "dp"),
        P("dp", "in"),
    )
    return jax.shard_map(
        per_device, mesh=mesh, in_specs=in_specs, out_specs=out_specs, check_vma=False
    )
```

time: 866 us -> 227 us (0.26)
  blocking collectives: 584 us -> 0 us
  waiting for transfers between devices: 167 us -> 35.7 us
  starting transfers between devices: 54.2 us -> 121 us
    psum x2 -> x0, blocking collectives: 584 us -> none  [the longest x1 492 us: per_device(): latent_out = lax.psum(latent_part, ('in', 'out')).astype(jnp.bfloat16)]
    reduce_scatter x6 -> x0, waiting for transfers between devices: 149 us -> none  [the longest x1 32.7 us: per_device(): lax.psum_scatter(second_right_part, 'dp', scatter_dimension=0, tiled=True)]
    all_to_all x0 -> x5, starting transfers between devices: none -> 56.8 us  [the longest x2 28.8 us: sum_rows(): got = lax.all_to_all(sent, axes, 0, 0, tiled=True)]
    all_to_all x0 -> x5, waiting for transfers between devices: none -> 31.8 us  [the longest x2 16.5 us: spread_rows(): got = lax.all_to_all(sent, axes, 0, 0, tiled=True)]
    ppermute x10 -> x16, starting transfers between devices: 53.9 us -> 63.7 us  [the longest x10 44.1 us: swap_bit(): return lax.ppermute(block, 'in', [(i, i ^ 1 << bit) for i in range(count)])]
  transfers between devices with their start and end apart: 19 -> 21, of which waited for: 8 -> 4; matrix products, arithmetic and copies ran while one was open for 4% -> 14% of each run, Pallas kernels for 0% -> 0%
where the time goes in v1:
time: 227 us; the launch traced here: 224 us
  starting transfers between devices  121 us (53%)
  waiting for transfers between devices  35.7 us (16%)
  between operations  18.9 us (8%)
  matrix products  17.4 us (8%)
  other arithmetic  16.2 us (7%)
  local copies, waits for them, and re-layouts  15.1 us (7%)
    ppermute x10, starting transfers between devices, swap_bit(): return lax.ppermute(block, 'in', [(i, i ^ 1 << bit) for i in range(count)])  44.1 us
    all_to_all x2, starting transfers between devices, sum_rows(): got = lax.all_to_all(sent, axes, 0, 0, tiled=True)  28.8 us
    all_to_all x2, starting transfers between devices, spread_rows(): got = lax.all_to_all(sent, axes, 0, 0, tiled=True)  24.5 us
    ppermute x6, starting transfers between devices, ring(): lax.ppermute(block, axis, [(i, (i + distance) % count) for i in range(cou...  19.7 us
    all_to_all x2, waiting for transfers between devices, spread_rows(): got = lax.all_to_all(sent, axes, 0, 0, tiled=True)  16.5 us
    dot_general x12, matrix products, dot(): lax.dot_general(a, b, (((ca,), (cb,)), ((), ())), preferred_element_type=...  14.3 us
    all_to_all x2, waiting for transfers between devices, sum_rows(): got = lax.all_to_all(sent, axes, 0, 0, tiled=True)  9.98 us
    unnamed x42, local copies, waits for them, and re-layouts  7.89 us
  transfers between devices with their start and end apart: 21, of which 4 were waited for; matrix products, arithmetic and copies ran while one was open for 14% of the time, Pallas kernels for 0%

profile of v1, /device:TPU:1, one launch (start us, length us, event | category | flops | bytes accessed | tf_op | source)
XLA Modules:
  0.0 223.9 jit_solution(730454658644274530)
XLA Ops:
  0.7 1.2 convolution_convert_fusion.9
  1.9 1.1 convolution_convert_fusion.8
  3.7 16.7 %all-to-all-start = ((bf16[32,8,128]{2,1,0:T(8,128)(2,1)}), bf16[32,8,128]{2,1,0:T(8,128)(2,1)S(1)}, u32[]{:S(2)}, u32[]{:S(2)}) async-start(bf16[32,8,128]{2,1,0:T(8,128)(2,1)} %pad_maximum_fusion.5), calls=%async_computation | async-start | bytes 131072 | tf_op jit(solution)/shard_map/all_to_all | solution.py:38
  20.5 1.3 compare_reduce_fusion.1
  21.8 1.5 convolution_bitcast_fusion.1
  23.6 10.0 %all-to-all-done = bf16[32,8,128]{2,1,0:T(8,128)(2,1)S(1)} async-done(((bf16[32,8,128]{2,1,0:T(8,128)(2,1)}), bf16[32,8,128]{2,1,0:T(8,128)(2,1)S(1)}, u32[]{:S(2)}, u32[]{:S(2)}) %all-to-all-start) | async-done | bytes 65568 | tf_op jit(solution)/shard_map/all_to_all | solution.py:38
  34.3 7.5 %all-to-all-start.1 = ((bf16[128,8,128]{2,1,0:T(8,128)(2,1)}), bf16[128,8,128]{2,1,0:T(8,128)(2,1)S(1)}, u32[]{:S(2)}, u32[]{:S(2)}) async-start(bf16[128,8,128]{2,1,0:T(8,128)(2,1)} %broadcast_in_dim.33), calls=%async_computation.1 | async-start | bytes 524288 | tf_op jit(solution)/shard_map/all_to_all | solution.py:44
  53.1 2.9 %collective-permute-start = (bf16[2,128,256]{1,2,0:T(8,128)(2,1)S(1)}, bf16[2,128,256]{1,2,0:T(8,128)(2,1)}, u32[]{:S(2)}, u32[]{:S(2)}) collective-permute-start(bf16[2,128,256]{1,2,0:T(8,128)(2,1)S(1)} %get-tuple-element.61), channel_id=1, source_target_pairs={{0,4},{4,0},{8,12},{12,8},{16,20},{20,16},{24,28},{28,24},{32,36},... | collective-permute-start | bytes 393224 | tf_op jit(solution)/shard_map/ppermute | solution.py:19
  56.0 2.8 %collective-permute-start.1 = (bf16[2,128,256]{1,2,0:T(8,128)(2,1)}, bf16[2,128,256]{1,2,0:T(8,128)(2,1)}, u32[]{:S(2)}, u32[]{:S(2)}) collective-permute-start(bf16[2,128,256]{1,2,0:T(8,128)(2,1)} %get-tuple-element.62), channel_id=1, source_target_pairs={{0,8},{4,12},{8,0},{12,4},{16,24},{20,28},{24,16},{28,20},{32,40},... | collective-permute-start | bytes 393224 | tf_op jit(solution)/shard_map/ppermute | solution.py:19
  58.8 4.0 %collective-permute-start.2 = (bf16[2,128,256]{1,2,0:T(8,128)(2,1)}, bf16[2,128,256]{1,2,0:T(8,128)(2,1)}, u32[]{:S(2)}, u32[]{:S(2)}) collective-permute-start(bf16[2,128,256]{1,2,0:T(8,128)(2,1)} %get-tuple-element.63), channel_id=1, source_target_pairs={{0,16},{4,20},{8,24},{12,28},{16,0},{20,4},{24,8},{28,12},{32,48},... | collective-permute-start | bytes 393224 | tf_op jit(solution)/shard_map/ppermute | solution.py:19
  62.8 7.0 %collective-permute-start.3 = (bf16[2,128,256]{1,2,0:T(8,128)(2,1)}, bf16[2,128,256]{1,2,0:T(8,128)(2,1)}, u32[]{:S(2)}, u32[]{:S(2)}) collective-permute-start(bf16[2,128,256]{1,2,0:T(8,128)(2,1)} %get-tuple-element.64), channel_id=1, source_target_pairs={{0,32},{4,36},{8,40},{12,44},{16,48},{20,52},{24,56},{28,60},{32,0... | collective-permute-start | bytes 393224 | tf_op jit(solution)/shard_map/ppermute | solution.py:19
  69.8 4.4 %collective-permute-start.4 = (bf16[2,128,256]{1,2,0:T(8,128)(2,1)}, bf16[2,128,256]{1,2,0:T(8,128)(2,1)}, u32[]{:S(2)}, u32[]{:S(2)}) collective-permute-start(bf16[2,128,256]{1,2,0:T(8,128)(2,1)} %get-tuple-element.65), channel_id=1, source_target_pairs={{0,64},{4,68},{8,72},{12,76},{16,80},{20,84},{24,88},{28,92},{32,9... | collective-permute-start | bytes 393224 | tf_op jit(solution)/shard_map/ppermute | solution.py:19
  84.2 0.9 convert_element_type.68
  85.2 1.6 convert_element_type.69
  86.8 1.6 convert_element_type.70
  88.4 3.9 %collective-permute-done.3 = bf16[2,128,256]{1,2,0:T(8,128)(2,1)} collective-permute-done((bf16[2,128,256]{1,2,0:T(8,128)(2,1)}, bf16[2,128,256]{1,2,0:T(8,128)(2,1)}, u32[]{:S(2)}, u32[]{:S(2)}) %collective-permute-start.3) | collective-permute-done | bytes 131104 | tf_op jit(solution)/shard_map/ppermute | solution.py:19
  92.3 1.6 convert_element_type.71
  93.9 1.6 convert_element_type.72
  95.6 4.6 %constant_dynamic-update-slice_fusion = (bf16[5,128,256]{1,2,0:T(8,128)(2,1)S(1)}, bf16[128,256]{0,1:T(8,128)(2,1)S(1)}, f32[128,256]{0,1:T(8,128)S(1)}) fusion(f32[2,128,256]{1,2,0:T(8,128)} %convert_element_type.72, pred[]{:T(512)} %bitcast.26, f32[2,128,256]{1,2,0:T(8,128)} %convert_element_type.71, pred[]{:T(512)} %bitcast.22, ...), kind=kOutput, calls=%fused_computation.148 | convolution fusion | flops 34078720 | bytes 1441797 | tf_op jit(solution)/shard_map/dot_general | solution.py:28
  100.3 4.3 %constant_dynamic-update-slice_fusion.1 = (bf16[5,128,256]{1,2,0:T(8,128)(2,1)S(1)}, bf16[128,256]{0,1:T(8,128)(2,1)S(1)}) fusion(f32[128,256]{0,1:T(8,128)S(1)} %get-tuple-element.82, f32[2,128,256]{1,2,0:T(8,128)S(1)} %copy-done.11, pred[]{:T(512)} %bitcast.26, f32[2,128,256]{1,2,0:T(8,128)S(1)} %copy-done.10, pred[]{:T(512)} %bitcast.22, ...), kind=kOutput, calls=%fused_computation.149 | convolution fusion | flops 34242560 | bytes 1441797 | tf_op jit(solution)/shard_map/dot_general | solution.py:28
  104.6 8.2 %collective-permute-start.9 = (bf16[2,128,256]{1,2,0:T(8,128)(2,1)S(1)}, bf16[2,128,256]{1,2,0:T(8,128)(2,1)S(1)}, u32[]{:S(2)}, u32[]{:S(2)}) collective-permute-start(bf16[2,128,256]{1,2,0:T(8,128)(2,1)S(1)} %pad_maximum_fusion.4), channel_id=1, source_target_pairs={{0,64},{4,68},{8,72},{12,76},{16,80},{20,84},{24,88},{28,92},{32,9... | collective-permute-start | bytes 393224 | tf_op jit(solution)/shard_map/ppermute | solution.py:19
  112.8 8.0 %collective-permute-start.8 = (bf16[2,128,256]{1,2,0:T(8,128)(2,1)S(1)}, bf16[2,128,256]{1,2,0:T(8,128)(2,1)}, u32[]{:S(2)}, u32[]{:S(2)}) collective-permute-start(bf16[2,128,256]{1,2,0:T(8,128)(2,1)S(1)} %pad_maximum_fusion.4), channel_id=1, source_target_pairs={{0,32},{4,36},{8,40},{12,44},{16,48},{20,52},{24,56},{28,60},{32,0... | collective-permute-start | bytes 393224 | tf_op jit(solution)/shard_map/ppermute | solution.py:19
  120.8 1.9 collective-permute-start.7
  122.7 1.9 collective-permute-start.6
  124.6 3.0 %collective-permute-start.5 = (bf16[2,128,256]{1,2,0:T(8,128)(2,1)S(1)}, bf16[2,128,256]{1,2,0:T(8,128)(2,1)}, u32[]{:S(2)}, u32[]{:S(2)}) collective-permute-start(bf16[2,128,256]{1,2,0:T(8,128)(2,1)S(1)} %pad_maximum_fusion.4), channel_id=1, source_target_pairs={{0,4},{4,0},{8,12},{12,8},{16,20},{20,16},{24,28},{28,24},{32,36},... | collective-permute-start | bytes 393224 | tf_op jit(solution)/shard_map/ppermute | solution.py:19
  128.3 0.9 copy.71
  129.2 12.1 %all-to-all-start.2 = ((bf16[128,8,128]{2,1,0:T(8,128)(2,1)}), bf16[128,8,128]{2,1,0:T(8,128)(2,1)S(1)}, u32[]{:S(2)}, u32[]{:S(2)}) async-start(bf16[128,8,128]{2,1,0:T(8,128)(2,1)} %copy.71), calls=%async_computation.2 | async-start | bytes 524288 | tf_op jit(solution)/shard_map/all_to_all | solution.py:38
  141.6 1.0 bitcast_dynamic-update-slice_fusion.4
  142.6 0.9 bitcast_dynamic-update-slice_fusion.3
  143.5 0.9 bitcast_dynamic-update-slice_fusion.2
  144.5 0.9 bitcast_dynamic-update-slice_fusion.1
  146.9 5.0 %collective-permute-start.12 = (bf16[2,128,256]{2,1,0:T(8,128)(2,1)}, bf16[2,128,256]{2,1,0:T(8,128)(2,1)S(1)}, u32[]{:S(2)}, u32[]{:S(2)}) collective-permute-start(bf16[2,128,256]{2,1,0:T(8,128)(2,1)} %fusion.8), channel_id=1, source_target_pairs={{0,3},{1,0},{2,1},{3,2},{4,7},{5,4},{6,5},{7,6},{8,11},{9,8},{10,9... | collective-permute-start | bytes 393224 | tf_op jit(solution)/shard_map/ppermute | solution.py:24
  152.9 1.1 dynamic-slice_bitcast_fusion.2
  154.1 3.1 %collective-permute-start.13 = (bf16[896,256]{1,0:T(8,128)(2,1)}, bf16[896,256]{1,0:T(8,128)(2,1)}, u32[]{:S(2)}, u32[]{:S(2)}) collective-permute-start(bf16[896,256]{1,0:T(8,128)(2,1)} %get-tuple-element.46), channel_id=1, source_target_pairs={{0,128},{128,256},{256,384},{384,0},{1,129},{129,257},{257,385},{3... | collective-permute-start | bytes 1376264 | tf_op jit(solution)/shard_map/ppermute | solution.py:24
  157.2 3.4 %collective-permute-start.15 = (bf16[896,256]{1,0:T(8,128)(2,1)}, bf16[896,256]{1,0:T(8,128)(2,1)}, u32[]{:S(2)}, u32[]{:S(2)}) collective-permute-start(bf16[896,256]{1,0:T(8,128)(2,1)} %get-tuple-element.47), channel_id=1, source_target_pairs={{0,384},{128,0},{256,128},{384,256},{1,385},{129,1},{257,129},{385... | collective-permute-start | bytes 1376264 | tf_op jit(solution)/shard_map/ppermute | solution.py:24
  160.6 3.4 %collective-permute-start.14 = (bf16[896,256]{1,0:T(8,128)(2,1)}, bf16[896,256]{1,0:T(8,128)(2,1)}, u32[]{:S(2)}, u32[]{:S(2)}) collective-permute-start(bf16[896,256]{1,0:T(8,128)(2,1)} %get-tuple-element.48), channel_id=1, source_target_pairs={{0,256},{128,384},{256,0},{384,128},{1,257},{129,385},{257,1},{385... | collective-permute-start | bytes 1376264 | tf_op jit(solution)/shard_map/ppermute | solution.py:24
  164.0 2.0 collective-permute-start.11
  166.8 2.7 %collective-permute-start.10 = (bf16[2,128,256]{2,1,0:T(8,128)(2,1)}, bf16[2,128,256]{2,1,0:T(8,128)(2,1)S(1)}, u32[]{:S(2)}, u32[]{:S(2)}) collective-permute-start(bf16[2,128,256]{2,1,0:T(8,128)(2,1)} %fusion.8), channel_id=1, source_target_pairs={{0,1},{1,2},{2,3},{3,0},{4,5},{5,6},{6,7},{7,4},{8,9},{9,10},{10,1... | collective-permute-start | bytes 393224 | tf_op jit(solution)/shard_map/ppermute | solution.py:24
  170.3 17.0 %all-to-all-start.3 = ((bf16[128,8,128]{2,1,0:T(8,128)(2,1)}), bf16[128,8,128]{2,1,0:T(8,128)(2,1)}, u32[]{:S(2)}, u32[]{:S(2)}) async-start(bf16[128,8,128]{2,1,0:T(8,128)(2,1)} %broadcast_in_dim.35), calls=%async_computation.3 | async-start | bytes 524288 | tf_op jit(solution)/shard_map/all_to_all | solution.py:44
  187.4 1.7 convert_add_fusion.1
  189.1 1.5 fusion.1
  192.1 0.9 fusion.85
  193.0 16.5 %all-to-all-done.3 = bf16[128,8,128]{2,1,0:T(8,128)(2,1)} async-done(((bf16[128,8,128]{2,1,0:T(8,128)(2,1)}), bf16[128,8,128]{2,1,0:T(8,128)(2,1)}, u32[]{:S(2)}, u32[]{:S(2)}) %all-to-all-start.3) | async-done | bytes 262176 | tf_op jit(solution)/shard_map/all_to_all | solution.py:44
  209.5 1.0 copy.96
  211.0 0.8 pad_maximum_fusion.1
  211.8 3.5 %all-to-all-start.4 = ((bf16[4,256,256]{2,1,0:T(8,128)(2,1)}), bf16[4,256,256]{2,1,0:T(8,128)(2,1)S(1)}, u32[]{:S(2)}, u32[]{:S(2)}) async-start(bf16[4,256,256]{2,1,0:T(8,128)(2,1)} %pad_maximum_fusion.1), calls=%async_computation.4 | async-start | bytes 1048576 | tf_op jit(solution)/shard_map/all_to_all | solution.py:153
  215.3 0.9 fusion.26
  217.0 5.4 %all-to-all-done.4 = bf16[4,256,256]{2,1,0:T(8,128)(2,1)S(1)} async-done(((bf16[4,256,256]{2,1,0:T(8,128)(2,1)}), bf16[4,256,256]{2,1,0:T(8,128)(2,1)S(1)}, u32[]{:S(2)}, u32[]{:S(2)}) %all-to-all-start.4) | async-done | bytes 524320 | tf_op jit(solution)/shard_map/all_to_all | solution.py:153
  (94 shorter events, 15.0 us)
Async XLA Ops:
  0.6 22.6 %copy-start = (bf16[1,1,5,256,256]{4,3,2,1,0:T(8,128)(2,1)S(1)}, bf16[1,1,5,256,256]{4,3,2,1,0:T(8,128)(2,1)}, u32[]{:S(2)}) copy-start(bf16[1,1,5,256,256]{4,3,2,1,0:T(8,128)(2,1)} %param.12) | copy-start | bytes 1966084
  0.6 22.6 %copy-start.6 = (bf16[128,256]{1,0:T(8,128)(2,1)S(1)}, bf16[128,256]{1,0:T(8,128)(2,1)}, u32[]{:S(2)}) copy-start(bf16[128,256]{1,0:T(8,128)(2,1)} %param.10) | copy-start | bytes 196612
  3.7 29.8 %all-to-all-start = ((bf16[32,8,128]{2,1,0:T(8,128)(2,1)}), bf16[32,8,128]{2,1,0:T(8,128)(2,1)S(1)}, u32[]{:S(2)}, u32[]{:S(2)}) async-start(bf16[32,8,128]{2,1,0:T(8,128)(2,1)} %pad_maximum_fusion.5), calls=%async_computation | async-start | bytes 131072 | tf_op jit(solution)/shard_map/all_to_all | solution.py:38
  34.3 39.9 %copy-start.14 = (s32[4]{0:T(128)S(1)}, s32[4]{0:T(128)}, u32[]{:S(2)}) copy-start(s32[4]{0:T(128)} %param.17) | copy-start | bytes 52
  34.3 61.2 %all-to-all-start.1 = ((bf16[128,8,128]{2,1,0:T(8,128)(2,1)}), bf16[128,8,128]{2,1,0:T(8,128)(2,1)S(1)}, u32[]{:S(2)}, u32[]{:S(2)}) async-start(bf16[128,8,128]{2,1,0:T(8,128)(2,1)} %broadcast_in_dim.33), calls=%async_computation.1 | async-start | bytes 524288 | tf_op jit(solution)/shard_map/all_to_all | solution.py:44
  41.9 38.9 %copy-start.12 = (bf16[1,256,512]{2,1,0:T(8,128)(2,1)S(1)}, bf16[1,256,512]{2,1,0:T(8,128)(2,1)}, u32[]{:S(2)}) copy-start(bf16[1,256,512]{2,1,0:T(8,128)(2,1)} %param.15) | copy-start | bytes 786436
  53.1 42.5 %copy-start.5 = (bf16[512,1,256]{2,0,1:T(8,128)(2,1)S(1)}, bf16[512,1,256]{2,0,1:T(8,128)(2,1)}, u32[]{:S(2)}) copy-start(bf16[512,1,256]{2,0,1:T(8,128)(2,1)} %param.14) | copy-start | bytes 786436
  53.1 31.1 %collective-permute-start = (bf16[2,128,256]{1,2,0:T(8,128)(2,1)S(1)}, bf16[2,128,256]{1,2,0:T(8,128)(2,1)}, u32[]{:S(2)}, u32[]{:S(2)}) collective-permute-start(bf16[2,128,256]{1,2,0:T(8,128)(2,1)S(1)} %get-tuple-element.61), channel_id=1, source_target_pairs={{0,4},{4,0},{8,12},{12,8},{16,20},{20,16},{24,28},{28,24},{32,36},... | collective-permute-start | bytes 393224 | tf_op jit(solution)/shard_map/ppermute | solution.py:19
  56.0 29.1 %collective-permute-start.1 = (bf16[2,128,256]{1,2,0:T(8,128)(2,1)}, bf16[2,128,256]{1,2,0:T(8,128)(2,1)}, u32[]{:S(2)}, u32[]{:S(2)}) collective-permute-start(bf16[2,128,256]{1,2,0:T(8,128)(2,1)} %get-tuple-element.62), channel_id=1, source_target_pairs={{0,8},{4,12},{8,0},{12,4},{16,24},{20,28},{24,16},{28,20},{32,40},... | collective-permute-start | bytes 393224 | tf_op jit(solution)/shard_map/ppermute | solution.py:19
  58.8 28.0 %collective-permute-start.2 = (bf16[2,128,256]{1,2,0:T(8,128)(2,1)}, bf16[2,128,256]{1,2,0:T(8,128)(2,1)}, u32[]{:S(2)}, u32[]{:S(2)}) collective-permute-start(bf16[2,128,256]{1,2,0:T(8,128)(2,1)} %get-tuple-element.63), channel_id=1, source_target_pairs={{0,16},{4,20},{8,24},{12,28},{16,0},{20,4},{24,8},{28,12},{32,48},... | collective-permute-start | bytes 393224 | tf_op jit(solution)/shard_map/ppermute | solution.py:19
  62.8 29.5 %collective-permute-start.3 = (bf16[2,128,256]{1,2,0:T(8,128)(2,1)}, bf16[2,128,256]{1,2,0:T(8,128)(2,1)}, u32[]{:S(2)}, u32[]{:S(2)}) collective-permute-start(bf16[2,128,256]{1,2,0:T(8,128)(2,1)} %get-tuple-element.64), channel_id=1, source_target_pairs={{0,32},{4,36},{8,40},{12,44},{16,48},{20,52},{24,56},{28,60},{32,0... | collective-permute-start | bytes 393224 | tf_op jit(solution)/shard_map/ppermute | solution.py:19
  69.8 24.1 %collective-permute-start.4 = (bf16[2,128,256]{1,2,0:T(8,128)(2,1)}, bf16[2,128,256]{1,2,0:T(8,128)(2,1)}, u32[]{:S(2)}, u32[]{:S(2)}) collective-permute-start(bf16[2,128,256]{1,2,0:T(8,128)(2,1)} %get-tuple-element.65), channel_id=1, source_target_pairs={{0,64},{4,68},{8,72},{12,76},{16,80},{20,84},{24,88},{28,92},{32,9... | collective-permute-start | bytes 393224 | tf_op jit(solution)/shard_map/ppermute | solution.py:19
  95.6 4.6 %copy-start.8 = (f32[2,128,256]{1,2,0:T(8,128)S(1)}, f32[2,128,256]{1,2,0:T(8,128)}, u32[]{:S(2)}) copy-start(f32[2,128,256]{1,2,0:T(8,128)} %convert_element_type.69) | copy-start | bytes 786436
  95.6 4.7 %copy-start.9 = (f32[2,128,256]{1,2,0:T(8,128)S(1)}, f32[2,128,256]{1,2,0:T(8,128)}, u32[]{:S(2)}) copy-start(f32[2,128,256]{1,2,0:T(8,128)} %convert_element_type.70) | copy-start | bytes 786436
  95.6 4.7 %copy-start.10 = (f32[2,128,256]{1,2,0:T(8,128)S(1)}, f32[2,128,256]{1,2,0:T(8,128)}, u32[]{:S(2)}) copy-start(f32[2,128,256]{1,2,0:T(8,128)} %convert_element_type.71) | copy-start | bytes 786436
  95.6 4.7 %copy-start.11 = (f32[2,128,256]{1,2,0:T(8,128)S(1)}, f32[2,128,256]{1,2,0:T(8,128)}, u32[]{:S(2)}) copy-start(f32[2,128,256]{1,2,0:T(8,128)} %convert_element_type.72) | copy-start | bytes 786436
  104.6 40.8 %collective-permute-start.9 = (bf16[2,128,256]{1,2,0:T(8,128)(2,1)S(1)}, bf16[2,128,256]{1,2,0:T(8,128)(2,1)S(1)}, u32[]{:S(2)}, u32[]{:S(2)}) collective-permute-start(bf16[2,128,256]{1,2,0:T(8,128)(2,1)S(1)} %pad_maximum_fusion.4), channel_id=1, source_target_pairs={{0,64},{4,68},{8,72},{12,76},{16,80},{20,84},{24,88},{28,92},{32,9... | collective-permute-start | bytes 393224 | tf_op jit(solution)/shard_map/ppermute | solution.py:19
  112.8 31.7 %collective-permute-start.8 = (bf16[2,128,256]{1,2,0:T(8,128)(2,1)S(1)}, bf16[2,128,256]{1,2,0:T(8,128)(2,1)}, u32[]{:S(2)}, u32[]{:S(2)}) collective-permute-start(bf16[2,128,256]{1,2,0:T(8,128)(2,1)S(1)} %pad_maximum_fusion.4), channel_id=1, source_target_pairs={{0,32},{4,36},{8,40},{12,44},{16,48},{20,52},{24,56},{28,60},{32,0... | collective-permute-start | bytes 393224 | tf_op jit(solution)/shard_map/ppermute | solution.py:19
  120.8 22.7 %collective-permute-start.7 = (bf16[2,128,256]{1,2,0:T(8,128)(2,1)S(1)}, bf16[2,128,256]{1,2,0:T(8,128)(2,1)}, u32[]{:S(2)}, u32[]{:S(2)}) collective-permute-start(bf16[2,128,256]{1,2,0:T(8,128)(2,1)S(1)} %pad_maximum_fusion.4), channel_id=1, source_target_pairs={{0,16},{4,20},{8,24},{12,28},{16,0},{20,4},{24,8},{28,12},{32,48},... | collective-permute-start | bytes 393224 | tf_op jit(solution)/shard_map/ppermute | solution.py:19
  122.7 19.9 %collective-permute-start.6 = (bf16[2,128,256]{1,2,0:T(8,128)(2,1)S(1)}, bf16[2,128,256]{1,2,0:T(8,128)(2,1)}, u32[]{:S(2)}, u32[]{:S(2)}) collective-permute-start(bf16[2,128,256]{1,2,0:T(8,128)(2,1)S(1)} %pad_maximum_fusion.4), channel_id=1, source_target_pairs={{0,8},{4,12},{8,0},{12,4},{16,24},{20,28},{24,16},{28,20},{32,40},... | collective-permute-start | bytes 393224 | tf_op jit(solution)/shard_map/ppermute | solution.py:19
  124.6 17.0 %collective-permute-start.5 = (bf16[2,128,256]{1,2,0:T(8,128)(2,1)S(1)}, bf16[2,128,256]{1,2,0:T(8,128)(2,1)}, u32[]{:S(2)}, u32[]{:S(2)}) collective-permute-start(bf16[2,128,256]{1,2,0:T(8,128)(2,1)S(1)} %pad_maximum_fusion.4), channel_id=1, source_target_pairs={{0,4},{4,0},{8,12},{12,8},{16,20},{20,16},{24,28},{28,24},{32,36},... | collective-permute-start | bytes 393224 | tf_op jit(solution)/shard_map/ppermute | solution.py:19
  129.2 40.2 %all-to-all-start.2 = ((bf16[128,8,128]{2,1,0:T(8,128)(2,1)}), bf16[128,8,128]{2,1,0:T(8,128)(2,1)S(1)}, u32[]{:S(2)}, u32[]{:S(2)}) async-start(bf16[128,8,128]{2,1,0:T(8,128)(2,1)} %copy.71), calls=%async_computation.2 | async-start | bytes 524288 | tf_op jit(solution)/shard_map/all_to_all | solution.py:38
  141.6 4.3 %copy-start.1 = (bf16[1,1,5,256,256]{4,3,2,1,0:T(8,128)(2,1)S(1)}, bf16[1,1,5,256,256]{4,3,2,1,0:T(8,128)(2,1)}, u32[]{:S(2)}) copy-start(bf16[1,1,5,256,256]{4,3,2,1,0:T(8,128)(2,1)} %param.11) | copy-start | bytes 1966084
  145.4 6.6 %copy-start.7 = (bf16[128,256]{1,0:T(8,128)(2,1)S(1)}, bf16[128,256]{1,0:T(8,128)(2,1)}, u32[]{:S(2)}) copy-start(bf16[128,256]{1,0:T(8,128)(2,1)} %param.9) | copy-start | bytes 196612
  146.9 19.1 %collective-permute-start.12 = (bf16[2,128,256]{2,1,0:T(8,128)(2,1)}, bf16[2,128,256]{2,1,0:T(8,128)(2,1)S(1)}, u32[]{:S(2)}, u32[]{:S(2)}) collective-permute-start(bf16[2,128,256]{2,1,0:T(8,128)(2,1)} %fusion.8), channel_id=1, source_target_pairs={{0,3},{1,0},{2,1},{3,2},{4,7},{5,4},{6,5},{7,6},{8,11},{9,8},{10,9... | collective-permute-start | bytes 393224 | tf_op jit(solution)/shard_map/ppermute | solution.py:24
  154.1 35.0 %collective-permute-start.13 = (bf16[896,256]{1,0:T(8,128)(2,1)}, bf16[896,256]{1,0:T(8,128)(2,1)}, u32[]{:S(2)}, u32[]{:S(2)}) collective-permute-start(bf16[896,256]{1,0:T(8,128)(2,1)} %get-tuple-element.46), channel_id=1, source_target_pairs={{0,128},{128,256},{256,384},{384,0},{1,129},{129,257},{257,385},{3... | collective-permute-start | bytes 1376264 | tf_op jit(solution)/shard_map/ppermute | solution.py:24
  157.2 31.9 %collective-permute-start.15 = (bf16[896,256]{1,0:T(8,128)(2,1)}, bf16[896,256]{1,0:T(8,128)(2,1)}, u32[]{:S(2)}, u32[]{:S(2)}) collective-permute-start(bf16[896,256]{1,0:T(8,128)(2,1)} %get-tuple-element.47), channel_id=1, source_target_pairs={{0,384},{128,0},{256,128},{384,256},{1,385},{129,1},{257,129},{385... | collective-permute-start | bytes 1376264 | tf_op jit(solution)/shard_map/ppermute | solution.py:24
  160.6 28.5 %collective-permute-start.14 = (bf16[896,256]{1,0:T(8,128)(2,1)}, bf16[896,256]{1,0:T(8,128)(2,1)}, u32[]{:S(2)}, u32[]{:S(2)}) collective-permute-start(bf16[896,256]{1,0:T(8,128)(2,1)} %get-tuple-element.48), channel_id=1, source_target_pairs={{0,256},{128,384},{256,0},{384,128},{1,257},{129,385},{257,1},{385... | collective-permute-start | bytes 1376264 | tf_op jit(solution)/shard_map/ppermute | solution.py:24
  164.0 23.3 %collective-permute-start.11 = (bf16[2,128,256]{2,1,0:T(8,128)(2,1)}, bf16[2,128,256]{2,1,0:T(8,128)(2,1)S(1)}, u32[]{:S(2)}, u32[]{:S(2)}) collective-permute-start(bf16[2,128,256]{2,1,0:T(8,128)(2,1)} %fusion.8), channel_id=1, source_target_pairs={{0,2},{1,3},{2,0},{3,1},{4,6},{5,7},{6,4},{7,5},{8,10},{9,11},{10,... | collective-permute-start | bytes 393224 | tf_op jit(solution)/shard_map/ppermute | solution.py:24
  166.1 0.7 copy-start.13
  166.8 20.6 %collective-permute-start.10 = (bf16[2,128,256]{2,1,0:T(8,128)(2,1)}, bf16[2,128,256]{2,1,0:T(8,128)(2,1)S(1)}, u32[]{:S(2)}, u32[]{:S(2)}) collective-permute-start(bf16[2,128,256]{2,1,0:T(8,128)(2,1)} %fusion.8), channel_id=1, source_target_pairs={{0,1},{1,2},{2,3},{3,0},{4,5},{5,6},{6,7},{7,4},{8,9},{9,10},{10,1... | collective-permute-start | bytes 393224 | tf_op jit(solution)/shard_map/ppermute | solution.py:24
  170.3 39.1 %all-to-all-start.3 = ((bf16[128,8,128]{2,1,0:T(8,128)(2,1)}), bf16[128,8,128]{2,1,0:T(8,128)(2,1)}, u32[]{:S(2)}, u32[]{:S(2)}) async-start(bf16[128,8,128]{2,1,0:T(8,128)(2,1)} %broadcast_in_dim.35), calls=%async_computation.3 | async-start | bytes 524288 | tf_op jit(solution)/shard_map/all_to_all | solution.py:44
  193.0 22.3 %copy-start.2 = (bf16[256,512]{1,0:T(8,128)(2,1)S(1)}, bf16[256,512]{1,0:T(8,128)(2,1)}, u32[]{:S(2)}) copy-start(bf16[256,512]{1,0:T(8,128)(2,1)} %param.13) | copy-start | bytes 786436
  193.0 22.3 %copy-start.4 = (f32[2,128,256]{2,1,0:T(8,128)S(1)}, f32[2,128,256]{2,1,0:T(8,128)}, u32[]{:S(2)}) copy-start(f32[2,128,256]{2,1,0:T(8,128)} %convert_add_fusion.1) | copy-start | bytes 786436
  210.5 5.7 %copy-start.3 = (bf16[512,256]{1,0:T(8,128)(2,1)S(1)}, bf16[512,256]{1,0:T(8,128)(2,1)}, u32[]{:S(2)}) copy-start(bf16[512,256]{1,0:T(8,128)(2,1)} %param.16) | copy-start | bytes 786436
  211.8 10.5 %all-to-all-start.4 = ((bf16[4,256,256]{2,1,0:T(8,128)(2,1)}), bf16[4,256,256]{2,1,0:T(8,128)(2,1)S(1)}, u32[]{:S(2)}, u32[]{:S(2)}) async-start(bf16[4,256,256]{2,1,0:T(8,128)(2,1)} %pad_maximum_fusion.1), calls=%async_computation.4 | async-start | bytes 1048576 | tf_op jit(solution)/shard_map/all_to_all | solution.py:153

commit v2 on v1

v2 whole, which is shorter than its diff:
```python
from functools import partial

import jax
import jax.numpy as jnp
from jax import lax
from jax.experimental import pallas as pl
from jax.experimental.pallas import tpu as pltpu
from jax.sharding import PartitionSpec as P

root_half = 0.7071067811865476
gauss_norm = 0.3989422804014327
f32 = jnp.float32
bf16 = jnp.bfloat16
BITS = 5
SLOTS = 5
FIRST = (4, 3)
FIRST_A = (4, 3)
LONG = 20 * 10**9
VMEM_LIMIT = 60 * 2**20
VM = pl.BlockSpec(memory_space=pltpu.VMEM)
SM = pl.BlockSpec(memory_space=pltpu.SMEM)


def swap_bit(block, bit):
    count = lax.axis_size("in")
    return lax.ppermute(block, "in", [(i, i ^ (1 << bit)) for i in range(count)])


def dot(a, b, ca, cb):
    return lax.dot_general(a, b, (((ca,), (cb,)), ((), ())), preferred_element_type=f32)


def exchange(parts, axes):
    return lax.all_to_all(parts, axes, 0, 0, tiled=True)


def spread(row, axes, group):
    return exchange(jnp.broadcast_to(row[None], (group,) + row.shape), axes)


def ring(block, axis, distance):
    count = lax.axis_size(axis)
    return lax.ppermute(block, axis, [(i, (i + distance) % count) for i in range(count)])


def pick(stack, index):
    return lax.dynamic_index_in_dim(stack, index, 0, keepdims=False)


def together(*values):
    return lax.optimization_barrier(values)


def kernel_call(body, specs, shapes, flops, name, after=None):
    tokens = [] if after is None else [after]
    call = pl.pallas_call(
        lambda *refs: body(*refs[len(tokens) :]),
        in_specs=[pl.BlockSpec(memory_space=pl.ANY)] * len(tokens) + specs,
        out_specs=[VM] * len(shapes),
        out_shape=[jax.ShapeDtypeStruct(s, d) for s, d in shapes],
        compiler_params=pltpu.CompilerParams(vmem_limit_bytes=VMEM_LIMIT),
        cost_estimate=pl.CostEstimate(flops=flops, bytes_accessed=4 * 2**20, transcendentals=0),
        name=name,
    )
    return lambda *values: call(*tokens, *values)


def gate(value, after=None):
    tokens = [] if after is None else [after]
    return pl.pallas_call(
        lambda *refs: None,
        in_specs=[pl.BlockSpec(memory_space=pl.ANY)] * (1 + len(tokens)),
        out_specs=pl.BlockSpec(memory_space=pl.ANY),
        out_shape=jax.ShapeDtypeStruct(value.shape, value.dtype),
        input_output_aliases={0: 0},
        cost_estimate=pl.CostEstimate(flops=LONG, bytes_accessed=2**20, transcendentals=0),
        name="gate",
    )(value, *tokens)


def slot_of_bit(strides_ref, bit):
    slot = 0
    for k in range(SLOTS - 1):
        slot = slot + jnp.where(strides_ref[k] == 1 << bit, k + 1, 0)
    return slot


def products(bits, strides_ref, x_ref, dy_ref, w1_ref, w2_ref, *send_refs):
    x, dy = x_ref[...], dy_ref[...]
    for bit, send_ref in zip(bits, send_refs):
        slot = slot_of_bit(strides_ref, bit)
        send_ref[0] = dot(x, w1_ref[slot], 1, 0).astype(bf16)
        send_ref[1] = dot(dy, w2_ref[slot], 1, 1).astype(bf16)


def sum_products(x_ref, dy_ref, w1_ref, w2_ref, *refs):
    got, total_ref = refs[:-1], refs[-1]
    own = (dot(x_ref[...], w1_ref[0], 1, 0), dot(dy_ref[...], w2_ref[0], 1, 1))
    for half in range(2):
        value = own[half]
        for ref in got:
            value = value + ref[half].astype(f32)
        total_ref[half] = value


def activations(base_ref, latent_ref, right1_ref, left2_ref, *refs):
    hd_refs, part_ref = refs[:3], refs[3]
    rank = right1_ref.shape[0]
    right1, left2 = right1_ref[...], left2_ref[...]
    z = base_ref[0] + dot(latent_ref[:, :rank], right1, 1, 0)
    g = base_ref[1] + dot(latent_ref[:, rank:], left2, 1, 1)
    cumul = 0.5 * (1.0 + lax.erf(z * root_half))
    slope = cumul + z * jnp.exp(-0.5 * z * z) * gauss_norm
    h = (z * cumul).astype(bf16)
    dz = (g * slope).astype(bf16)
    for hd_ref in hd_refs:
        hd_ref[0] = h
        hd_ref[1] = dz
    part_ref[:, :rank] = dot(h, left2, 1, 0).astype(bf16)
    part_ref[:, rank:] = dot(dz, right1, 1, 1).astype(bf16)


def block_outputs(bits, strides_ref, w1_ref, w2_ref, hd_ref, *refs):
    near, out_ref = refs[:-1], refs[-1]
    size = w1_ref.shape[1]
    block_out = dot(hd_ref[0], w2_ref[0], 1, 0)
    block_in = dot(hd_ref[1], w1_ref[0], 1, 1)
    for bit, ref in zip(bits, near):
        slot = slot_of_bit(strides_ref, bit)
        block_out = block_out + dot(ref[0], w2_ref[slot], 1, 0)
        block_in = block_in + dot(ref[1], w1_ref[slot], 1, 1)
    out_ref[:, :size] = block_out.astype(bf16)
    out_ref[:, size:] = block_in.astype(bf16)


def block_grads(bits, strides_ref, x_ref, dy_ref, latent_ref, hd_ref, *refs):
    near, out_ref = refs[:-1], refs[-1]
    size = x_ref.shape[1]
    rank = latent_ref.shape[1] // 2
    parts = out_ref.shape[0]
    rows = size // parts
    x, dy = x_ref[...], dy_ref[...]

    def store(slot, ref):
        grad1, grad2 = dot(x, ref[1], 0, 0), dot(ref[0], dy, 0, 0)
        for d in range(parts):
            own = slice(d * rows, (d + 1) * rows)
            start = pl.multiple_of(slot * rows, rows)
            out_ref[d, pl.ds(start, rows), :] = grad1[own].astype(bf16)
            start = pl.multiple_of((slot + SLOTS) * rows, rows)
            out_ref[d, pl.ds(start, rows), :] = grad2[own].astype(bf16)

    store(0, hd_ref)
    for bit, ref in zip(bits, near):
        store(slot_of_bit(strides_ref, bit), ref)
    first = 2 * SLOTS * rows
    take = rank // parts
    for d in range(parts):
        right1 = dot(latent_ref[:, d * take : (d + 1) * take], hd_ref[1], 0, 0)
        left2 = dot(latent_ref[:, rank + d * take : rank + (d + 1) * take], hd_ref[0], 0, 0)
        out_ref[d, first : first + take, :] = right1.astype(bf16)
        out_ref[d, first + take : first + 2 * take, :] = left2.astype(bf16)


def sum_grads(*refs):
    got, (first_ref, second_ref, right1_ref, left2_ref) = refs[:-4], refs[-4:]
    rows = first_ref.shape[0]
    take = right1_ref.shape[0]

    def total(low, high):
        value = got[0][low:high, :].astype(f32)
        for ref in got[1:]:
            value = value + ref[low:high, :].astype(f32)
        return value

    first_ref[...] = total(0, rows)
    second_ref[...] = total(rows, 2 * rows)
    right1_ref[...] = total(2 * rows, 2 * rows + take)
    left2_ref[...] = total(2 * rows + take, 2 * rows + 2 * take).T


def for_bits(
    bits,
    tokens,
    cotangent,
    first_blocks,
    second_blocks,
    first_left,
    first_right,
    second_left,
    second_right,
    strides,
):
    count, size = tokens.shape
    rank = first_left.shape[1]
    n_in = lax.axis_size("in")
    n_out = lax.axis_size("out")
    n_dp = lax.axis_size("dp")
    p = lax.axis_index("out")
    w1 = first_blocks[0, 0]
    w2 = second_blocks[0, 0]
    right1 = first_right[:, 0]
    left2 = second_left[0]
    share = count // n_out
    wide = 2 * rank
    tile = (wide // 128, 128)
    flops = 2 * count * size * size
    pair = ((2, count, size), bf16)

    x_share = lax.dynamic_slice_in_dim(tokens, p * share, share, 0)
    dy_share = lax.dynamic_slice_in_dim(cotangent, p * share, share, 0)
    part = jnp.concatenate([dot(x_share, first_left, 1, 0), dot(dy_share, second_right, 1, 1)], axis=1)
    got = exchange(part.astype(bf16).reshape((share,) + tile), "in")

    def sent(some, after):
        sends = kernel_call(
            partial(products, some), [SM, VM, VM, VM, VM], [pair] * len(some), LONG, "products", after
        )(strides, tokens, cotangent, w1, w2)
        return [swap_bit(send, bit) for send, bit in zip(sends, some)]

    arrived = sent([b for b in bits if b in FIRST_A], None)
    row = jnp.sum(got.astype(f32), axis=0).astype(bf16)
    arrived += sent([b for b in bits if b not in FIRST_A], row)
    (base,) = kernel_call(
        sum_products, [VM] * (4 + len(bits)), [((2, count, size), f32)], LONG, "sum_products"
    )(tokens, cotangent, w1, w2, *arrived)
    mine = spread(row, "in", n_in)
    latent = spread(gate(mine), "out", n_out).reshape(count, wide)

    hd, first_hd, second_hd, part = kernel_call(
        activations, [VM] * 4, [pair] * 3 + [((count, wide), bf16)], 16 * flops, "activations"
    )(base, latent, right1, left2)

    got = exchange(part.reshape(n_out, share, wide), "out")
    first_hd = gate(first_hd)
    part = jnp.sum(got.astype(f32), axis=0).astype(bf16)
    second_hd = gate(second_hd, part)
    near = [swap_bit(first_hd if bit in FIRST else second_hd, bit) for bit in bits]
    got = exchange(part.reshape((share,) + tile), "in")
    row = jnp.sum(got.astype(f32), axis=0).astype(bf16)
    (blocks,) = kernel_call(
        partial(block_outputs, bits), [SM] + [VM] * (3 + len(bits)), [((count, 2 * size), bf16)], LONG, "block_outputs", row
    )(strides, w1, w2, hd, *near)

    rows = SLOTS * size // n_dp
    take = rank // n_dp
    (grads,) = kernel_call(
        partial(block_grads, bits),
        [SM] + [VM] * (4 + len(bits)),
        [((n_dp, 2 * (rows + take), size), bf16)],
        LONG,
        "block_grads",
        row,
    )(strides, tokens, cotangent, latent, hd, *near)
    mine = spread(row, "in", n_in).reshape(share, wide)
    me = lax.axis_index("dp")
    grads = [pick(grads, me)] + [ring(pick(grads, (me + d) % n_dp), "dp", d) for d in range(1, n_dp)]
    both = jnp.concatenate([mine.reshape(share * wide // 256, 256), blocks.reshape(count * 2 * size // 256, 256)])
    both = spread(gate(both), "out", n_out)
    cut = share * wide // 256
    cf = both[:, :cut].reshape(count, wide)
    blocks = jnp.sum(both[:, cut:].astype(f32), axis=0).reshape(count, 2 * size)
    c, f = cf[:, :rank], cf[:, rank:]
    parts = jnp.concatenate(
        [dot(f, tokens, 0, 0).reshape(n_dp, take, size), dot(c, cotangent, 0, 0).reshape(n_dp, take, size)], axis=1
    ).astype(bf16)
    first_grad, second_grad, right1_grad, left2_grad = kernel_call(
        sum_grads,
        [VM] * n_dp,
        [((rows, size), f32), ((rows, size), f32), ((take, size), f32), ((size, take), f32)],
        LONG,
        "sum_grads",
    )(*grads)
    parts, first_grad, second_grad, right1_grad, left2_grad = together(
        parts, first_grad, second_grad, right1_grad, left2_grad
    )
    parts = exchange(parts, "dp")
    output = (blocks[:, :size] + dot(c, second_right, 1, 0)).astype(bf16)
    input_grad = (blocks[:, size:] + dot(f, first_left, 1, 1)).astype(bf16)
    late = jnp.sum(parts.astype(f32), axis=0)
    left1_grad, right2_grad = late[:take].T, late[take:]
    block_shape = (1, 1, SLOTS, size // n_dp, size)
    return (
        output,
        input_grad,
        first_grad.reshape(block_shape),
        second_grad.reshape(block_shape),
        left1_grad,
        right1_grad[:, None],
        left2_grad[None],
        right2_grad,
    )


def per_device(*args):
    absent = (1 << BITS) - 1 - jnp.sum(args[-1])
    index = sum((absent >= (1 << b)).astype(jnp.int32) for b in range(1, BITS - 1))
    cases = [tuple(b for b in range(BITS) if b != gone) for gone in range(BITS - 1)]
    return lax.switch(index, [partial(for_bits, bits) for bits in cases], *args)


def solution(mesh):
    in_specs = (
        P("dp", "in"),
        P("dp", "in"),
        P("in", "out", None, None, None),
        P("in", "out", None, None, None),
        P("in", None),
        P(None, "out", "in"),
        P("out", "in", None),
        P(None, "in"),
        P(),
    )
    out_specs = (
        P("dp", "in"),
        P("dp", "in"),
        P("in", "out", None, "dp", None),
        P("in", "out", None, "dp", None),
        P("in", "dp"),
        P("dp", "out", "in"),
        P("out", "in", "dp"),
        P("dp", "in"),
    )
    return jax.shard_map(
        per_device, mesh=mesh, in_specs=in_specs, out_specs=out_specs, check_vma=False
    )
```

time: 227 us -> 189 us (0.83); the launches traced: 224 us -> 189 us
  between operations: 18.9 us -> 1.41 us
  Pallas kernels: 0 us -> 16 us
  matrix products: 17.4 us -> 3.16 us
  other arithmetic: 16.2 us -> 3.75 us
  starting transfers between devices: 121 us -> 112 us
  waiting for transfers between devices: 35.7 us -> 38.5 us
  local copies, waits for them, and re-layouts: 15.1 us -> 12.7 us
    pallas_call x0 -> x11, Pallas kernels: none -> 16 us  [the longest x7 16 us: kernel_call(): return lambda *values: call(*tokens, *values)]
    ppermute x6 -> x3, waiting for transfers between devices: 0.02 us -> 14 us  [ring(): lax.ppermute(block, axis, [(i, (i + distance) % count) for i in range(cou...]
    dot_general x12 -> x6, matrix products: 14.3 us -> 3.16 us  [dot(): lax.dot_general(a, b, (((ca,), (cb,)), ((), ())), preferred_element_type=...]
    ppermute x6 -> x3, starting transfers between devices: 19.7 us -> 9.32 us  [ring(): lax.ppermute(block, axis, [(i, (i + distance) % count) for i in range(cou...]
    convert_element_type x6 -> x0, other arithmetic: 8.09 us -> none  [the longest x5 7.42 us: per_device(): got = arrived[b].astype(f32)]
    all_to_all x5 -> x8, waiting for transfers between devices: 31.8 us -> 24.4 us  [exchange(): return lax.all_to_all(parts, axes, 0, 0, tiled=True)]
    ppermute x10 -> x8, waiting for transfers between devices: 3.93 us -> 0.02 us  [swap_bit(): return lax.ppermute(block, 'in', [(i, i ^ 1 << bit) for i in range(count)])]
    slice x5 -> x1, local copies, waits for them, and re-layouts: 3.4 us -> 0.02 us  [for_bits(): cf = both[:, :cut].reshape(count, wide)]
  transfers between devices with their start and end apart: 21 -> 19, of which waited for: 4 -> 6; matrix products, arithmetic and copies ran while one was open for 14% -> 5% of each run, Pallas kernels for 0% -> 7%
where the time goes in v2:
time: 189 us
  starting transfers between devices  112 us (59%)
  waiting for transfers between devices  38.5 us (20%)
  Pallas kernels  16 us (8%)
  local copies, waits for them, and re-layouts  12.7 us (7%)
  other arithmetic  3.75 us (2%)
  matrix products  3.16 us (2%)
    all_to_all x8, starting transfers between devices, exchange(): return lax.all_to_all(parts, axes, 0, 0, tiled=True)  59.8 us
    ppermute x8, starting transfers between devices, swap_bit(): return lax.ppermute(block, 'in', [(i, i ^ 1 << bit) for i in range(count)])  43.2 us
    all_to_all x8, waiting for transfers between devices, exchange(): return lax.all_to_all(parts, axes, 0, 0, tiled=True)  24.4 us
    pallas_call x7, Pallas kernels, kernel_call(): return lambda *values: call(*tokens, *values)  16 us
    ppermute x3, waiting for transfers between devices, ring(): lax.ppermute(block, axis, [(i, (i + distance) % count) for i in range(cou...  14 us
    ppermute x3, starting transfers between devices, ring(): lax.ppermute(block, axis, [(i, (i + distance) % count) for i in range(cou...  9.32 us
    unnamed x66, local copies, waits for them, and re-layouts  5.25 us
    broadcast_in_dim x4, local copies, waits for them, and re-layouts, spread(): return exchange(jnp.broadcast_to(row[None], (group,) + row.shape), axes)  4.71 us
  transfers between devices with their start and end apart: 19, of which 6 were waited for; matrix products, arithmetic and copies ran while one was open for 5% of the time, Pallas kernels for 7%

profile of v2, /device:TPU:1, one launch (start us, length us, event | category | flops | bytes accessed | tf_op | source)
XLA Modules:
  0.0 189.0 jit_solution(10660186012725155977)
XLA Ops:
  0.6 1.3 reduce_sum.225
  2.6 185.4 %conditional.4 = (f32[1,1,5,64,256]{4,3,2,1,0:T(8,128)S(1)}, f32[1,1,5,64,256]{4,3,2,1,0:T(8,128)}, f32[1,256,128]{2,1,0:T(8,128)S(1)}, f32[128,256]{1,0:T(8,128...) conditional(s32[]{:T(128)} %clamp.3, ...), branch_computations={%region_1.7_spmd, %region_7.13_spmd, %region_13.19_spmd, %region_1... | conditional | flops 200422490112 | bytes 82372664
  2.6 1.1 convolution_convert_fusion.3
  3.8 1.1 convolution_convert_fusion.2
  4.9 0.7 pad_maximum_fusion.2
  5.6 16.8 %all-to-all-start = ((bf16[32,8,128]{2,1,0:T(8,128)(2,1)}), bf16[32,8,128]{2,1,0:T(8,128)(2,1)S(1)}, u32[]{:S(2)}, u32[]{:S(2)}) async-start(bf16[32,8,128]{2,1,0:T(8,128)(2,1)} %pad_maximum_fusion.2), calls=%async_computation | async-start | bytes 131072 | tf_op jit(solution)/shard_map/cond/branch_0_fun/all_to_all | solution.py:34
  22.4 2.4 %products.8 = (bf16[2,128,256]{2,1,0:T(8,128)(2,1)}, bf16[2,128,256]{2,1,0:T(8,128)(2,1)}) custom-call(s32[4]{0:T(128)} %get-tuple-element.100.refs_0_.refs_1_, bf16[128,256]{1,0:T(8,128)(2,1)} %get-tuple-element.96.refs_1_.refs_2_.refs_0_, bf16[128,256]{1,0:T(8,128)(2,1)} %get-tuple-element.97.refs_2_.refs_3_.refs_1_, bf16[5,256,256]{2,1,0:T(8,128)(2,1)} %bitcast.176, ...), custom_call_target="tpu_custom_call" | custom-call | flops 20000000000 | bytes 4194304 | tf_op jit(solution)/shard_map/cond/branch_0_fun/products/pallas_call | solution.py:65
  24.9 7.2 %collective-permute-start = (bf16[2,128,256]{2,1,0:T(8,128)(2,1)}, bf16[2,128,256]{2,1,0:T(8,128)(2,1)S(1)}, u32[]{:S(2)}, u32[]{:S(2)}) collective-permute-start(bf16[2,128,256]{2,1,0:T(8,128)(2,1)} %get-tuple-element.101), channel_id=1, source_target_pairs={{0,32},{4,36},{8,40},{12,44},{16,48},{20,52},{24,56},{28,60},{32,0... | collective-permute-start | bytes 393224 | tf_op jit(solution)/shard_map/cond/branch_0_fun/ppermute | solution.py:26
  32.1 7.0 %collective-permute-start.1 = (bf16[2,128,256]{2,1,0:T(8,128)(2,1)}, bf16[2,128,256]{2,1,0:T(8,128)(2,1)S(1)}, u32[]{:S(2)}, u32[]{:S(2)}) collective-permute-start(bf16[2,128,256]{2,1,0:T(8,128)(2,1)} %get-tuple-element.102), channel_id=1, source_target_pairs={{0,64},{4,68},{8,72},{12,76},{16,80},{20,84},{24,88},{28,92},{32,9... | collective-permute-start | bytes 393224 | tf_op jit(solution)/shard_map/cond/branch_0_fun/ppermute | solution.py:26
  39.2 0.6 broadcast_in_dim.36
  39.8 7.7 %all-to-all-start.1 = ((bf16[32,8,128]{2,1,0:T(8,128)(2,1)}), bf16[32,8,128]{2,1,0:T(8,128)(2,1)S(1)}, u32[]{:S(2)}, u32[]{:S(2)}) async-start(bf16[32,8,128]{2,1,0:T(8,128)(2,1)} %broadcast_in_dim.36), calls=%async_computation.1 | async-start | bytes 131072 | tf_op jit(solution)/shard_map/cond/branch_0_fun/all_to_all | solution.py:34
  47.6 1.5 products.9
  49.1 3.3 %collective-permute-start.2 = (bf16[2,128,256]{2,1,0:T(8,128)(2,1)}, bf16[2,128,256]{2,1,0:T(8,128)(2,1)S(1)}, u32[]{:S(2)}, u32[]{:S(2)}) collective-permute-start(bf16[2,128,256]{2,1,0:T(8,128)(2,1)} %get-tuple-element.105), channel_id=1, source_target_pairs={{0,8},{4,12},{8,0},{12,4},{16,24},{20,28},{24,16},{28,20},{32,40},... | collective-permute-start | bytes 393224 | tf_op jit(solution)/shard_map/cond/branch_0_fun/ppermute | solution.py:26
  52.4 4.0 %collective-permute-start.3 = (bf16[2,128,256]{2,1,0:T(8,128)(2,1)}, bf16[2,128,256]{2,1,0:T(8,128)(2,1)S(1)}, u32[]{:S(2)}, u32[]{:S(2)}) collective-permute-start(bf16[2,128,256]{2,1,0:T(8,128)(2,1)} %get-tuple-element.106), channel_id=1, source_target_pairs={{0,16},{4,20},{8,24},{12,28},{16,0},{20,4},{24,8},{28,12},{32,48},... | collective-permute-start | bytes 393224 | tf_op jit(solution)/shard_map/cond/branch_0_fun/ppermute | solution.py:26
  56.4 7.9 %all-to-all-done.1.refs_0_ = bf16[32,8,128]{2,1,0:T(8,128)(2,1)S(1)} async-done(((bf16[32,8,128]{2,1,0:T(8,128)(2,1)}), bf16[32,8,128]{2,1,0:T(8,128)(2,1)S(1)}, u32[]{:S(2)}, u32[]{:S(2)}) %all-to-all-start.1) | async-done | bytes 65568 | tf_op jit(solution)/shard_map/cond/branch_0_fun/all_to_all | solution.py:34
  64.3 0.6 copy-done.25
  64.9 1.6 broadcast_in_dim.37
  66.5 4.2 %all-to-all-start.2 = ((bf16[4,32,8,128]{3,2,1,0:T(8,128)(2,1)}), bf16[4,32,8,128]{3,2,1,0:T(8,128)(2,1)S(1)}, u32[]{:S(2)}, u32[]{:S(2)}) async-start(bf16[4,32,8,128]{3,2,1,0:T(8,128)(2,1)} %broadcast_in_dim.37), calls=%async_computation.2 | async-start | bytes 524288 | tf_op jit(solution)/shard_map/cond/branch_0_fun/all_to_all | solution.py:34
  71.4 0.7 copy-done.93
  72.1 2.0 %sum_products.4.refs_0_ = f32[2,128,256]{2,1,0:T(8,128)} custom-call(bf16[128,256]{1,0:T(8,128)(2,1)S(1)} %copy-done.16, bf16[128,256]{1,0:T(8,128)(2,1)S(1)} %copy-done.20, bf16[5,256,256]{2,1,0:T(8,128)(2,1)S(1)} %bitcast.178, bf16[5,256,256]{2,1,0:T(8,128)(2,1)S(1)} %bitcast.194, bf16[2,128,256]{2,1,0:T(8,128)(2,1)} %copy-done.81, ...), custom_call_target="tpu_custom_call" | custom-call | flops 20000000000 | bytes 4194304 | tf_op jit(solution)/shard_map/cond/branch_0_fun/sum_products/pallas_call | solution.py:65
  74.1 2.1 %all-to-all-done.2 = bf16[4,32,8,128]{3,2,1,0:T(8,128)(2,1)S(1)} async-done(((bf16[4,32,8,128]{3,2,1,0:T(8,128)(2,1)}), bf16[4,32,8,128]{3,2,1,0:T(8,128)(2,1)S(1)}, u32[]{:S(2)}, u32[]{:S(2)}) %all-to-all-start.2) | async-done | bytes 262176 | tf_op jit(solution)/shard_map/cond/branch_0_fun/all_to_all | solution.py:34
  76.2 0.8 copy.57
  76.9 2.2 %activations.4 = (bf16[2,128,256]{2,1,0:T(8,128)(2,1)}, bf16[2,128,256]{2,1,0:T(8,128)(2,1)}, bf16[2,128,256]{2,1,0:T(8,128)(2,1)}, bf16[128,1024]{1,0:T(8,128)(2,1)}) custom-call(f32[2,128,256]{2,1,0:T(8,128)} %sum_products.4.refs_0_, bf16[128,1024]{1,0:T(8,128)(2,1)} %bitcast.156, bf16[512,256]{1,0:T(8,128)(2,1)S(1)} %bitcast.136, ...), custom_call_target="tpu_custom_call" | custom-call | flops 268435456 | bytes 4194304 | tf_op jit(solution)/shard_map/cond/branch_0_fun/activations/pallas_call | solution.py:65
  79.2 3.4 %all-to-all-start.3 = ((bf16[4,32,1024]{2,1,0:T(8,128)(2,1)}), bf16[4,32,1024]{2,1,0:T(8,128)(2,1)S(1)}, u32[]{:S(2)}, u32[]{:S(2)}) async-start(bf16[4,32,1024]{2,1,0:T(8,128)(2,1)} %bitcast.168), calls=%async_computation.3 | async-start | bytes 524288 | tf_op jit(solution)/shard_map/cond/branch_0_fun/all_to_all | solution.py:34
  82.6 6.7 %collective-permute-start.7 = (bf16[2,128,256]{2,1,0:T(8,128)(2,1)}, bf16[2,128,256]{2,1,0:T(8,128)(2,1)S(1)}, u32[]{:S(2)}, u32[]{:S(2)}) collective-permute-start(bf16[2,128,256]{2,1,0:T(8,128)(2,1)} %gate.18), channel_id=1, source_target_pairs={{0,64},{4,68},{8,72},{12,76},{16,80},{20,84},{24,88},{28,92},{32,9... | collective-permute-start | bytes 393224 | tf_op jit(solution)/shard_map/cond/branch_0_fun/ppermute | solution.py:26
  89.3 7.7 %collective-permute-start.6 = (bf16[2,128,256]{2,1,0:T(8,128)(2,1)}, bf16[2,128,256]{2,1,0:T(8,128)(2,1)S(1)}, u32[]{:S(2)}, u32[]{:S(2)}) collective-permute-start(bf16[2,128,256]{2,1,0:T(8,128)(2,1)} %gate.18), channel_id=1, source_target_pairs={{0,32},{4,36},{8,40},{12,44},{16,48},{20,52},{24,56},{28,60},{32,0... | collective-permute-start | bytes 393224 | tf_op jit(solution)/shard_map/cond/branch_0_fun/ppermute | solution.py:26
  97.1 0.6 copy.46
  97.7 10.4 %all-to-all-start.4 = ((bf16[32,8,128]{2,1,0:T(8,128)(2,1)}), bf16[32,8,128]{2,1,0:T(8,128)(2,1)S(1)}, u32[]{:S(2)}, u32[]{:S(2)}) async-start(bf16[32,8,128]{2,1,0:T(8,128)(2,1)} %bitcast.68), calls=%async_computation.4 | async-start | bytes 131072 | tf_op jit(solution)/shard_map/cond/branch_0_fun/all_to_all | solution.py:34
  108.1 4.2 %collective-permute-start.5 = (bf16[2,128,256]{2,1,0:T(8,128)(2,1)}, bf16[2,128,256]{2,1,0:T(8,128)(2,1)S(1)}, u32[]{:S(2)}, u32[]{:S(2)}) collective-permute-start(bf16[2,128,256]{2,1,0:T(8,128)(2,1)} %gate.17), channel_id=1, source_target_pairs={{0,16},{4,20},{8,24},{12,28},{16,0},{20,4},{24,8},{28,12},{32,48},... | collective-permute-start | bytes 393224 | tf_op jit(solution)/shard_map/cond/branch_0_fun/ppermute | solution.py:26
  112.3 3.1 %collective-permute-start.4 = (bf16[2,128,256]{2,1,0:T(8,128)(2,1)}, bf16[2,128,256]{2,1,0:T(8,128)(2,1)S(1)}, u32[]{:S(2)}, u32[]{:S(2)}) collective-permute-start(bf16[2,128,256]{2,1,0:T(8,128)(2,1)} %gate.17), channel_id=1, source_target_pairs={{0,8},{4,12},{8,0},{12,4},{16,24},{20,28},{24,16},{28,20},{32,40},... | collective-permute-start | bytes 393224 | tf_op jit(solution)/shard_map/cond/branch_0_fun/ppermute | solution.py:26
  115.5 6.0 %all-to-all-done.4 = bf16[32,8,128]{2,1,0:T(8,128)(2,1)S(1)} async-done(((bf16[32,8,128]{2,1,0:T(8,128)(2,1)}), bf16[32,8,128]{2,1,0:T(8,128)(2,1)S(1)}, u32[]{:S(2)}, u32[]{:S(2)}) %all-to-all-start.4) | async-done | bytes 65568 | tf_op jit(solution)/shard_map/cond/branch_0_fun/all_to_all | solution.py:34
  121.5 0.6 broadcast_in_dim.38
  122.1 9.7 %all-to-all-start.5 = ((bf16[32,8,128]{2,1,0:T(8,128)(2,1)}), bf16[32,8,128]{2,1,0:T(8,128)(2,1)S(1)}, u32[]{:S(2)}, u32[]{:S(2)}) async-start(bf16[32,8,128]{2,1,0:T(8,128)(2,1)} %broadcast_in_dim.38), calls=%async_computation.5 | async-start | bytes 131072 | tf_op jit(solution)/shard_map/cond/branch_0_fun/all_to_all | solution.py:34
  132.7 2.3 %block_outputs.4 = bf16[128,512]{1,0:T(8,128)(2,1)} custom-call(bf16[8,128]{1,0:T(8,128)(2,1)} %copy-done.45, s32[4]{0:T(128)S(1)} %copy-done.97, bf16[5,256,256]{2,1,0:T(8,128)(2,1)S(1)} %bitcast.179, bf16[5,256,256]{2,1,0:T(8,128)(2,1)S(1)} %bitcast.195, bf16[2,128,256]{2,1,0:T(8,128)(2,1)} %get-tuple-element.110.refs_4_.refs_5_, ...), custom_call_target="tpu_custom_call" | custom-call | flops 20000000000 | bytes 4194304 | tf_op jit(solution)/shard_map/cond/branch_0_fun/block_outputs/pallas_call | solution.py:65
  134.9 3.1 %block_grads.4 = bf16[4,896,256]{2,1,0:T(8,128)(2,1)} custom-call(bf16[8,128]{1,0:T(8,128)(2,1)} %copy-done.45, s32[4]{0:T(128)S(1)} %copy-done.97, bf16[128,256]{1,0:T(8,128)(2,1)S(1)} %copy-done.16, bf16[128,256]{1,0:T(8,128)(2,1)S(1)} %copy-done.20, bf16[128,1024]{1,0:T(8,128)(2,1)} %bitcast.157, bf16[2,128,256]{2,1,0:T(8,128)(2,1)} %get-tuple-element.110.refs_4_.refs_5_, ...), custom_call_target="tpu_custom_call" | custom-call | flops 20000000000 | bytes 4194304 | tf_op jit(solution)/shard_map/cond/branch_0_fun/block_grads/pallas_call | solution.py:65
  138.1 2.3 %dynamic-slice_bitcast_fusion = (bf16[896,256]{1,0:T(8,128)(2,1)S(1)}, bf16[896,256]{1,0:T(8,128)(2,1)S(1)}, bf16[896,256]{1,0:T(8,128)(2,1)S(1)}, bf16[896,256]{1,0:T(8,128)(2,1)}) fusion(bf16[4,896,256]{2,1,0:T(8,128)(2,1)} %block_grads.4, s32[]{:T(128)S(6)} %select_n.91, s32[]{:T(128)S(6)} %select_n.89, s32[]{:T(128)S(6)} %select_n.87, s32[]{:T(128)S(6)} %select_n.85), kind=kLoop, calls=%fused_computation.11 | loop fusion | bytes 3670032 | tf_op jit(solution)/shard_map/cond/branch_0_fun/jit(dynamic_index_in_dim)/squeeze | solution.py:47
  140.4 4.4 %collective-permute-start.10 = (bf16[896,256]{1,0:T(8,128)(2,1)S(1)}, bf16[896,256]{1,0:T(8,128)(2,1)S(1)}, u32[]{:S(2)}, u32[]{:S(2)}) collective-permute-start(bf16[896,256]{1,0:T(8,128)(2,1)S(1)} %get-tuple-element.253), channel_id=1, source_target_pairs={{0,384},{128,0},{256,128},{384,256},{1,385},{129,1},{257,129},{385... | collective-permute-start | bytes 1376264 | tf_op jit(solution)/shard_map/cond/branch_0_fun/ppermute | solution.py:43
  144.8 2.4 %collective-permute-start.9 = (bf16[896,256]{1,0:T(8,128)(2,1)S(1)}, bf16[896,256]{1,0:T(8,128)(2,1)}, u32[]{:S(2)}, u32[]{:S(2)}) collective-permute-start(bf16[896,256]{1,0:T(8,128)(2,1)S(1)} %get-tuple-element.254), channel_id=1, source_target_pairs={{0,256},{128,384},{256,0},{384,128},{1,257},{129,385},{257,1},{385... | collective-permute-start | bytes 1376264 | tf_op jit(solution)/shard_map/cond/branch_0_fun/ppermute | solution.py:43
  147.3 2.5 %collective-permute-start.8 = (bf16[896,256]{1,0:T(8,128)(2,1)S(1)}, bf16[896,256]{1,0:T(8,128)(2,1)}, u32[]{:S(2)}, u32[]{:S(2)}) collective-permute-start(bf16[896,256]{1,0:T(8,128)(2,1)S(1)} %get-tuple-element.255), channel_id=1, source_target_pairs={{0,128},{128,256},{256,384},{384,0},{1,129},{129,257},{257,385},{3... | collective-permute-start | bytes 1376264 | tf_op jit(solution)/shard_map/cond/branch_0_fun/ppermute | solution.py:43
  149.8 0.7 pad_maximum_fusion.1.refs_0_
  150.5 1.9 broadcast_in_dim.39
  152.4 4.2 %all-to-all-start.6 = ((bf16[4,384,256]{2,1,0:T(8,128)(2,1)}), bf16[4,384,256]{2,1,0:T(8,128)(2,1)S(1)}, u32[]{:S(2)}, u32[]{:S(2)}) async-start(bf16[4,384,256]{2,1,0:T(8,128)(2,1)} %broadcast_in_dim.39), calls=%async_computation.6 | async-start | bytes 1572864 | tf_op jit(solution)/shard_map/cond/branch_0_fun/all_to_all | solution.py:34
  156.6 7.6 %collective-permute-done.10.refs_3_ = bf16[896,256]{1,0:T(8,128)(2,1)S(1)} collective-permute-done((bf16[896,256]{1,0:T(8,128)(2,1)S(1)}, bf16[896,256]{1,0:T(8,128)(2,1)S(1)}, u32[]{:S(2)}, u32[]{:S(2)}) %collective-permute-start.10) | collective-permute-done | bytes 458784 | tf_op jit(solution)/shard_map/cond/branch_0_fun/ppermute | solution.py:43
  164.2 6.4 %collective-permute-done.8.refs_1_ = bf16[896,256]{1,0:T(8,128)(2,1)} collective-permute-done((bf16[896,256]{1,0:T(8,128)(2,1)S(1)}, bf16[896,256]{1,0:T(8,128)(2,1)}, u32[]{:S(2)}, u32[]{:S(2)}) %collective-permute-start.8) | collective-permute-done | bytes 458784 | tf_op jit(solution)/shard_map/cond/branch_0_fun/ppermute | solution.py:43
  170.6 2.4 %sum_grads.4 = (f32[320,256]{1,0:T(8,128)S(1)}, f32[320,256]{1,0:T(8,128)}, f32[128,256]{1,0:T(8,128)}, f32[256,128]{1,0:T(8,128)S(1)}) custom-call(bf16[896,256]{1,0:T(8,128)(2,1)} %get-tuple-element.256.refs_0_, bf16[896,256]{1,0:T(8,128)(2,1)} %collective-permute-done.8.refs_1_, bf16[896,256]{1,0:T(8,128)(2,1)} %collective-permute-done.9.refs_2_, ...), custom_call_target="tpu_custom_call" | custom-call | flops 20000000000 | bytes 4194304 | tf_op jit(solution)/shard_map/cond/branch_0_fun/sum_grads/pallas_call | solution.py:65
  173.9 0.8 pad_maximum_fusion
  174.8 3.5 %all-to-all-start.7 = ((bf16[4,256,256]{2,1,0:T(8,128)(2,1)}), bf16[4,256,256]{2,1,0:T(8,128)(2,1)S(1)}, u32[]{:S(2)}, u32[]{:S(2)}) async-start(bf16[4,256,256]{2,1,0:T(8,128)(2,1)} %pad_maximum_fusion), calls=%async_computation.7 | async-start | bytes 1048576 | tf_op jit(solution)/shard_map/cond/branch_0_fun/all_to_all | solution.py:34
  178.9 8.4 %all-to-all-done.7 = bf16[4,256,256]{2,1,0:T(8,128)(2,1)S(1)} async-done(((bf16[4,256,256]{2,1,0:T(8,128)(2,1)}), bf16[4,256,256]{2,1,0:T(8,128)(2,1)S(1)}, u32[]{:S(2)}, u32[]{:S(2)}) %all-to-all-start.7) | async-done | bytes 524320 | tf_op jit(solution)/shard_map/cond/branch_0_fun/all_to_all | solution.py:34
  (96 shorter events, 4.2 us)
Async XLA Ops:
  5.6 33.5 %all-to-all-start = ((bf16[32,8,128]{2,1,0:T(8,128)(2,1)}), bf16[32,8,128]{2,1,0:T(8,128)(2,1)S(1)}, u32[]{:S(2)}, u32[]{:S(2)}) async-start(bf16[32,8,128]{2,1,0:T(8,128)(2,1)} %pad_maximum_fusion.2), calls=%async_computation | async-start | bytes 131072 | tf_op jit(solution)/shard_map/cond/branch_0_fun/all_to_all | solution.py:34
  22.4 25.2 %copy-start.16 = (bf16[128,256]{1,0:T(8,128)(2,1)S(1)}, bf16[128,256]{1,0:T(8,128)(2,1)}, u32[]{:S(2)}) copy-start(bf16[128,256]{1,0:T(8,128)(2,1)} %get-tuple-element.96.refs_1_.refs_2_.refs_0_) | copy-start | bytes 196612
  22.4 25.2 %copy-start.20 = (bf16[128,256]{1,0:T(8,128)(2,1)S(1)}, bf16[128,256]{1,0:T(8,128)(2,1)}, u32[]{:S(2)}) copy-start(bf16[128,256]{1,0:T(8,128)(2,1)} %get-tuple-element.97.refs_2_.refs_3_.refs_1_) | copy-start | bytes 196612
  22.4 25.2 %copy-start.53 = (bf16[1,1,5,256,256]{4,3,2,1,0:T(8,128)(2,1)S(1)}, bf16[1,1,5,256,256]{4,3,2,1,0:T(8,128)(2,1)}, u32[]{:S(2)}) copy-start(bf16[1,1,5,256,256]{4,3,2,1,0:T(8,128)(2,1)} %get-tuple-element.98) | copy-start | bytes 1966084
  22.4 25.2 %copy-start.57 = (bf16[1,1,5,256,256]{4,3,2,1,0:T(8,128)(2,1)S(1)}, bf16[1,1,5,256,256]{4,3,2,1,0:T(8,128)(2,1)}, u32[]{:S(2)}) copy-start(bf16[1,1,5,256,256]{4,3,2,1,0:T(8,128)(2,1)} %get-tuple-element.99) | copy-start | bytes 1966084
  22.4 25.2 %copy-start.97 = (s32[4]{0:T(128)S(1)}, s32[4]{0:T(128)}, u32[]{:S(2)}) copy-start(s32[4]{0:T(128)} %get-tuple-element.100.refs_0_.refs_1_) | copy-start | bytes 52
  24.9 45.8 %collective-permute-start = (bf16[2,128,256]{2,1,0:T(8,128)(2,1)}, bf16[2,128,256]{2,1,0:T(8,128)(2,1)S(1)}, u32[]{:S(2)}, u32[]{:S(2)}) collective-permute-start(bf16[2,128,256]{2,1,0:T(8,128)(2,1)} %get-tuple-element.101), channel_id=1, source_target_pairs={{0,32},{4,36},{8,40},{12,44},{16,48},{20,52},{24,56},{28,60},{32,0... | collective-permute-start | bytes 393224 | tf_op jit(solution)/shard_map/cond/branch_0_fun/ppermute | solution.py:26
  32.1 38.6 %collective-permute-start.1 = (bf16[2,128,256]{2,1,0:T(8,128)(2,1)}, bf16[2,128,256]{2,1,0:T(8,128)(2,1)S(1)}, u32[]{:S(2)}, u32[]{:S(2)}) collective-permute-start(bf16[2,128,256]{2,1,0:T(8,128)(2,1)} %get-tuple-element.102), channel_id=1, source_target_pairs={{0,64},{4,68},{8,72},{12,76},{16,80},{20,84},{24,88},{28,92},{32,9... | collective-permute-start | bytes 393224 | tf_op jit(solution)/shard_map/cond/branch_0_fun/ppermute | solution.py:26
  39.2 8.4 %copy-start.50 = (bf16[8,128]{1,0:T(8,128)(2,1)}, bf16[8,128]{1,0:T(8,128)(2,1)S(1)}, u32[]{:S(2)}) copy-start(bf16[8,128]{1,0:T(8,128)(2,1)S(1)} %reduce_sum.204.refs_0_) | copy-start | bytes 6148
  39.8 24.5 %all-to-all-start.1 = ((bf16[32,8,128]{2,1,0:T(8,128)(2,1)}), bf16[32,8,128]{2,1,0:T(8,128)(2,1)S(1)}, u32[]{:S(2)}, u32[]{:S(2)}) async-start(bf16[32,8,128]{2,1,0:T(8,128)(2,1)} %broadcast_in_dim.36), calls=%async_computation.1 | async-start | bytes 131072 | tf_op jit(solution)/shard_map/cond/branch_0_fun/all_to_all | solution.py:34
  49.1 21.6 %collective-permute-start.2 = (bf16[2,128,256]{2,1,0:T(8,128)(2,1)}, bf16[2,128,256]{2,1,0:T(8,128)(2,1)S(1)}, u32[]{:S(2)}, u32[]{:S(2)}) collective-permute-start(bf16[2,128,256]{2,1,0:T(8,128)(2,1)} %get-tuple-element.105), channel_id=1, source_target_pairs={{0,8},{4,12},{8,0},{12,4},{16,24},{20,28},{24,16},{28,20},{32,40},... | collective-permute-start | bytes 393224 | tf_op jit(solution)/shard_map/cond/branch_0_fun/ppermute | solution.py:26
  52.4 18.3 %collective-permute-start.3 = (bf16[2,128,256]{2,1,0:T(8,128)(2,1)}, bf16[2,128,256]{2,1,0:T(8,128)(2,1)S(1)}, u32[]{:S(2)}, u32[]{:S(2)}) collective-permute-start(bf16[2,128,256]{2,1,0:T(8,128)(2,1)} %get-tuple-element.106), channel_id=1, source_target_pairs={{0,16},{4,20},{8,24},{12,28},{16,0},{20,4},{24,8},{28,12},{32,48},... | collective-permute-start | bytes 393224 | tf_op jit(solution)/shard_map/cond/branch_0_fun/ppermute | solution.py:26
  66.5 9.7 %all-to-all-start.2 = ((bf16[4,32,8,128]{3,2,1,0:T(8,128)(2,1)}), bf16[4,32,8,128]{3,2,1,0:T(8,128)(2,1)S(1)}, u32[]{:S(2)}, u32[]{:S(2)}) async-start(bf16[4,32,8,128]{3,2,1,0:T(8,128)(2,1)} %broadcast_in_dim.37), calls=%async_computation.2 | async-start | bytes 524288 | tf_op jit(solution)/shard_map/cond/branch_0_fun/all_to_all | solution.py:34
  70.7 6.3 %copy-start.8 = (bf16[512,1,256]{2,0,1:T(8,128)(2,1)S(1)}, bf16[512,1,256]{2,0,1:T(8,128)(2,1)}, u32[]{:S(2)}) copy-start(bf16[512,1,256]{2,0,1:T(8,128)(2,1)} %get-tuple-element.107) | copy-start | bytes 786436
  70.7 6.3 %copy-start.12 = (bf16[1,256,512]{2,1,0:T(8,128)(2,1)S(1)}, bf16[1,256,512]{2,1,0:T(8,128)(2,1)}, u32[]{:S(2)}) copy-start(bf16[1,256,512]{2,1,0:T(8,128)(2,1)} %get-tuple-element.108) | copy-start | bytes 786436
  70.7 0.7 copy-start.81
  70.7 0.7 copy-start.85
  70.7 0.7 copy-start.89
  79.2 17.8 %all-to-all-start.3 = ((bf16[4,32,1024]{2,1,0:T(8,128)(2,1)}), bf16[4,32,1024]{2,1,0:T(8,128)(2,1)S(1)}, u32[]{:S(2)}, u32[]{:S(2)}) async-start(bf16[4,32,1024]{2,1,0:T(8,128)(2,1)} %bitcast.168), calls=%async_computation.3 | async-start | bytes 524288 | tf_op jit(solution)/shard_map/cond/branch_0_fun/all_to_all | solution.py:34
  82.6 49.3 %collective-permute-start.7 = (bf16[2,128,256]{2,1,0:T(8,128)(2,1)}, bf16[2,128,256]{2,1,0:T(8,128)(2,1)S(1)}, u32[]{:S(2)}, u32[]{:S(2)}) collective-permute-start(bf16[2,128,256]{2,1,0:T(8,128)(2,1)} %gate.18), channel_id=1, source_target_pairs={{0,64},{4,68},{8,72},{12,76},{16,80},{20,84},{24,88},{28,92},{32,9... | collective-permute-start | bytes 393224 | tf_op jit(solution)/shard_map/cond/branch_0_fun/ppermute | solution.py:26
  89.3 42.6 %collective-permute-start.6 = (bf16[2,128,256]{2,1,0:T(8,128)(2,1)}, bf16[2,128,256]{2,1,0:T(8,128)(2,1)S(1)}, u32[]{:S(2)}, u32[]{:S(2)}) collective-permute-start(bf16[2,128,256]{2,1,0:T(8,128)(2,1)} %gate.18), channel_id=1, source_target_pairs={{0,32},{4,36},{8,40},{12,44},{16,48},{20,52},{24,56},{28,60},{32,0... | collective-permute-start | bytes 393224 | tf_op jit(solution)/shard_map/cond/branch_0_fun/ppermute | solution.py:26
  97.1 11.1 %copy-start.28 = (bf16[32,1024]{1,0:T(8,128)(2,1)}, bf16[32,1024]{1,0:T(8,128)(2,1)S(1)}, u32[]{:S(2)}) copy-start(bf16[32,1024]{1,0:T(8,128)(2,1)S(1)} %reduce_sum.205.refs_1_) | copy-start | bytes 196612
  97.7 23.7 %all-to-all-start.4 = ((bf16[32,8,128]{2,1,0:T(8,128)(2,1)}), bf16[32,8,128]{2,1,0:T(8,128)(2,1)S(1)}, u32[]{:S(2)}, u32[]{:S(2)}) async-start(bf16[32,8,128]{2,1,0:T(8,128)(2,1)} %bitcast.68), calls=%async_computation.4 | async-start | bytes 131072 | tf_op jit(solution)/shard_map/cond/branch_0_fun/all_to_all | solution.py:34
  108.1 23.8 %collective-permute-start.5 = (bf16[2,128,256]{2,1,0:T(8,128)(2,1)}, bf16[2,128,256]{2,1,0:T(8,128)(2,1)S(1)}, u32[]{:S(2)}, u32[]{:S(2)}) collective-permute-start(bf16[2,128,256]{2,1,0:T(8,128)(2,1)} %gate.17), channel_id=1, source_target_pairs={{0,16},{4,20},{8,24},{12,28},{16,0},{20,4},{24,8},{28,12},{32,48},... | collective-permute-start | bytes 393224 | tf_op jit(solution)/shard_map/cond/branch_0_fun/ppermute | solution.py:26
  112.3 19.6 %collective-permute-start.4 = (bf16[2,128,256]{2,1,0:T(8,128)(2,1)}, bf16[2,128,256]{2,1,0:T(8,128)(2,1)S(1)}, u32[]{:S(2)}, u32[]{:S(2)}) collective-permute-start(bf16[2,128,256]{2,1,0:T(8,128)(2,1)} %gate.17), channel_id=1, source_target_pairs={{0,8},{4,12},{8,0},{12,4},{16,24},{20,28},{24,16},{28,20},{32,40},... | collective-permute-start | bytes 393224 | tf_op jit(solution)/shard_map/cond/branch_0_fun/ppermute | solution.py:26
  121.5 10.5 %copy-start.45 = (bf16[8,128]{1,0:T(8,128)(2,1)}, bf16[8,128]{1,0:T(8,128)(2,1)S(1)}, u32[]{:S(2)}) copy-start(bf16[8,128]{1,0:T(8,128)(2,1)S(1)} %reduce_sum.206.refs_0_) | copy-start | bytes 6148
  122.1 27.6 %all-to-all-start.5 = ((bf16[32,8,128]{2,1,0:T(8,128)(2,1)}), bf16[32,8,128]{2,1,0:T(8,128)(2,1)S(1)}, u32[]{:S(2)}, u32[]{:S(2)}) async-start(bf16[32,8,128]{2,1,0:T(8,128)(2,1)} %broadcast_in_dim.38), calls=%async_computation.5 | async-start | bytes 131072 | tf_op jit(solution)/shard_map/cond/branch_0_fun/all_to_all | solution.py:34
  131.9 0.7 copy-start.65
  131.9 0.7 copy-start.69
  131.9 0.7 copy-start.73
  131.9 0.7 copy-start.77
  134.9 3.1 %copy-start.38 = (bf16[128,512]{1,0:T(8,128)(2,1)S(1)}, bf16[128,512]{1,0:T(8,128)(2,1)}, u32[]{:S(2)}) copy-start(bf16[128,512]{1,0:T(8,128)(2,1)} %block_outputs.4) | copy-start | bytes 393220
  140.4 23.7 %collective-permute-start.10 = (bf16[896,256]{1,0:T(8,128)(2,1)S(1)}, bf16[896,256]{1,0:T(8,128)(2,1)S(1)}, u32[]{:S(2)}, u32[]{:S(2)}) collective-permute-start(bf16[896,256]{1,0:T(8,128)(2,1)S(1)} %get-tuple-element.253), channel_id=1, source_target_pairs={{0,384},{128,0},{256,128},{384,256},{1,385},{129,1},{257,129},{385... | collective-permute-start | bytes 1376264 | tf_op jit(solution)/shard_map/cond/branch_0_fun/ppermute | solution.py:43
  144.8 19.4 %collective-permute-start.9 = (bf16[896,256]{1,0:T(8,128)(2,1)S(1)}, bf16[896,256]{1,0:T(8,128)(2,1)}, u32[]{:S(2)}, u32[]{:S(2)}) collective-permute-start(bf16[896,256]{1,0:T(8,128)(2,1)S(1)} %get-tuple-element.254), channel_id=1, source_target_pairs={{0,256},{128,384},{256,0},{384,128},{1,257},{129,385},{257,1},{385... | collective-permute-start | bytes 1376264 | tf_op jit(solution)/shard_map/cond/branch_0_fun/ppermute | solution.py:43
  147.3 23.3 %collective-permute-start.8 = (bf16[896,256]{1,0:T(8,128)(2,1)S(1)}, bf16[896,256]{1,0:T(8,128)(2,1)}, u32[]{:S(2)}, u32[]{:S(2)}) collective-permute-start(bf16[896,256]{1,0:T(8,128)(2,1)S(1)} %get-tuple-element.255), channel_id=1, source_target_pairs={{0,128},{128,256},{256,384},{384,0},{1,129},{129,257},{257,385},{3... | collective-permute-start | bytes 1376264 | tf_op jit(solution)/shard_map/cond/branch_0_fun/ppermute | solution.py:43
  152.4 20.7 %all-to-all-start.6 = ((bf16[4,384,256]{2,1,0:T(8,128)(2,1)}), bf16[4,384,256]{2,1,0:T(8,128)(2,1)S(1)}, u32[]{:S(2)}, u32[]{:S(2)}) async-start(bf16[4,384,256]{2,1,0:T(8,128)(2,1)} %broadcast_in_dim.39), calls=%async_computation.6 | async-start | bytes 1572864 | tf_op jit(solution)/shard_map/cond/branch_0_fun/all_to_all | solution.py:34
  164.2 6.4 %copy-start.61 = (bf16[896,256]{1,0:T(8,128)(2,1)}, bf16[896,256]{1,0:T(8,128)(2,1)S(1)}, u32[]{:S(2)}) copy-start(bf16[896,256]{1,0:T(8,128)(2,1)S(1)} %collective-permute-done.10.refs_3_) | copy-start | bytes 1376260
  173.5 4.8 %copy-start.32 = (f32[128,256]{1,0:T(8,128)S(1)}, f32[128,256]{1,0:T(8,128)}, u32[]{:S(2)}) copy-start(f32[128,256]{1,0:T(8,128)} %get-tuple-element.120) | copy-start | bytes 393220
  173.8 4.7 %copy-start = (bf16[256,512]{1,0:T(8,128)(2,1)S(1)}, bf16[256,512]{1,0:T(8,128)(2,1)}, u32[]{:S(2)}) copy-start(bf16[256,512]{1,0:T(8,128)(2,1)} %get-tuple-element.103) | copy-start | bytes 786436
  173.8 4.8 %copy-start.4 = (bf16[512,256]{1,0:T(8,128)(2,1)S(1)}, bf16[512,256]{1,0:T(8,128)(2,1)}, u32[]{:S(2)}) copy-start(bf16[512,256]{1,0:T(8,128)(2,1)} %get-tuple-element.104) | copy-start | bytes 786436
  174.8 12.5 %all-to-all-start.7 = ((bf16[4,256,256]{2,1,0:T(8,128)(2,1)}), bf16[4,256,256]{2,1,0:T(8,128)(2,1)S(1)}, u32[]{:S(2)}, u32[]{:S(2)}) async-start(bf16[4,256,256]{2,1,0:T(8,128)(2,1)} %pad_maximum_fusion), calls=%async_computation.7 | async-start | bytes 1048576 | tf_op jit(solution)/shard_map/cond/branch_0_fun/all_to_all | solution.py:34
  188.0 0.7 copy-start.36
  188.1 0.7 copy-start.37
  188.1 0.7 copy-start.42
  188.1 0.7 copy-start.43
  188.1 0.7 copy-start.44
  188.1 0.8 copy-start.101
  188.1 0.9 copy-start.102
  (2 other events, 1.3 us)

commit v3 on v2

--- a/solution.py
+++ b/solution.py
@@ -13,8 +13,8 @@
 bf16 = jnp.bfloat16
 BITS = 5
 SLOTS = 5
-FIRST = (4, 3)
-FIRST_A = (4, 3)
+FIRST = (4,)
+FIRST_A = (4,)
 LONG = 20 * 10**9
 VMEM_LIMIT = 60 * 2**20
 VM = pl.BlockSpec(memory_space=pltpu.VMEM)
@@ -65,8 +65,7 @@
     return lambda *values: call(*tokens, *values)
 
 
-def gate(value, after=None):
-    tokens = [] if after is None else [after]
+def gate(value, *tokens):
     return pl.pallas_call(
         lambda *refs: None,
         in_specs=[pl.BlockSpec(memory_space=pl.ANY)] * (1 + len(tokens)),
@@ -254,9 +253,9 @@
     )(strides, tokens, cotangent, latent, hd, *near)
     mine = spread(row, "in", n_in).reshape(share, wide)
     me = lax.axis_index("dp")
-    grads = [pick(grads, me)] + [ring(pick(grads, (me + d) % n_dp), "dp", d) for d in range(1, n_dp)]
+    sums = [pick(grads, me)] + [ring(pick(grads, (me + d) % n_dp), "dp", d) for d in range(1, n_dp)]
     both = jnp.concatenate([mine.reshape(share * wide // 256, 256), blocks.reshape(count * 2 * size // 256, 256)])
-    both = spread(gate(both), "out", n_out)
+    both = spread(gate(both, grads), "out", n_out)
     cut = share * wide // 256
     cf = both[:, :cut].reshape(count, wide)
     blocks = jnp.sum(both[:, cut:].astype(f32), axis=0).reshape(count, 2 * size)
@@ -264,16 +263,16 @@
     parts = jnp.concatenate(
         [dot(f, tokens, 0, 0).reshape(n_dp, take, size), dot(c, cotangent, 0, 0).reshape(n_dp, take, size)], axis=1
     ).astype(bf16)
+    sums[0] = gate(sums[0], *sums[1:])
+    parts, sums[0] = together(parts, sums[0])
     first_grad, second_grad, right1_grad, left2_grad = kernel_call(
         sum_grads,
         [VM] * n_dp,
         [((rows, size), f32), ((rows, size), f32), ((take, size), f32), ((size, take), f32)],
         LONG,
         "sum_grads",
-    )(*grads)
-    parts, first_grad, second_grad, right1_grad, left2_grad = together(
-        parts, first_grad, second_grad, right1_grad, left2_grad
-    )
+        parts,
+    )(*sums)
     parts = exchange(parts, "dp")
     output = (blocks[:, :size] + dot(c, second_right, 1, 0)).astype(bf16)
     input_grad = (blocks[:, size:] + dot(f, first_left, 1, 1)).astype(bf16)

time: 189 us -> 175 us (0.926)
  waiting for transfers between devices: 38.5 us -> 26.4 us
  starting transfers between devices: 112 us -> 108 us
    all_to_all x8, waiting for transfers between devices: 24.4 us -> 5.13 us  [exchange(): return lax.all_to_all(parts, axes, 0, 0, tiled=True)]
    all_to_all x8, starting transfers between devices: 59.8 us -> 49.7 us  [exchange(): return lax.all_to_all(parts, axes, 0, 0, tiled=True)]
    ppermute x8, waiting for transfers between devices: 0.02 us -> 6.63 us  [swap_bit(): return lax.ppermute(block, 'in', [(i, i ^ 1 << bit) for i in range(count)])]
    ppermute x8, starting transfers between devices: 43.2 us -> 49.4 us  [swap_bit(): return lax.ppermute(block, 'in', [(i, i ^ 1 << bit) for i in range(count)])]
    unnamed x66 -> x68, local copies, waits for them, and re-layouts: 5.25 us -> 5.57 us
  transfers between devices with their start and end apart: 19 -> 19, of which waited for: 6 -> 5; matrix products, arithmetic and copies ran while one was open for 5% -> 6% of each run, Pallas kernels for 7% -> 8%
where the time goes in v3:
time: 175 us; the launch traced here: 173 us
  starting transfers between devices  108 us (62%)
  waiting for transfers between devices  26.4 us (15%)
  Pallas kernels  15.9 us (9%)
  local copies, waits for them, and re-layouts  13 us (7%)
  other arithmetic  3.75 us (2%)
  matrix products  3.16 us (2%)
    all_to_all x8, starting transfers between devices, exchange(): return lax.all_to_all(parts, axes, 0, 0, tiled=True)  49.7 us
    ppermute x8, starting transfers between devices, swap_bit(): return lax.ppermute(block, 'in', [(i, i ^ 1 << bit) for i in range(count)])  49.4 us
    pallas_call x7, Pallas kernels, kernel_call(): return lambda *values: call(*tokens, *values)  15.9 us
    ppermute x3, waiting for transfers between devices, ring(): lax.ppermute(block, axis, [(i, (i + distance) % count) for i in range(cou...  14.7 us
    ppermute x3, starting transfers between devices, ring(): lax.ppermute(block, axis, [(i, (i + distance) % count) for i in range(cou...  9.32 us
    ppermute x8, waiting for transfers between devices, swap_bit(): return lax.ppermute(block, 'in', [(i, i ^ 1 << bit) for i in range(count)])  6.63 us
    unnamed x68, local copies, waits for them, and re-layouts  5.57 us
    all_to_all x8, waiting for transfers between devices, exchange(): return lax.all_to_all(parts, axes, 0, 0, tiled=True)  5.13 us
  transfers between devices with their start and end apart: 19, of which 5 were waited for; matrix products, arithmetic and copies ran while one was open for 6% of the time, Pallas kernels for 8%

profile of v3, /device:TPU:1, one launch (start us, length us, event | category | flops | bytes accessed | tf_op | source)
XLA Modules:
  0.0 173.3 jit_solution(11072006765994678842)
XLA Ops:
  0.6 1.3 reduce_sum.225
  2.6 169.7 %conditional.4 = (f32[1,1,5,64,256]{4,3,2,1,0:T(8,128)S(1)}, f32[1,1,5,64,256]{4,3,2,1,0:T(8,128)S(1)}, f32[1,256,128]{2,1,0:T(8,128)S(1)}, f32[128,256]{1,0:T(8...) conditional(s32[]{:T(128)} %clamp.3, ...), branch_computations={%region_1.7_spmd, %region_7.13_spmd, %region_13.19_spmd, %region_1... | conditional | flops 220422488064 | bytes 84731960
  2.8 1.1 convolution_convert_fusion.11
  4.0 1.1 convolution_convert_fusion.10
  5.2 0.7 pad_maximum_fusion.8
  5.8 16.7 %all-to-all-start.16 = ((bf16[32,8,128]{2,1,0:T(8,128)(2,1)}), bf16[32,8,128]{2,1,0:T(8,128)(2,1)S(1)}, u32[]{:S(2)}, u32[]{:S(2)}) async-start(bf16[32,8,128]{2,1,0:T(8,128)(2,1)} %pad_maximum_fusion.8), calls=%async_computation.16 | async-start | bytes 131072 | tf_op jit(solution)/shard_map/cond/branch_2_fun/all_to_all | solution.py:34
  22.7 2.3 %products.12 = bf16[2,128,256]{2,1,0:T(8,128)(2,1)} custom-call(s32[4]{0:T(128)} %get-tuple-element.144.refs_0_.refs_1_, bf16[128,256]{1,0:T(8,128)(2,1)} %get-tuple-element.140.refs_1_.refs_2_.refs_0_, bf16[128,256]{1,0:T(8,128)(2,1)} %get-tuple-element.141.refs_2_.refs_3_.refs_1_, bf16[5,256,256]{2,1,0:T(8,128)(2,1)} %bitcast.184, ...), custom_call_target="tpu_custom_call" | custom-call | flops 20000000000 | bytes 4194304 | tf_op jit(solution)/shard_map/cond/branch_2_fun/products/pallas_call | solution.py:65
  25.0 12.0 %collective-permute-start.22 = (bf16[2,128,256]{2,1,0:T(8,128)(2,1)}, bf16[2,128,256]{2,1,0:T(8,128)(2,1)S(1)}, u32[]{:S(2)}, u32[]{:S(2)}) collective-permute-start(bf16[2,128,256]{2,1,0:T(8,128)(2,1)} %products.12), channel_id=1, source_target_pairs={{0,64},{4,68},{8,72},{12,76},{16,80},{20,84},{24,88},{28,92},{32,9... | collective-permute-start | bytes 393224 | tf_op jit(solution)/shard_map/cond/branch_2_fun/ppermute | solution.py:26
  37.1 0.6 broadcast_in_dim.72
  37.7 4.1 %all-to-all-start.17 = ((bf16[32,8,128]{2,1,0:T(8,128)(2,1)}), bf16[32,8,128]{2,1,0:T(8,128)(2,1)S(1)}, u32[]{:S(2)}, u32[]{:S(2)}) async-start(bf16[32,8,128]{2,1,0:T(8,128)(2,1)} %broadcast_in_dim.72), calls=%async_computation.17 | async-start | bytes 131072 | tf_op jit(solution)/shard_map/cond/branch_2_fun/all_to_all | solution.py:34
  41.9 1.5 products.13
  43.5 2.2 %collective-permute-start.23 = (bf16[2,128,256]{2,1,0:T(8,128)(2,1)}, bf16[2,128,256]{2,1,0:T(8,128)(2,1)S(1)}, u32[]{:S(2)}, u32[]{:S(2)}) collective-permute-start(bf16[2,128,256]{2,1,0:T(8,128)(2,1)} %get-tuple-element.147), channel_id=1, source_target_pairs={{0,4},{4,0},{8,12},{12,8},{16,20},{20,16},{24,28},{28,24},{32,36},... | collective-permute-start | bytes 393224 | tf_op jit(solution)/shard_map/cond/branch_2_fun/ppermute | solution.py:26
  45.7 3.3 %collective-permute-start.24 = (bf16[2,128,256]{2,1,0:T(8,128)(2,1)}, bf16[2,128,256]{2,1,0:T(8,128)(2,1)S(1)}, u32[]{:S(2)}, u32[]{:S(2)}) collective-permute-start(bf16[2,128,256]{2,1,0:T(8,128)(2,1)} %get-tuple-element.148), channel_id=1, source_target_pairs={{0,8},{4,12},{8,0},{12,4},{16,24},{20,28},{24,16},{28,20},{32,40},... | collective-permute-start | bytes 393224 | tf_op jit(solution)/shard_map/cond/branch_2_fun/ppermute | solution.py:26
  49.0 7.1 %collective-permute-start.25 = (bf16[2,128,256]{2,1,0:T(8,128)(2,1)}, bf16[2,128,256]{2,1,0:T(8,128)(2,1)S(1)}, u32[]{:S(2)}, u32[]{:S(2)}) collective-permute-start(bf16[2,128,256]{2,1,0:T(8,128)(2,1)} %get-tuple-element.149), channel_id=1, source_target_pairs={{0,32},{4,36},{8,40},{12,44},{16,48},{20,52},{24,56},{28,60},{32,0... | collective-permute-start | bytes 393224 | tf_op jit(solution)/shard_map/cond/branch_2_fun/ppermute | solution.py:26
  56.1 0.6 copy-done.26
  56.7 1.6 broadcast_in_dim.73
  58.3 4.2 %all-to-all-start.18 = ((bf16[4,32,8,128]{3,2,1,0:T(8,128)(2,1)}), bf16[4,32,8,128]{3,2,1,0:T(8,128)(2,1)S(1)}, u32[]{:S(2)}, u32[]{:S(2)}) async-start(bf16[4,32,8,128]{3,2,1,0:T(8,128)(2,1)} %broadcast_in_dim.73), calls=%async_computation.18 | async-start | bytes 524288 | tf_op jit(solution)/shard_map/cond/branch_2_fun/all_to_all | solution.py:34
  62.6 5.6 %collective-permute-done.25.refs_7_ = bf16[2,128,256]{2,1,0:T(8,128)(2,1)S(1)} collective-permute-done((bf16[2,128,256]{2,1,0:T(8,128)(2,1)}, bf16[2,128,256]{2,1,0:T(8,128)(2,1)S(1)}, u32[]{:S(2)}, u32[]{:S(2)}) %collective-permute-start.25) | collective-permute-done | bytes 131104 | tf_op jit(solution)/shard_map/cond/branch_2_fun/ppermute | solution.py:26
  68.2 0.6 copy-done.95
  68.9 2.0 %sum_products.6.refs_0_ = f32[2,128,256]{2,1,0:T(8,128)} custom-call(bf16[128,256]{1,0:T(8,128)(2,1)S(1)} %copy-done.18, bf16[128,256]{1,0:T(8,128)(2,1)S(1)} %copy-done.22, bf16[5,256,256]{2,1,0:T(8,128)(2,1)S(1)} %bitcast.186, bf16[5,256,256]{2,1,0:T(8,128)(2,1)S(1)} %bitcast.202, bf16[2,128,256]{2,1,0:T(8,128)(2,1)} %copy-done.83, ...), custom_call_target="tpu_custom_call" | custom-call | flops 20000000000 | bytes 4194304 | tf_op jit(solution)/shard_map/cond/branch_2_fun/sum_products/pallas_call | solution.py:65
  70.9 0.8 copy.63
  71.6 2.2 %activations.6 = (bf16[2,128,256]{2,1,0:T(8,128)(2,1)}, bf16[2,128,256]{2,1,0:T(8,128)(2,1)}, bf16[2,128,256]{2,1,0:T(8,128)(2,1)}, bf16[128,1024]{1,0:T(8,128)(2,1)}) custom-call(f32[2,128,256]{2,1,0:T(8,128)} %sum_products.6.refs_0_, bf16[128,1024]{1,0:T(8,128)(2,1)} %bitcast.160, bf16[512,256]{1,0:T(8,128)(2,1)S(1)} %bitcast.138, ...), custom_call_target="tpu_custom_call" | custom-call | flops 268435456 | bytes 4194304 | tf_op jit(solution)/shard_map/cond/branch_2_fun/activations/pallas_call | solution.py:65
  73.8 4.2 %all-to-all-start.19 = ((bf16[4,32,1024]{2,1,0:T(8,128)(2,1)}), bf16[4,32,1024]{2,1,0:T(8,128)(2,1)S(1)}, u32[]{:S(2)}, u32[]{:S(2)}) async-start(bf16[4,32,1024]{2,1,0:T(8,128)(2,1)} %bitcast.170), calls=%async_computation.19 | async-start | bytes 524288 | tf_op jit(solution)/shard_map/cond/branch_2_fun/all_to_all | solution.py:34
  78.0 11.7 %collective-permute-start.29 = (bf16[2,128,256]{2,1,0:T(8,128)(2,1)}, bf16[2,128,256]{2,1,0:T(8,128)(2,1)S(1)}, u32[]{:S(2)}, u32[]{:S(2)}) collective-permute-start(bf16[2,128,256]{2,1,0:T(8,128)(2,1)} %gate.32), channel_id=1, source_target_pairs={{0,64},{4,68},{8,72},{12,76},{16,80},{20,84},{24,88},{28,92},{32,9... | collective-permute-start | bytes 393224 | tf_op jit(solution)/shard_map/cond/branch_2_fun/ppermute | solution.py:26
  89.8 0.6 copy.54
  90.4 7.4 %all-to-all-start.20 = ((bf16[32,8,128]{2,1,0:T(8,128)(2,1)}), bf16[32,8,128]{2,1,0:T(8,128)(2,1)S(1)}, u32[]{:S(2)}, u32[]{:S(2)}) async-start(bf16[32,8,128]{2,1,0:T(8,128)(2,1)} %bitcast.78), calls=%async_computation.20 | async-start | bytes 131072 | tf_op jit(solution)/shard_map/cond/branch_2_fun/all_to_all | solution.py:34
  97.9 7.2 %collective-permute-start.28 = (bf16[2,128,256]{2,1,0:T(8,128)(2,1)}, bf16[2,128,256]{2,1,0:T(8,128)(2,1)S(1)}, u32[]{:S(2)}, u32[]{:S(2)}) collective-permute-start(bf16[2,128,256]{2,1,0:T(8,128)(2,1)} %gate.31), channel_id=1, source_target_pairs={{0,32},{4,36},{8,40},{12,44},{16,48},{20,52},{24,56},{28,60},{32,0... | collective-permute-start | bytes 393224 | tf_op jit(solution)/shard_map/cond/branch_2_fun/ppermute | solution.py:26
  105.1 3.1 %collective-permute-start.27 = (bf16[2,128,256]{2,1,0:T(8,128)(2,1)}, bf16[2,128,256]{2,1,0:T(8,128)(2,1)S(1)}, u32[]{:S(2)}, u32[]{:S(2)}) collective-permute-start(bf16[2,128,256]{2,1,0:T(8,128)(2,1)} %gate.31), channel_id=1, source_target_pairs={{0,8},{4,12},{8,0},{12,4},{16,24},{20,28},{24,16},{28,20},{32,40},... | collective-permute-start | bytes 393224 | tf_op jit(solution)/shard_map/cond/branch_2_fun/ppermute | solution.py:26
  108.2 2.8 %collective-permute-start.26 = (bf16[2,128,256]{2,1,0:T(8,128)(2,1)}, bf16[2,128,256]{2,1,0:T(8,128)(2,1)S(1)}, u32[]{:S(2)}, u32[]{:S(2)}) collective-permute-start(bf16[2,128,256]{2,1,0:T(8,128)(2,1)} %gate.31), channel_id=1, source_target_pairs={{0,4},{4,0},{8,12},{12,8},{16,20},{20,16},{24,28},{28,24},{32,36},... | collective-permute-start | bytes 393224 | tf_op jit(solution)/shard_map/cond/branch_2_fun/ppermute | solution.py:26
  111.1 0.6 broadcast_in_dim.74
  111.8 6.1 %all-to-all-start.21 = ((bf16[32,8,128]{2,1,0:T(8,128)(2,1)}), bf16[32,8,128]{2,1,0:T(8,128)(2,1)S(1)}, u32[]{:S(2)}, u32[]{:S(2)}) async-start(bf16[32,8,128]{2,1,0:T(8,128)(2,1)} %broadcast_in_dim.74), calls=%async_computation.21 | async-start | bytes 131072 | tf_op jit(solution)/shard_map/cond/branch_2_fun/all_to_all | solution.py:34
  117.9 1.0 collective-permute-done.28.refs_7_.refs_8_
  119.6 2.3 %block_outputs.6 = bf16[128,512]{1,0:T(8,128)(2,1)} custom-call(bf16[8,128]{1,0:T(8,128)(2,1)} %copy-done.43, s32[4]{0:T(128)S(1)} %copy-done.99, bf16[5,256,256]{2,1,0:T(8,128)(2,1)S(1)} %bitcast.187, bf16[5,256,256]{2,1,0:T(8,128)(2,1)S(1)} %bitcast.203, bf16[2,128,256]{2,1,0:T(8,128)(2,1)} %get-tuple-element.153.refs_4_.refs_5_, ...), custom_call_target="tpu_custom_call" | custom-call | flops 20000000000 | bytes 4194304 | tf_op jit(solution)/shard_map/cond/branch_2_fun/block_outputs/pallas_call | solution.py:65
  121.9 3.1 %block_grads.6.refs_1_ = bf16[4,896,256]{2,1,0:T(8,128)(2,1)} custom-call(bf16[8,128]{1,0:T(8,128)(2,1)} %copy-done.43, s32[4]{0:T(128)S(1)} %copy-done.99, bf16[128,256]{1,0:T(8,128)(2,1)S(1)} %copy-done.18, bf16[128,256]{1,0:T(8,128)(2,1)S(1)} %copy-done.22, bf16[128,1024]{1,0:T(8,128)(2,1)} %bitcast.161, ...), custom_call_target="tpu_custom_call" | custom-call | flops 20000000000 | bytes 4194304 | tf_op jit(solution)/shard_map/cond/branch_2_fun/block_grads/pallas_call | solution.py:65
  125.0 2.3 %dynamic-slice_bitcast_fusion.8 = (bf16[896,256]{1,0:T(8,128)(2,1)S(1)}, bf16[896,256]{1,0:T(8,128)(2,1)S(1)}, bf16[896,256]{1,0:T(8,128)(2,1)S(1)}, bf16[896,256]{1,0:T(8,128)(2,1)}) fusion(bf16[4,896,256]{2,1,0:T(8,128)(2,1)} %block_grads.6.refs_1_, s32[]{:T(128)S(6)} %select_n.107, s32[]{:T(128)S(6)} %select_n.105, s32[]{:T(128)S(6)} %select_n.103, ...), kind=kLoop, calls=%fused_computation.65 | loop fusion | bytes 3670032 | tf_op jit(solution)/shard_map/cond/branch_2_fun/jit(dynamic_index_in_dim)/squeeze | solution.py:47
  127.4 4.4 %collective-permute-start.32 = (bf16[896,256]{1,0:T(8,128)(2,1)S(1)}, bf16[896,256]{1,0:T(8,128)(2,1)S(1)}, u32[]{:S(2)}, u32[]{:S(2)}) collective-permute-start(bf16[896,256]{1,0:T(8,128)(2,1)S(1)} %get-tuple-element.250), channel_id=1, source_target_pairs={{0,384},{128,0},{256,128},{384,256},{1,385},{129,1},{257,129},{385... | collective-permute-start | bytes 1376264 | tf_op jit(solution)/shard_map/cond/branch_2_fun/ppermute | solution.py:43
  131.8 2.4 %collective-permute-start.31 = (bf16[896,256]{1,0:T(8,128)(2,1)S(1)}, bf16[896,256]{1,0:T(8,128)(2,1)S(1)}, u32[]{:S(2)}, u32[]{:S(2)}) collective-permute-start(bf16[896,256]{1,0:T(8,128)(2,1)S(1)} %get-tuple-element.251), channel_id=1, source_target_pairs={{0,256},{128,384},{256,0},{384,128},{1,257},{129,385},{257,1},{385... | collective-permute-start | bytes 1376264 | tf_op jit(solution)/shard_map/cond/branch_2_fun/ppermute | solution.py:43
  134.2 2.5 %collective-permute-start.30 = (bf16[896,256]{1,0:T(8,128)(2,1)S(1)}, bf16[896,256]{1,0:T(8,128)(2,1)}, u32[]{:S(2)}, u32[]{:S(2)}) collective-permute-start(bf16[896,256]{1,0:T(8,128)(2,1)S(1)} %get-tuple-element.252), channel_id=1, source_target_pairs={{0,128},{128,256},{256,384},{384,0},{1,129},{129,257},{257,385},{3... | collective-permute-start | bytes 1376264 | tf_op jit(solution)/shard_map/cond/branch_2_fun/ppermute | solution.py:43
  136.8 0.7 pad_maximum_fusion.7.refs_0_
  137.5 1.9 %broadcast_in_dim.75 = bf16[4,384,256]{2,1,0:T(8,128)(2,1)} broadcast(bf16[384,256]{1,0:T(8,128)(2,1)} %gate.33), dimensions={1,2} | broadcast | bytes 983040 | tf_op jit(solution)/shard_map/cond/branch_2_fun/broadcast_in_dim | solution.py:38
  139.3 3.5 %all-to-all-start.22 = ((bf16[4,384,256]{2,1,0:T(8,128)(2,1)}), bf16[4,384,256]{2,1,0:T(8,128)(2,1)S(1)}, u32[]{:S(2)}, u32[]{:S(2)}) async-start(bf16[4,384,256]{2,1,0:T(8,128)(2,1)} %broadcast_in_dim.75), calls=%async_computation.22 | async-start | bytes 1572864 | tf_op jit(solution)/shard_map/cond/branch_2_fun/all_to_all | solution.py:34
  142.9 3.2 %collective-permute-done.31.refs_2_.refs_3_ = bf16[896,256]{1,0:T(8,128)(2,1)S(1)} collective-permute-done((bf16[896,256]{1,0:T(8,128)(2,1)S(1)}, bf16[896,256]{1,0:T(8,128)(2,1)S(1)}, u32[]{:S(2)}, u32[]{:S(2)}) %collective-permute-start.31) | collective-permute-done | bytes 458784 | tf_op jit(solution)/shard_map/cond/branch_2_fun/ppermute | solution.py:43
  146.1 11.4 %collective-permute-done.30.refs_1_.refs_2_ = bf16[896,256]{1,0:T(8,128)(2,1)} collective-permute-done((bf16[896,256]{1,0:T(8,128)(2,1)S(1)}, bf16[896,256]{1,0:T(8,128)(2,1)}, u32[]{:S(2)}, u32[]{:S(2)}) %collective-permute-start.30) | collective-permute-done | bytes 458784 | tf_op jit(solution)/shard_map/cond/branch_2_fun/ppermute | solution.py:43
  158.4 0.8 pad_maximum_fusion.6.refs_0_
  159.3 3.5 %all-to-all-start.23 = ((bf16[4,256,256]{2,1,0:T(8,128)(2,1)}), bf16[4,256,256]{2,1,0:T(8,128)(2,1)S(1)}, u32[]{:S(2)}, u32[]{:S(2)}) async-start(bf16[4,256,256]{2,1,0:T(8,128)(2,1)} %pad_maximum_fusion.6.refs_0_), calls=%async_computation.23 | async-start | bytes 1048576 | tf_op jit(solution)/shard_map/cond/branch_2_fun/all_to_all | solution.py:34
  162.8 2.4 %sum_grads.6 = (f32[320,256]{1,0:T(8,128)S(1)}, f32[320,256]{1,0:T(8,128)S(1)}, f32[128,256]{1,0:T(8,128)}, f32[256,128]{1,0:T(8,128)S(1)}) custom-call(bf16[4,256,256]{2,1,0:T(8,128)(2,1)} %pad_maximum_fusion.6.refs_0_, bf16[896,256]{1,0:T(8,128)(2,1)} %gate.34.refs_1_, bf16[896,256]{1,0:T(8,128)(2,1)} %collective-permute-done.30.refs_1_.refs_2_, ...), custom_call_target="tpu_custom_call" | custom-call | flops 20000000000 | bytes 4194304 | tf_op jit(solution)/shard_map/cond/branch_2_fun/sum_grads/pallas_call | solution.py:65
  165.2 1.0 copy.47
  166.7 5.1 %all-to-all-done.23 = bf16[4,256,256]{2,1,0:T(8,128)(2,1)S(1)} async-done(((bf16[4,256,256]{2,1,0:T(8,128)(2,1)}), bf16[4,256,256]{2,1,0:T(8,128)(2,1)S(1)}, u32[]{:S(2)}, u32[]{:S(2)}) %all-to-all-start.23) | async-done | bytes 524320 | tf_op jit(solution)/shard_map/cond/branch_2_fun/all_to_all | solution.py:34
  (99 shorter events, 3.5 us)
Async XLA Ops:
  5.8 31.2 %all-to-all-start.16 = ((bf16[32,8,128]{2,1,0:T(8,128)(2,1)}), bf16[32,8,128]{2,1,0:T(8,128)(2,1)S(1)}, u32[]{:S(2)}, u32[]{:S(2)}) async-start(bf16[32,8,128]{2,1,0:T(8,128)(2,1)} %pad_maximum_fusion.8), calls=%async_computation.16 | async-start | bytes 131072 | tf_op jit(solution)/shard_map/cond/branch_2_fun/all_to_all | solution.py:34
  22.6 19.3 %copy-start.18 = (bf16[128,256]{1,0:T(8,128)(2,1)S(1)}, bf16[128,256]{1,0:T(8,128)(2,1)}, u32[]{:S(2)}) copy-start(bf16[128,256]{1,0:T(8,128)(2,1)} %get-tuple-element.140.refs_1_.refs_2_.refs_0_) | copy-start | bytes 196612
  22.6 19.3 %copy-start.22 = (bf16[128,256]{1,0:T(8,128)(2,1)S(1)}, bf16[128,256]{1,0:T(8,128)(2,1)}, u32[]{:S(2)}) copy-start(bf16[128,256]{1,0:T(8,128)(2,1)} %get-tuple-element.141.refs_2_.refs_3_.refs_1_) | copy-start | bytes 196612
  22.6 19.3 %copy-start.51 = (bf16[1,1,5,256,256]{4,3,2,1,0:T(8,128)(2,1)S(1)}, bf16[1,1,5,256,256]{4,3,2,1,0:T(8,128)(2,1)}, u32[]{:S(2)}) copy-start(bf16[1,1,5,256,256]{4,3,2,1,0:T(8,128)(2,1)} %get-tuple-element.142) | copy-start | bytes 1966084
  22.6 19.3 %copy-start.55 = (bf16[1,1,5,256,256]{4,3,2,1,0:T(8,128)(2,1)S(1)}, bf16[1,1,5,256,256]{4,3,2,1,0:T(8,128)(2,1)}, u32[]{:S(2)}) copy-start(bf16[1,1,5,256,256]{4,3,2,1,0:T(8,128)(2,1)} %get-tuple-element.143) | copy-start | bytes 1966084
  22.6 19.3 %copy-start.99 = (s32[4]{0:T(128)S(1)}, s32[4]{0:T(128)}, u32[]{:S(2)}) copy-start(s32[4]{0:T(128)} %get-tuple-element.144.refs_0_.refs_1_) | copy-start | bytes 52
  25.0 37.5 %collective-permute-start.22 = (bf16[2,128,256]{2,1,0:T(8,128)(2,1)}, bf16[2,128,256]{2,1,0:T(8,128)(2,1)S(1)}, u32[]{:S(2)}, u32[]{:S(2)}) collective-permute-start(bf16[2,128,256]{2,1,0:T(8,128)(2,1)} %products.12), channel_id=1, source_target_pairs={{0,64},{4,68},{8,72},{12,76},{16,80},{20,84},{24,88},{28,92},{32,9... | collective-permute-start | bytes 393224 | tf_op jit(solution)/shard_map/cond/branch_2_fun/ppermute | solution.py:26
  37.1 4.8 %copy-start.47 = (bf16[8,128]{1,0:T(8,128)(2,1)}, bf16[8,128]{1,0:T(8,128)(2,1)S(1)}, u32[]{:S(2)}) copy-start(bf16[8,128]{1,0:T(8,128)(2,1)S(1)} %reduce_sum.214.refs_0_) | copy-start | bytes 6148
  37.7 18.4 %all-to-all-start.17 = ((bf16[32,8,128]{2,1,0:T(8,128)(2,1)}), bf16[32,8,128]{2,1,0:T(8,128)(2,1)S(1)}, u32[]{:S(2)}, u32[]{:S(2)}) async-start(bf16[32,8,128]{2,1,0:T(8,128)(2,1)} %broadcast_in_dim.72), calls=%async_computation.17 | async-start | bytes 131072 | tf_op jit(solution)/shard_map/cond/branch_2_fun/all_to_all | solution.py:34
  43.5 19.1 %collective-permute-start.23 = (bf16[2,128,256]{2,1,0:T(8,128)(2,1)}, bf16[2,128,256]{2,1,0:T(8,128)(2,1)S(1)}, u32[]{:S(2)}, u32[]{:S(2)}) collective-permute-start(bf16[2,128,256]{2,1,0:T(8,128)(2,1)} %get-tuple-element.147), channel_id=1, source_target_pairs={{0,4},{4,0},{8,12},{12,8},{16,20},{20,16},{24,28},{28,24},{32,36},... | collective-permute-start | bytes 393224 | tf_op jit(solution)/shard_map/cond/branch_2_fun/ppermute | solution.py:26
  45.7 16.8 %collective-permute-start.24 = (bf16[2,128,256]{2,1,0:T(8,128)(2,1)}, bf16[2,128,256]{2,1,0:T(8,128)(2,1)S(1)}, u32[]{:S(2)}, u32[]{:S(2)}) collective-permute-start(bf16[2,128,256]{2,1,0:T(8,128)(2,1)} %get-tuple-element.148), channel_id=1, source_target_pairs={{0,8},{4,12},{8,0},{12,4},{16,24},{20,28},{24,16},{28,20},{32,40},... | collective-permute-start | bytes 393224 | tf_op jit(solution)/shard_map/cond/branch_2_fun/ppermute | solution.py:26
  49.0 19.2 %collective-permute-start.25 = (bf16[2,128,256]{2,1,0:T(8,128)(2,1)}, bf16[2,128,256]{2,1,0:T(8,128)(2,1)S(1)}, u32[]{:S(2)}, u32[]{:S(2)}) collective-permute-start(bf16[2,128,256]{2,1,0:T(8,128)(2,1)} %get-tuple-element.149), channel_id=1, source_target_pairs={{0,32},{4,36},{8,40},{12,44},{16,48},{20,52},{24,56},{28,60},{32,0... | collective-permute-start | bytes 393224 | tf_op jit(solution)/shard_map/cond/branch_2_fun/ppermute | solution.py:26
  58.3 12.6 %all-to-all-start.18 = ((bf16[4,32,8,128]{3,2,1,0:T(8,128)(2,1)}), bf16[4,32,8,128]{3,2,1,0:T(8,128)(2,1)S(1)}, u32[]{:S(2)}, u32[]{:S(2)}) async-start(bf16[4,32,8,128]{3,2,1,0:T(8,128)(2,1)} %broadcast_in_dim.73), calls=%async_computation.18 | async-start | bytes 524288 | tf_op jit(solution)/shard_map/cond/branch_2_fun/all_to_all | solution.py:34
  62.5 9.1 %copy-start.10 = (bf16[512,1,256]{2,0,1:T(8,128)(2,1)S(1)}, bf16[512,1,256]{2,0,1:T(8,128)(2,1)}, u32[]{:S(2)}) copy-start(bf16[512,1,256]{2,0,1:T(8,128)(2,1)} %get-tuple-element.150) | copy-start | bytes 786436
  62.5 9.1 %copy-start.14 = (bf16[1,256,512]{2,1,0:T(8,128)(2,1)S(1)}, bf16[1,256,512]{2,1,0:T(8,128)(2,1)}, u32[]{:S(2)}) copy-start(bf16[1,256,512]{2,1,0:T(8,128)(2,1)} %get-tuple-element.151) | copy-start | bytes 786436
  62.5 5.7 %copy-start.83 = (bf16[2,128,256]{2,1,0:T(8,128)(2,1)}, bf16[2,128,256]{2,1,0:T(8,128)(2,1)S(1)}, u32[]{:S(2)}) copy-start(bf16[2,128,256]{2,1,0:T(8,128)(2,1)S(1)} %collective-permute-done.22.refs_4_) | copy-start | bytes 393220
  62.5 5.7 %copy-start.87 = (bf16[2,128,256]{2,1,0:T(8,128)(2,1)}, bf16[2,128,256]{2,1,0:T(8,128)(2,1)S(1)}, u32[]{:S(2)}) copy-start(bf16[2,128,256]{2,1,0:T(8,128)(2,1)S(1)} %collective-permute-done.23.refs_5_) | copy-start | bytes 393220
  62.6 5.6 %copy-start.91 = (bf16[2,128,256]{2,1,0:T(8,128)(2,1)}, bf16[2,128,256]{2,1,0:T(8,128)(2,1)S(1)}, u32[]{:S(2)}) copy-start(bf16[2,128,256]{2,1,0:T(8,128)(2,1)S(1)} %collective-permute-done.24.refs_6_) | copy-start | bytes 393220
  73.8 15.9 %all-to-all-start.19 = ((bf16[4,32,1024]{2,1,0:T(8,128)(2,1)}), bf16[4,32,1024]{2,1,0:T(8,128)(2,1)S(1)}, u32[]{:S(2)}, u32[]{:S(2)}) async-start(bf16[4,32,1024]{2,1,0:T(8,128)(2,1)} %bitcast.170), calls=%async_computation.19 | async-start | bytes 524288 | tf_op jit(solution)/shard_map/cond/branch_2_fun/all_to_all | solution.py:34
  78.0 39.8 %collective-permute-start.29 = (bf16[2,128,256]{2,1,0:T(8,128)(2,1)}, bf16[2,128,256]{2,1,0:T(8,128)(2,1)S(1)}, u32[]{:S(2)}, u32[]{:S(2)}) collective-permute-start(bf16[2,128,256]{2,1,0:T(8,128)(2,1)} %gate.32), channel_id=1, source_target_pairs={{0,64},{4,68},{8,72},{12,76},{16,80},{20,84},{24,88},{28,92},{32,9... | collective-permute-start | bytes 393224 | tf_op jit(solution)/shard_map/cond/branch_2_fun/ppermute | solution.py:26
  89.8 8.1 %copy-start.30 = (bf16[32,1024]{1,0:T(8,128)(2,1)}, bf16[32,1024]{1,0:T(8,128)(2,1)S(1)}, u32[]{:S(2)}) copy-start(bf16[32,1024]{1,0:T(8,128)(2,1)S(1)} %reduce_sum.215.refs_1_) | copy-start | bytes 196612
  90.4 20.6 %all-to-all-start.20 = ((bf16[32,8,128]{2,1,0:T(8,128)(2,1)}), bf16[32,8,128]{2,1,0:T(8,128)(2,1)S(1)}, u32[]{:S(2)}, u32[]{:S(2)}) async-start(bf16[32,8,128]{2,1,0:T(8,128)(2,1)} %bitcast.78), calls=%async_computation.20 | async-start | bytes 131072 | tf_op jit(solution)/shard_map/cond/branch_2_fun/all_to_all | solution.py:34
  97.9 21.0 %collective-permute-start.28 = (bf16[2,128,256]{2,1,0:T(8,128)(2,1)}, bf16[2,128,256]{2,1,0:T(8,128)(2,1)S(1)}, u32[]{:S(2)}, u32[]{:S(2)}) collective-permute-start(bf16[2,128,256]{2,1,0:T(8,128)(2,1)} %gate.31), channel_id=1, source_target_pairs={{0,32},{4,36},{8,40},{12,44},{16,48},{20,52},{24,56},{28,60},{32,0... | collective-permute-start | bytes 393224 | tf_op jit(solution)/shard_map/cond/branch_2_fun/ppermute | solution.py:26
  105.1 13.8 %collective-permute-start.27 = (bf16[2,128,256]{2,1,0:T(8,128)(2,1)}, bf16[2,128,256]{2,1,0:T(8,128)(2,1)S(1)}, u32[]{:S(2)}, u32[]{:S(2)}) collective-permute-start(bf16[2,128,256]{2,1,0:T(8,128)(2,1)} %gate.31), channel_id=1, source_target_pairs={{0,8},{4,12},{8,0},{12,4},{16,24},{20,28},{24,16},{28,20},{32,40},... | collective-permute-start | bytes 393224 | tf_op jit(solution)/shard_map/cond/branch_2_fun/ppermute | solution.py:26
  108.2 10.7 %collective-permute-start.26 = (bf16[2,128,256]{2,1,0:T(8,128)(2,1)}, bf16[2,128,256]{2,1,0:T(8,128)(2,1)S(1)}, u32[]{:S(2)}, u32[]{:S(2)}) collective-permute-start(bf16[2,128,256]{2,1,0:T(8,128)(2,1)} %gate.31), channel_id=1, source_target_pairs={{0,4},{4,0},{8,12},{12,8},{16,20},{20,16},{24,28},{28,24},{32,36},... | collective-permute-start | bytes 393224 | tf_op jit(solution)/shard_map/cond/branch_2_fun/ppermute | solution.py:26
  111.1 7.8 %copy-start.43 = (bf16[8,128]{1,0:T(8,128)(2,1)}, bf16[8,128]{1,0:T(8,128)(2,1)S(1)}, u32[]{:S(2)}) copy-start(bf16[8,128]{1,0:T(8,128)(2,1)S(1)} %reduce_sum.216.refs_0_) | copy-start | bytes 6148
  111.8 25.0 %all-to-all-start.21 = ((bf16[32,8,128]{2,1,0:T(8,128)(2,1)}), bf16[32,8,128]{2,1,0:T(8,128)(2,1)S(1)}, u32[]{:S(2)}, u32[]{:S(2)}) async-start(bf16[32,8,128]{2,1,0:T(8,128)(2,1)} %broadcast_in_dim.74), calls=%async_computation.21 | async-start | bytes 131072 | tf_op jit(solution)/shard_map/cond/branch_2_fun/all_to_all | solution.py:34
  117.9 1.0 copy-start.67
  118.9 0.7 copy-start.75
  118.9 0.7 copy-start.79
  121.9 3.1 %copy-start.36 = (bf16[128,512]{1,0:T(8,128)(2,1)S(1)}, bf16[128,512]{1,0:T(8,128)(2,1)}, u32[]{:S(2)}) copy-start(bf16[128,512]{1,0:T(8,128)(2,1)} %block_outputs.6) | copy-start | bytes 393220
  127.4 15.5 %collective-permute-start.32 = (bf16[896,256]{1,0:T(8,128)(2,1)S(1)}, bf16[896,256]{1,0:T(8,128)(2,1)S(1)}, u32[]{:S(2)}, u32[]{:S(2)}) collective-permute-start(bf16[896,256]{1,0:T(8,128)(2,1)S(1)} %get-tuple-element.250), channel_id=1, source_target_pairs={{0,384},{128,0},{256,128},{384,256},{1,385},{129,1},{257,129},{385... | collective-permute-start | bytes 1376264 | tf_op jit(solution)/shard_map/cond/branch_2_fun/ppermute | solution.py:43
  131.8 14.3 %collective-permute-start.31 = (bf16[896,256]{1,0:T(8,128)(2,1)S(1)}, bf16[896,256]{1,0:T(8,128)(2,1)S(1)}, u32[]{:S(2)}, u32[]{:S(2)}) collective-permute-start(bf16[896,256]{1,0:T(8,128)(2,1)S(1)} %get-tuple-element.251), channel_id=1, source_target_pairs={{0,256},{128,384},{256,0},{384,128},{1,257},{129,385},{257,1},{385... | collective-permute-start | bytes 1376264 | tf_op jit(solution)/shard_map/cond/branch_2_fun/ppermute | solution.py:43
  134.2 23.4 %collective-permute-start.30 = (bf16[896,256]{1,0:T(8,128)(2,1)S(1)}, bf16[896,256]{1,0:T(8,128)(2,1)}, u32[]{:S(2)}, u32[]{:S(2)}) collective-permute-start(bf16[896,256]{1,0:T(8,128)(2,1)S(1)} %get-tuple-element.252), channel_id=1, source_target_pairs={{0,128},{128,256},{256,384},{384,0},{1,129},{129,257},{257,385},{3... | collective-permute-start | bytes 1376264 | tf_op jit(solution)/shard_map/cond/branch_2_fun/ppermute | solution.py:43
  139.3 18.2 %all-to-all-start.22 = ((bf16[4,384,256]{2,1,0:T(8,128)(2,1)}), bf16[4,384,256]{2,1,0:T(8,128)(2,1)S(1)}, u32[]{:S(2)}, u32[]{:S(2)}) async-start(bf16[4,384,256]{2,1,0:T(8,128)(2,1)} %broadcast_in_dim.75), calls=%async_computation.22 | async-start | bytes 1572864 | tf_op jit(solution)/shard_map/cond/branch_2_fun/all_to_all | solution.py:34
  142.9 14.7 %copy-start.59 = (bf16[896,256]{1,0:T(8,128)(2,1)}, bf16[896,256]{1,0:T(8,128)(2,1)S(1)}, u32[]{:S(2)}) copy-start(bf16[896,256]{1,0:T(8,128)(2,1)S(1)} %collective-permute-done.32.refs_3_.refs_4_) | copy-start | bytes 1376260
  146.1 11.4 %copy-start.63 = (bf16[896,256]{1,0:T(8,128)(2,1)}, bf16[896,256]{1,0:T(8,128)(2,1)S(1)}, u32[]{:S(2)}) copy-start(bf16[896,256]{1,0:T(8,128)(2,1)S(1)} %collective-permute-done.31.refs_2_.refs_3_) | copy-start | bytes 1376260
  159.3 12.5 %all-to-all-start.23 = ((bf16[4,256,256]{2,1,0:T(8,128)(2,1)}), bf16[4,256,256]{2,1,0:T(8,128)(2,1)S(1)}, u32[]{:S(2)}, u32[]{:S(2)}) async-start(bf16[4,256,256]{2,1,0:T(8,128)(2,1)} %pad_maximum_fusion.6.refs_0_), calls=%async_computation.23 | async-start | bytes 1048576 | tf_op jit(solution)/shard_map/cond/branch_2_fun/all_to_all | solution.py:34
  162.7 3.5 %copy-start.2 = (bf16[256,512]{1,0:T(8,128)(2,1)S(1)}, bf16[256,512]{1,0:T(8,128)(2,1)}, u32[]{:S(2)}) copy-start(bf16[256,512]{1,0:T(8,128)(2,1)} %get-tuple-element.145) | copy-start | bytes 786436
  162.7 3.7 %copy-start.6 = (bf16[512,256]{1,0:T(8,128)(2,1)S(1)}, bf16[512,256]{1,0:T(8,128)(2,1)}, u32[]{:S(2)}) copy-start(bf16[512,256]{1,0:T(8,128)(2,1)} %get-tuple-element.146) | copy-start | bytes 786436
  172.3 0.7 copy-start.32
  172.3 0.7 copy-start.33
  172.3 0.7 copy-start.38
  172.3 0.7 copy-start.39
  172.3 0.7 copy-start.40
  172.3 0.8 copy-start.101
  172.4 0.9 copy-start.102
  172.4 1.0 copy-start.103
  (3 other events, 1.9 us)

commit v4 on v3

--- a/solution.py
+++ b/solution.py
@@ -219,7 +219,7 @@
 
     arrived = sent([b for b in bits if b in FIRST_A], None)
     row = jnp.sum(got.astype(f32), axis=0).astype(bf16)
-    arrived += sent([b for b in bits if b not in FIRST_A], row)
+    arrived += sent([b for b in reversed(bits) if b not in FIRST_A], row)
     (base,) = kernel_call(
         sum_products, [VM] * (4 + len(bits)), [((2, count, size), f32)], LONG, "sum_products"
     )(tokens, cotangent, w1, w2, *arrived)

time: 175 us -> 172 us (0.983)
  waiting for transfers between devices: 26.4 us -> 23 us
    ppermute x8, waiting for transfers between devices: 6.63 us -> 1.48 us  [swap_bit(): return lax.ppermute(block, 'in', [(i, i ^ 1 << bit) for i in range(count)])]
    all_to_all x8, waiting for transfers between devices: 5.13 us -> 7.23 us  [exchange(): return lax.all_to_all(parts, axes, 0, 0, tiled=True)]
  transfers between devices with their start and end apart: 19 -> 19, of which waited for: 5 -> 7; matrix products, arithmetic and copies ran while one was open for 6% -> 6% of each run, Pallas kernels for 8% -> 8%
where the time goes in v4:
time: 172 us; the launch traced here: 171 us
  starting transfers between devices  109 us (63%)
  waiting for transfers between devices  23 us (13%)
  Pallas kernels  15.9 us (9%)
  local copies, waits for them, and re-layouts  13.5 us (8%)
  other arithmetic  3.75 us (2%)
  matrix products  3.16 us (2%)
    ppermute x8, starting transfers between devices, swap_bit(): return lax.ppermute(block, 'in', [(i, i ^ 1 << bit) for i in range(count)])  50.7 us
    all_to_all x8, starting transfers between devices, exchange(): return lax.all_to_all(parts, axes, 0, 0, tiled=True)  48.6 us
    pallas_call x7, Pallas kernels, kernel_call(): return lambda *values: call(*tokens, *values)  15.9 us
    ppermute x3, waiting for transfers between devices, ring(): lax.ppermute(block, axis, [(i, (i + distance) % count) for i in range(cou...  14.3 us
    ppermute x3, starting transfers between devices, ring(): lax.ppermute(block, axis, [(i, (i + distance) % count) for i in range(cou...  9.37 us
    all_to_all x8, waiting for transfers between devices, exchange(): return lax.all_to_all(parts, axes, 0, 0, tiled=True)  7.23 us
    unnamed x68, local copies, waits for them, and re-layouts  5.99 us
    broadcast_in_dim x4, local copies, waits for them, and re-layouts, spread(): return exchange(jnp.broadcast_to(row[None], (group,) + row.shape), axes)  4.74 us
  transfers between devices with their start and end apart: 19, of which 7 were waited for; matrix products, arithmetic and copies ran while one was open for 6% of the time, Pallas kernels for 8%

profile of v4, /device:TPU:1, one launch (start us, length us, event | category | flops | bytes accessed | tf_op | source)
XLA Modules:
  0.0 170.5 jit_solution(18017625701154531318)
XLA Ops:
  0.6 1.3 reduce_sum.225
  2.6 166.9 %conditional.4 = (f32[1,1,5,64,256]{4,3,2,1,0:T(8,128)S(1)}, f32[1,1,5,64,256]{4,3,2,1,0:T(8,128)S(1)}, f32[1,256,128]{2,1,0:T(8,128)S(1)}, f32[128,256]{1,0:T(8...) conditional(s32[]{:T(128)} %clamp.3, ...), branch_computations={%region_1.7_spmd, %region_7.13_spmd, %region_13.19_spmd, %region_1... | conditional | flops 220422488064 | bytes 84731960
  2.6 1.1 convolution_convert_fusion.3
  3.8 1.1 convolution_convert_fusion.2
  4.9 0.7 pad_maximum_fusion.2
  5.6 16.8 %all-to-all-start = ((bf16[32,8,128]{2,1,0:T(8,128)(2,1)}), bf16[32,8,128]{2,1,0:T(8,128)(2,1)S(1)}, u32[]{:S(2)}, u32[]{:S(2)}) async-start(bf16[32,8,128]{2,1,0:T(8,128)(2,1)} %pad_maximum_fusion.2), calls=%async_computation | async-start | bytes 131072 | tf_op jit(solution)/shard_map/cond/branch_0_fun/all_to_all | solution.py:34
  22.4 2.3 %products.8 = bf16[2,128,256]{2,1,0:T(8,128)(2,1)} custom-call(s32[4]{0:T(128)} %get-tuple-element.100.refs_0_.refs_1_, bf16[128,256]{1,0:T(8,128)(2,1)} %get-tuple-element.96.refs_1_.refs_2_.refs_0_, bf16[128,256]{1,0:T(8,128)(2,1)} %get-tuple-element.97.refs_2_.refs_3_.refs_1_, bf16[5,256,256]{2,1,0:T(8,128)(2,1)} %bitcast.176, bf16[5,256,256]{2,1,0:T(8,128)(2,1)} %bitcast.192), custom_call_target="tpu_custom_call" | custom-call | flops 20000000000 | bytes 4194304 | tf_op jit(solution)/shard_map/cond/branch_0_fun/products/pallas_call | solution.py:65
  24.8 12.0 %collective-permute-start = (bf16[2,128,256]{2,1,0:T(8,128)(2,1)}, bf16[2,128,256]{2,1,0:T(8,128)(2,1)S(1)}, u32[]{:S(2)}, u32[]{:S(2)}) collective-permute-start(bf16[2,128,256]{2,1,0:T(8,128)(2,1)} %products.8), channel_id=1, source_target_pairs={{0,64},{4,68},{8,72},{12,76},{16,80},{20,84},{24,88},{28,92},{32,9... | collective-permute-start | bytes 393224 | tf_op jit(solution)/shard_map/cond/branch_0_fun/ppermute | solution.py:26
  36.8 0.6 broadcast_in_dim.36
  37.5 4.1 %all-to-all-start.1 = ((bf16[32,8,128]{2,1,0:T(8,128)(2,1)}), bf16[32,8,128]{2,1,0:T(8,128)(2,1)S(1)}, u32[]{:S(2)}, u32[]{:S(2)}) async-start(bf16[32,8,128]{2,1,0:T(8,128)(2,1)} %broadcast_in_dim.36), calls=%async_computation.1 | async-start | bytes 131072 | tf_op jit(solution)/shard_map/cond/branch_0_fun/all_to_all | solution.py:34
  41.7 1.5 products.9
  43.2 7.2 %collective-permute-start.1 = (bf16[2,128,256]{2,1,0:T(8,128)(2,1)}, bf16[2,128,256]{2,1,0:T(8,128)(2,1)S(1)}, u32[]{:S(2)}, u32[]{:S(2)}) collective-permute-start(bf16[2,128,256]{2,1,0:T(8,128)(2,1)} %get-tuple-element.103), channel_id=1, source_target_pairs={{0,32},{4,36},{8,40},{12,44},{16,48},{20,52},{24,56},{28,60},{32,0... | collective-permute-start | bytes 393224 | tf_op jit(solution)/shard_map/cond/branch_0_fun/ppermute | solution.py:26
  50.5 4.0 %collective-permute-start.2 = (bf16[2,128,256]{2,1,0:T(8,128)(2,1)}, bf16[2,128,256]{2,1,0:T(8,128)(2,1)S(1)}, u32[]{:S(2)}, u32[]{:S(2)}) collective-permute-start(bf16[2,128,256]{2,1,0:T(8,128)(2,1)} %get-tuple-element.104), channel_id=1, source_target_pairs={{0,16},{4,20},{8,24},{12,28},{16,0},{20,4},{24,8},{28,12},{32,48},... | collective-permute-start | bytes 393224 | tf_op jit(solution)/shard_map/cond/branch_0_fun/ppermute | solution.py:26
  54.5 3.1 %collective-permute-start.3 = (bf16[2,128,256]{2,1,0:T(8,128)(2,1)}, bf16[2,128,256]{2,1,0:T(8,128)(2,1)S(1)}, u32[]{:S(2)}, u32[]{:S(2)}) collective-permute-start(bf16[2,128,256]{2,1,0:T(8,128)(2,1)} %get-tuple-element.105), channel_id=1, source_target_pairs={{0,8},{4,12},{8,0},{12,4},{16,24},{20,28},{24,16},{28,20},{32,40},... | collective-permute-start | bytes 393224 | tf_op jit(solution)/shard_map/cond/branch_0_fun/ppermute | solution.py:26
  58.3 1.6 broadcast_in_dim.37
  59.8 4.2 %all-to-all-start.2 = ((bf16[4,32,8,128]{3,2,1,0:T(8,128)(2,1)}), bf16[4,32,8,128]{3,2,1,0:T(8,128)(2,1)S(1)}, u32[]{:S(2)}, u32[]{:S(2)}) async-start(bf16[4,32,8,128]{3,2,1,0:T(8,128)(2,1)} %broadcast_in_dim.37), calls=%async_computation.2 | async-start | bytes 524288 | tf_op jit(solution)/shard_map/cond/branch_0_fun/all_to_all | solution.py:34
  64.8 0.7 copy-done.93
  65.4 2.0 %sum_products.4.refs_0_ = f32[2,128,256]{2,1,0:T(8,128)} custom-call(bf16[128,256]{1,0:T(8,128)(2,1)S(1)} %copy-done.16, bf16[128,256]{1,0:T(8,128)(2,1)S(1)} %copy-done.20, bf16[5,256,256]{2,1,0:T(8,128)(2,1)S(1)} %bitcast.178, bf16[5,256,256]{2,1,0:T(8,128)(2,1)S(1)} %bitcast.194, bf16[2,128,256]{2,1,0:T(8,128)(2,1)} %copy-done.81, ...), custom_call_target="tpu_custom_call" | custom-call | flops 20000000000 | bytes 4194304 | tf_op jit(solution)/shard_map/cond/branch_0_fun/sum_products/pallas_call | solution.py:65
  67.4 2.1 %all-to-all-done.2 = bf16[4,32,8,128]{3,2,1,0:T(8,128)(2,1)S(1)} async-done(((bf16[4,32,8,128]{3,2,1,0:T(8,128)(2,1)}), bf16[4,32,8,128]{3,2,1,0:T(8,128)(2,1)S(1)}, u32[]{:S(2)}, u32[]{:S(2)}) %all-to-all-start.2) | async-done | bytes 262176 | tf_op jit(solution)/shard_map/cond/branch_0_fun/all_to_all | solution.py:34
  69.6 0.8 copy.61
  70.3 2.2 %activations.4 = (bf16[2,128,256]{2,1,0:T(8,128)(2,1)}, bf16[2,128,256]{2,1,0:T(8,128)(2,1)}, bf16[2,128,256]{2,1,0:T(8,128)(2,1)}, bf16[128,1024]{1,0:T(8,128)(2,1)}) custom-call(f32[2,128,256]{2,1,0:T(8,128)} %sum_products.4.refs_0_, bf16[128,1024]{1,0:T(8,128)(2,1)} %bitcast.156, bf16[512,256]{1,0:T(8,128)(2,1)S(1)} %bitcast.136, ...), custom_call_target="tpu_custom_call" | custom-call | flops 268435456 | bytes 4194304 | tf_op jit(solution)/shard_map/cond/branch_0_fun/activations/pallas_call | solution.py:65
  72.5 3.4 %all-to-all-start.3 = ((bf16[4,32,1024]{2,1,0:T(8,128)(2,1)}), bf16[4,32,1024]{2,1,0:T(8,128)(2,1)S(1)}, u32[]{:S(2)}, u32[]{:S(2)}) async-start(bf16[4,32,1024]{2,1,0:T(8,128)(2,1)} %bitcast.168), calls=%async_computation.3 | async-start | bytes 524288 | tf_op jit(solution)/shard_map/cond/branch_0_fun/all_to_all | solution.py:34
  76.0 10.0 %collective-permute-start.7 = (bf16[2,128,256]{2,1,0:T(8,128)(2,1)}, bf16[2,128,256]{2,1,0:T(8,128)(2,1)S(1)}, u32[]{:S(2)}, u32[]{:S(2)}) collective-permute-start(bf16[2,128,256]{2,1,0:T(8,128)(2,1)} %gate.22), channel_id=1, source_target_pairs={{0,64},{4,68},{8,72},{12,76},{16,80},{20,84},{24,88},{28,92},{32,9... | collective-permute-start | bytes 393224 | tf_op jit(solution)/shard_map/cond/branch_0_fun/ppermute | solution.py:26
  86.1 0.6 copy.50
  86.7 7.4 %all-to-all-start.4 = ((bf16[32,8,128]{2,1,0:T(8,128)(2,1)}), bf16[32,8,128]{2,1,0:T(8,128)(2,1)S(1)}, u32[]{:S(2)}, u32[]{:S(2)}) async-start(bf16[32,8,128]{2,1,0:T(8,128)(2,1)} %bitcast.68), calls=%async_computation.4 | async-start | bytes 131072 | tf_op jit(solution)/shard_map/cond/branch_0_fun/all_to_all | solution.py:34
  94.2 7.2 %collective-permute-start.6 = (bf16[2,128,256]{2,1,0:T(8,128)(2,1)}, bf16[2,128,256]{2,1,0:T(8,128)(2,1)S(1)}, u32[]{:S(2)}, u32[]{:S(2)}) collective-permute-start(bf16[2,128,256]{2,1,0:T(8,128)(2,1)} %gate.21), channel_id=1, source_target_pairs={{0,32},{4,36},{8,40},{12,44},{16,48},{20,52},{24,56},{28,60},{32,0... | collective-permute-start | bytes 393224 | tf_op jit(solution)/shard_map/cond/branch_0_fun/ppermute | solution.py:26
  101.4 4.0 %collective-permute-start.5 = (bf16[2,128,256]{2,1,0:T(8,128)(2,1)}, bf16[2,128,256]{2,1,0:T(8,128)(2,1)S(1)}, u32[]{:S(2)}, u32[]{:S(2)}) collective-permute-start(bf16[2,128,256]{2,1,0:T(8,128)(2,1)} %gate.21), channel_id=1, source_target_pairs={{0,16},{4,20},{8,24},{12,28},{16,0},{20,4},{24,8},{28,12},{32,48},... | collective-permute-start | bytes 393224 | tf_op jit(solution)/shard_map/cond/branch_0_fun/ppermute | solution.py:26
  105.4 3.1 %collective-permute-start.4 = (bf16[2,128,256]{2,1,0:T(8,128)(2,1)}, bf16[2,128,256]{2,1,0:T(8,128)(2,1)S(1)}, u32[]{:S(2)}, u32[]{:S(2)}) collective-permute-start(bf16[2,128,256]{2,1,0:T(8,128)(2,1)} %gate.21), channel_id=1, source_target_pairs={{0,8},{4,12},{8,0},{12,4},{16,24},{20,28},{24,16},{28,20},{32,40},... | collective-permute-start | bytes 393224 | tf_op jit(solution)/shard_map/cond/branch_0_fun/ppermute | solution.py:26
  108.6 0.6 broadcast_in_dim.38
  109.2 5.4 %all-to-all-start.5 = ((bf16[32,8,128]{2,1,0:T(8,128)(2,1)}), bf16[32,8,128]{2,1,0:T(8,128)(2,1)S(1)}, u32[]{:S(2)}, u32[]{:S(2)}) async-start(bf16[32,8,128]{2,1,0:T(8,128)(2,1)} %broadcast_in_dim.38), calls=%async_computation.5 | async-start | bytes 131072 | tf_op jit(solution)/shard_map/cond/branch_0_fun/all_to_all | solution.py:34
  115.0 0.9 collective-permute-done.4.refs_5_.refs_6_
  115.9 0.6 copy-done.77
  116.6 2.3 %block_outputs.4 = bf16[128,512]{1,0:T(8,128)(2,1)} custom-call(bf16[8,128]{1,0:T(8,128)(2,1)} %copy-done.41, s32[4]{0:T(128)S(1)} %copy-done.97, bf16[5,256,256]{2,1,0:T(8,128)(2,1)S(1)} %bitcast.179, bf16[5,256,256]{2,1,0:T(8,128)(2,1)S(1)} %bitcast.195, bf16[2,128,256]{2,1,0:T(8,128)(2,1)} %get-tuple-element.109.refs_4_.refs_5_, ...), custom_call_target="tpu_custom_call" | custom-call | flops 20000000000 | bytes 4194304 | tf_op jit(solution)/shard_map/cond/branch_0_fun/block_outputs/pallas_call | solution.py:65
  118.8 3.1 %block_grads.4.refs_1_ = bf16[4,896,256]{2,1,0:T(8,128)(2,1)} custom-call(bf16[8,128]{1,0:T(8,128)(2,1)} %copy-done.41, s32[4]{0:T(128)S(1)} %copy-done.97, bf16[128,256]{1,0:T(8,128)(2,1)S(1)} %copy-done.16, bf16[128,256]{1,0:T(8,128)(2,1)S(1)} %copy-done.20, bf16[128,1024]{1,0:T(8,128)(2,1)} %bitcast.157, ...), custom_call_target="tpu_custom_call" | custom-call | flops 20000000000 | bytes 4194304 | tf_op jit(solution)/shard_map/cond/branch_0_fun/block_grads/pallas_call | solution.py:65
  122.0 2.3 %dynamic-slice_bitcast_fusion = (bf16[896,256]{1,0:T(8,128)(2,1)S(1)}, bf16[896,256]{1,0:T(8,128)(2,1)S(1)}, bf16[896,256]{1,0:T(8,128)(2,1)S(1)}, bf16[896,256]{1,0:T(8,128)(2,1)}) fusion(bf16[4,896,256]{2,1,0:T(8,128)(2,1)} %block_grads.4.refs_1_, s32[]{:T(128)S(6)} %select_n.91, s32[]{:T(128)S(6)} %select_n.89, s32[]{:T(128)S(6)} %select_n.87, ...), kind=kLoop, calls=%fused_computation.11 | loop fusion | bytes 3670032 | tf_op jit(solution)/shard_map/cond/branch_0_fun/jit(dynamic_index_in_dim)/squeeze | solution.py:47
  124.3 4.4 %collective-permute-start.10 = (bf16[896,256]{1,0:T(8,128)(2,1)S(1)}, bf16[896,256]{1,0:T(8,128)(2,1)S(1)}, u32[]{:S(2)}, u32[]{:S(2)}) collective-permute-start(bf16[896,256]{1,0:T(8,128)(2,1)S(1)} %get-tuple-element.238), channel_id=1, source_target_pairs={{0,384},{128,0},{256,128},{384,256},{1,385},{129,1},{257,129},{385... | collective-permute-start | bytes 1376264 | tf_op jit(solution)/shard_map/cond/branch_0_fun/ppermute | solution.py:43
  128.7 2.5 %collective-permute-start.9 = (bf16[896,256]{1,0:T(8,128)(2,1)S(1)}, bf16[896,256]{1,0:T(8,128)(2,1)S(1)}, u32[]{:S(2)}, u32[]{:S(2)}) collective-permute-start(bf16[896,256]{1,0:T(8,128)(2,1)S(1)} %get-tuple-element.239), channel_id=1, source_target_pairs={{0,256},{128,384},{256,0},{384,128},{1,257},{129,385},{257,1},{385... | collective-permute-start | bytes 1376264 | tf_op jit(solution)/shard_map/cond/branch_0_fun/ppermute | solution.py:43
  131.2 2.5 %collective-permute-start.8 = (bf16[896,256]{1,0:T(8,128)(2,1)S(1)}, bf16[896,256]{1,0:T(8,128)(2,1)}, u32[]{:S(2)}, u32[]{:S(2)}) collective-permute-start(bf16[896,256]{1,0:T(8,128)(2,1)S(1)} %get-tuple-element.240), channel_id=1, source_target_pairs={{0,128},{128,256},{256,384},{384,0},{1,129},{129,257},{257,385},{3... | collective-permute-start | bytes 1376264 | tf_op jit(solution)/shard_map/cond/branch_0_fun/ppermute | solution.py:43
  133.8 0.7 pad_maximum_fusion.1.refs_0_
  134.5 1.9 %broadcast_in_dim.39 = bf16[4,384,256]{2,1,0:T(8,128)(2,1)} broadcast(bf16[384,256]{1,0:T(8,128)(2,1)} %gate.23), dimensions={1,2} | broadcast | bytes 983040 | tf_op jit(solution)/shard_map/cond/branch_0_fun/broadcast_in_dim | solution.py:38
  136.3 3.9 %all-to-all-start.6 = ((bf16[4,384,256]{2,1,0:T(8,128)(2,1)}), bf16[4,384,256]{2,1,0:T(8,128)(2,1)S(1)}, u32[]{:S(2)}, u32[]{:S(2)}) async-start(bf16[4,384,256]{2,1,0:T(8,128)(2,1)} %broadcast_in_dim.39), calls=%async_computation.6 | async-start | bytes 1572864 | tf_op jit(solution)/shard_map/cond/branch_0_fun/all_to_all | solution.py:34
  140.2 2.3 %collective-permute-done.9.refs_2_.refs_3_ = bf16[896,256]{1,0:T(8,128)(2,1)S(1)} collective-permute-done((bf16[896,256]{1,0:T(8,128)(2,1)S(1)}, bf16[896,256]{1,0:T(8,128)(2,1)S(1)}, u32[]{:S(2)}, u32[]{:S(2)}) %collective-permute-start.9) | collective-permute-done | bytes 458784 | tf_op jit(solution)/shard_map/cond/branch_0_fun/ppermute | solution.py:43
  142.5 12.0 %collective-permute-done.8.refs_1_.refs_2_ = bf16[896,256]{1,0:T(8,128)(2,1)} collective-permute-done((bf16[896,256]{1,0:T(8,128)(2,1)S(1)}, bf16[896,256]{1,0:T(8,128)(2,1)}, u32[]{:S(2)}, u32[]{:S(2)}) %collective-permute-start.8) | collective-permute-done | bytes 458784 | tf_op jit(solution)/shard_map/cond/branch_0_fun/ppermute | solution.py:43
  155.4 0.8 pad_maximum_fusion.refs_0_
  156.2 3.5 %all-to-all-start.7 = ((bf16[4,256,256]{2,1,0:T(8,128)(2,1)}), bf16[4,256,256]{2,1,0:T(8,128)(2,1)S(1)}, u32[]{:S(2)}, u32[]{:S(2)}) async-start(bf16[4,256,256]{2,1,0:T(8,128)(2,1)} %pad_maximum_fusion.refs_0_), calls=%async_computation.7 | async-start | bytes 1048576 | tf_op jit(solution)/shard_map/cond/branch_0_fun/all_to_all | solution.py:34
  159.7 2.4 %sum_grads.4 = (f32[320,256]{1,0:T(8,128)S(1)}, f32[320,256]{1,0:T(8,128)S(1)}, f32[128,256]{1,0:T(8,128)}, f32[256,128]{1,0:T(8,128)S(1)}) custom-call(bf16[4,256,256]{2,1,0:T(8,128)(2,1)} %pad_maximum_fusion.refs_0_, bf16[896,256]{1,0:T(8,128)(2,1)} %gate.24.refs_1_, bf16[896,256]{1,0:T(8,128)(2,1)} %collective-permute-done.8.refs_1_.refs_2_, ...), custom_call_target="tpu_custom_call" | custom-call | flops 20000000000 | bytes 4194304 | tf_op jit(solution)/shard_map/cond/branch_0_fun/sum_grads/pallas_call | solution.py:65
  162.1 1.0 copy.45
  163.6 5.1 %all-to-all-done.7 = bf16[4,256,256]{2,1,0:T(8,128)(2,1)S(1)} async-done(((bf16[4,256,256]{2,1,0:T(8,128)(2,1)}), bf16[4,256,256]{2,1,0:T(8,128)(2,1)S(1)}, u32[]{:S(2)}, u32[]{:S(2)}) %all-to-all-start.7) | async-done | bytes 524320 | tf_op jit(solution)/shard_map/cond/branch_0_fun/all_to_all | solution.py:34
  (99 shorter events, 4.4 us)
Async XLA Ops:
  5.6 31.2 %all-to-all-start = ((bf16[32,8,128]{2,1,0:T(8,128)(2,1)}), bf16[32,8,128]{2,1,0:T(8,128)(2,1)S(1)}, u32[]{:S(2)}, u32[]{:S(2)}) async-start(bf16[32,8,128]{2,1,0:T(8,128)(2,1)} %pad_maximum_fusion.2), calls=%async_computation | async-start | bytes 131072 | tf_op jit(solution)/shard_map/cond/branch_0_fun/all_to_all | solution.py:34
  22.4 19.3 %copy-start.16 = (bf16[128,256]{1,0:T(8,128)(2,1)S(1)}, bf16[128,256]{1,0:T(8,128)(2,1)}, u32[]{:S(2)}) copy-start(bf16[128,256]{1,0:T(8,128)(2,1)} %get-tuple-element.96.refs_1_.refs_2_.refs_0_) | copy-start | bytes 196612
  22.4 19.3 %copy-start.20 = (bf16[128,256]{1,0:T(8,128)(2,1)S(1)}, bf16[128,256]{1,0:T(8,128)(2,1)}, u32[]{:S(2)}) copy-start(bf16[128,256]{1,0:T(8,128)(2,1)} %get-tuple-element.97.refs_2_.refs_3_.refs_1_) | copy-start | bytes 196612
  22.4 19.3 %copy-start.49 = (bf16[1,1,5,256,256]{4,3,2,1,0:T(8,128)(2,1)S(1)}, bf16[1,1,5,256,256]{4,3,2,1,0:T(8,128)(2,1)}, u32[]{:S(2)}) copy-start(bf16[1,1,5,256,256]{4,3,2,1,0:T(8,128)(2,1)} %get-tuple-element.98) | copy-start | bytes 1966084
  22.4 19.3 %copy-start.53 = (bf16[1,1,5,256,256]{4,3,2,1,0:T(8,128)(2,1)S(1)}, bf16[1,1,5,256,256]{4,3,2,1,0:T(8,128)(2,1)}, u32[]{:S(2)}) copy-start(bf16[1,1,5,256,256]{4,3,2,1,0:T(8,128)(2,1)} %get-tuple-element.99) | copy-start | bytes 1966084
  22.4 19.3 %copy-start.97 = (s32[4]{0:T(128)S(1)}, s32[4]{0:T(128)}, u32[]{:S(2)}) copy-start(s32[4]{0:T(128)} %get-tuple-element.100.refs_0_.refs_1_) | copy-start | bytes 52
  24.8 39.3 %collective-permute-start = (bf16[2,128,256]{2,1,0:T(8,128)(2,1)}, bf16[2,128,256]{2,1,0:T(8,128)(2,1)S(1)}, u32[]{:S(2)}, u32[]{:S(2)}) collective-permute-start(bf16[2,128,256]{2,1,0:T(8,128)(2,1)} %products.8), channel_id=1, source_target_pairs={{0,64},{4,68},{8,72},{12,76},{16,80},{20,84},{24,88},{28,92},{32,9... | collective-permute-start | bytes 393224 | tf_op jit(solution)/shard_map/cond/branch_0_fun/ppermute | solution.py:26
  36.8 4.8 %copy-start.45 = (bf16[8,128]{1,0:T(8,128)(2,1)}, bf16[8,128]{1,0:T(8,128)(2,1)S(1)}, u32[]{:S(2)}) copy-start(bf16[8,128]{1,0:T(8,128)(2,1)S(1)} %reduce_sum.204.refs_0_) | copy-start | bytes 6148
  37.5 20.1 %all-to-all-start.1 = ((bf16[32,8,128]{2,1,0:T(8,128)(2,1)}), bf16[32,8,128]{2,1,0:T(8,128)(2,1)S(1)}, u32[]{:S(2)}, u32[]{:S(2)}) async-start(bf16[32,8,128]{2,1,0:T(8,128)(2,1)} %broadcast_in_dim.36), calls=%async_computation.1 | async-start | bytes 131072 | tf_op jit(solution)/shard_map/cond/branch_0_fun/all_to_all | solution.py:34
  43.2 20.8 %collective-permute-start.1 = (bf16[2,128,256]{2,1,0:T(8,128)(2,1)}, bf16[2,128,256]{2,1,0:T(8,128)(2,1)S(1)}, u32[]{:S(2)}, u32[]{:S(2)}) collective-permute-start(bf16[2,128,256]{2,1,0:T(8,128)(2,1)} %get-tuple-element.103), channel_id=1, source_target_pairs={{0,32},{4,36},{8,40},{12,44},{16,48},{20,52},{24,56},{28,60},{32,0... | collective-permute-start | bytes 393224 | tf_op jit(solution)/shard_map/cond/branch_0_fun/ppermute | solution.py:26
  50.5 13.6 %collective-permute-start.2 = (bf16[2,128,256]{2,1,0:T(8,128)(2,1)}, bf16[2,128,256]{2,1,0:T(8,128)(2,1)S(1)}, u32[]{:S(2)}, u32[]{:S(2)}) collective-permute-start(bf16[2,128,256]{2,1,0:T(8,128)(2,1)} %get-tuple-element.104), channel_id=1, source_target_pairs={{0,16},{4,20},{8,24},{12,28},{16,0},{20,4},{24,8},{28,12},{32,48},... | collective-permute-start | bytes 393224 | tf_op jit(solution)/shard_map/cond/branch_0_fun/ppermute | solution.py:26
  54.5 9.8 %collective-permute-start.3 = (bf16[2,128,256]{2,1,0:T(8,128)(2,1)}, bf16[2,128,256]{2,1,0:T(8,128)(2,1)S(1)}, u32[]{:S(2)}, u32[]{:S(2)}) collective-permute-start(bf16[2,128,256]{2,1,0:T(8,128)(2,1)} %get-tuple-element.105), channel_id=1, source_target_pairs={{0,8},{4,12},{8,0},{12,4},{16,24},{20,28},{24,16},{28,20},{32,40},... | collective-permute-start | bytes 393224 | tf_op jit(solution)/shard_map/cond/branch_0_fun/ppermute | solution.py:26
  59.8 9.7 %all-to-all-start.2 = ((bf16[4,32,8,128]{3,2,1,0:T(8,128)(2,1)}), bf16[4,32,8,128]{3,2,1,0:T(8,128)(2,1)S(1)}, u32[]{:S(2)}, u32[]{:S(2)}) async-start(bf16[4,32,8,128]{3,2,1,0:T(8,128)(2,1)} %broadcast_in_dim.37), calls=%async_computation.2 | async-start | bytes 524288 | tf_op jit(solution)/shard_map/cond/branch_0_fun/all_to_all | solution.py:34
  64.0 6.3 %copy-start.8 = (bf16[512,1,256]{2,0,1:T(8,128)(2,1)S(1)}, bf16[512,1,256]{2,0,1:T(8,128)(2,1)}, u32[]{:S(2)}) copy-start(bf16[512,1,256]{2,0,1:T(8,128)(2,1)} %get-tuple-element.106) | copy-start | bytes 786436
  64.0 6.3 %copy-start.12 = (bf16[1,256,512]{2,1,0:T(8,128)(2,1)S(1)}, bf16[1,256,512]{2,1,0:T(8,128)(2,1)}, u32[]{:S(2)}) copy-start(bf16[1,256,512]{2,1,0:T(8,128)(2,1)} %get-tuple-element.107) | copy-start | bytes 786436
  64.0 0.7 copy-start.81
  64.1 0.7 copy-start.85
  64.1 0.7 copy-start.89
  72.5 13.5 %all-to-all-start.3 = ((bf16[4,32,1024]{2,1,0:T(8,128)(2,1)}), bf16[4,32,1024]{2,1,0:T(8,128)(2,1)S(1)}, u32[]{:S(2)}, u32[]{:S(2)}) async-start(bf16[4,32,1024]{2,1,0:T(8,128)(2,1)} %bitcast.168), calls=%async_computation.3 | async-start | bytes 524288 | tf_op jit(solution)/shard_map/cond/branch_0_fun/all_to_all | solution.py:34
  76.0 38.7 %collective-permute-start.7 = (bf16[2,128,256]{2,1,0:T(8,128)(2,1)}, bf16[2,128,256]{2,1,0:T(8,128)(2,1)S(1)}, u32[]{:S(2)}, u32[]{:S(2)}) collective-permute-start(bf16[2,128,256]{2,1,0:T(8,128)(2,1)} %gate.22), channel_id=1, source_target_pairs={{0,64},{4,68},{8,72},{12,76},{16,80},{20,84},{24,88},{28,92},{32,9... | collective-permute-start | bytes 393224 | tf_op jit(solution)/shard_map/cond/branch_0_fun/ppermute | solution.py:26
  86.1 8.1 %copy-start.28 = (bf16[32,1024]{1,0:T(8,128)(2,1)}, bf16[32,1024]{1,0:T(8,128)(2,1)S(1)}, u32[]{:S(2)}) copy-start(bf16[32,1024]{1,0:T(8,128)(2,1)S(1)} %reduce_sum.205.refs_1_) | copy-start | bytes 196612
  86.7 21.8 %all-to-all-start.4 = ((bf16[32,8,128]{2,1,0:T(8,128)(2,1)}), bf16[32,8,128]{2,1,0:T(8,128)(2,1)S(1)}, u32[]{:S(2)}, u32[]{:S(2)}) async-start(bf16[32,8,128]{2,1,0:T(8,128)(2,1)} %bitcast.68), calls=%async_computation.4 | async-start | bytes 131072 | tf_op jit(solution)/shard_map/cond/branch_0_fun/all_to_all | solution.py:34
  94.2 20.5 %collective-permute-start.6 = (bf16[2,128,256]{2,1,0:T(8,128)(2,1)}, bf16[2,128,256]{2,1,0:T(8,128)(2,1)S(1)}, u32[]{:S(2)}, u32[]{:S(2)}) collective-permute-start(bf16[2,128,256]{2,1,0:T(8,128)(2,1)} %gate.21), channel_id=1, source_target_pairs={{0,32},{4,36},{8,40},{12,44},{16,48},{20,52},{24,56},{28,60},{32,0... | collective-permute-start | bytes 393224 | tf_op jit(solution)/shard_map/cond/branch_0_fun/ppermute | solution.py:26
  101.4 13.6 %collective-permute-start.5 = (bf16[2,128,256]{2,1,0:T(8,128)(2,1)}, bf16[2,128,256]{2,1,0:T(8,128)(2,1)S(1)}, u32[]{:S(2)}, u32[]{:S(2)}) collective-permute-start(bf16[2,128,256]{2,1,0:T(8,128)(2,1)} %gate.21), channel_id=1, source_target_pairs={{0,16},{4,20},{8,24},{12,28},{16,0},{20,4},{24,8},{28,12},{32,48},... | collective-permute-start | bytes 393224 | tf_op jit(solution)/shard_map/cond/branch_0_fun/ppermute | solution.py:26
  105.4 10.5 %collective-permute-start.4 = (bf16[2,128,256]{2,1,0:T(8,128)(2,1)}, bf16[2,128,256]{2,1,0:T(8,128)(2,1)S(1)}, u32[]{:S(2)}, u32[]{:S(2)}) collective-permute-start(bf16[2,128,256]{2,1,0:T(8,128)(2,1)} %gate.21), channel_id=1, source_target_pairs={{0,8},{4,12},{8,0},{12,4},{16,24},{20,28},{24,16},{28,20},{32,40},... | collective-permute-start | bytes 393224 | tf_op jit(solution)/shard_map/cond/branch_0_fun/ppermute | solution.py:26
  108.6 7.3 %copy-start.41 = (bf16[8,128]{1,0:T(8,128)(2,1)}, bf16[8,128]{1,0:T(8,128)(2,1)S(1)}, u32[]{:S(2)}) copy-start(bf16[8,128]{1,0:T(8,128)(2,1)S(1)} %reduce_sum.206.refs_0_) | copy-start | bytes 6148
  109.2 24.5 %all-to-all-start.5 = ((bf16[32,8,128]{2,1,0:T(8,128)(2,1)}), bf16[32,8,128]{2,1,0:T(8,128)(2,1)S(1)}, u32[]{:S(2)}, u32[]{:S(2)}) async-start(bf16[32,8,128]{2,1,0:T(8,128)(2,1)} %broadcast_in_dim.38), calls=%async_computation.5 | async-start | bytes 131072 | tf_op jit(solution)/shard_map/cond/branch_0_fun/all_to_all | solution.py:34
  114.6 1.3 copy-start.65
  114.6 1.3 copy-start.69
  115.0 0.9 copy-start.73
  118.8 3.1 %copy-start.34 = (bf16[128,512]{1,0:T(8,128)(2,1)S(1)}, bf16[128,512]{1,0:T(8,128)(2,1)}, u32[]{:S(2)}) copy-start(bf16[128,512]{1,0:T(8,128)(2,1)} %block_outputs.4) | copy-start | bytes 393220
  124.3 15.9 %collective-permute-start.10 = (bf16[896,256]{1,0:T(8,128)(2,1)S(1)}, bf16[896,256]{1,0:T(8,128)(2,1)S(1)}, u32[]{:S(2)}, u32[]{:S(2)}) collective-permute-start(bf16[896,256]{1,0:T(8,128)(2,1)S(1)} %get-tuple-element.238), channel_id=1, source_target_pairs={{0,384},{128,0},{256,128},{384,256},{1,385},{129,1},{257,129},{385... | collective-permute-start | bytes 1376264 | tf_op jit(solution)/shard_map/cond/branch_0_fun/ppermute | solution.py:43
  128.7 13.8 %collective-permute-start.9 = (bf16[896,256]{1,0:T(8,128)(2,1)S(1)}, bf16[896,256]{1,0:T(8,128)(2,1)S(1)}, u32[]{:S(2)}, u32[]{:S(2)}) collective-permute-start(bf16[896,256]{1,0:T(8,128)(2,1)S(1)} %get-tuple-element.239), channel_id=1, source_target_pairs={{0,256},{128,384},{256,0},{384,128},{1,257},{129,385},{257,1},{385... | collective-permute-start | bytes 1376264 | tf_op jit(solution)/shard_map/cond/branch_0_fun/ppermute | solution.py:43
  131.2 23.3 %collective-permute-start.8 = (bf16[896,256]{1,0:T(8,128)(2,1)S(1)}, bf16[896,256]{1,0:T(8,128)(2,1)}, u32[]{:S(2)}, u32[]{:S(2)}) collective-permute-start(bf16[896,256]{1,0:T(8,128)(2,1)S(1)} %get-tuple-element.240), channel_id=1, source_target_pairs={{0,128},{128,256},{256,384},{384,0},{1,129},{129,257},{257,385},{3... | collective-permute-start | bytes 1376264 | tf_op jit(solution)/shard_map/cond/branch_0_fun/ppermute | solution.py:43
  136.3 18.2 %all-to-all-start.6 = ((bf16[4,384,256]{2,1,0:T(8,128)(2,1)}), bf16[4,384,256]{2,1,0:T(8,128)(2,1)S(1)}, u32[]{:S(2)}, u32[]{:S(2)}) async-start(bf16[4,384,256]{2,1,0:T(8,128)(2,1)} %broadcast_in_dim.39), calls=%async_computation.6 | async-start | bytes 1572864 | tf_op jit(solution)/shard_map/cond/branch_0_fun/all_to_all | solution.py:34
  140.2 14.3 %copy-start.57 = (bf16[896,256]{1,0:T(8,128)(2,1)}, bf16[896,256]{1,0:T(8,128)(2,1)S(1)}, u32[]{:S(2)}) copy-start(bf16[896,256]{1,0:T(8,128)(2,1)S(1)} %collective-permute-done.10.refs_3_.refs_4_) | copy-start | bytes 1376260
  142.5 12.0 %copy-start.61 = (bf16[896,256]{1,0:T(8,128)(2,1)}, bf16[896,256]{1,0:T(8,128)(2,1)S(1)}, u32[]{:S(2)}) copy-start(bf16[896,256]{1,0:T(8,128)(2,1)S(1)} %collective-permute-done.9.refs_2_.refs_3_) | copy-start | bytes 1376260
  156.2 12.5 %all-to-all-start.7 = ((bf16[4,256,256]{2,1,0:T(8,128)(2,1)}), bf16[4,256,256]{2,1,0:T(8,128)(2,1)S(1)}, u32[]{:S(2)}, u32[]{:S(2)}) async-start(bf16[4,256,256]{2,1,0:T(8,128)(2,1)} %pad_maximum_fusion.refs_0_), calls=%async_computation.7 | async-start | bytes 1048576 | tf_op jit(solution)/shard_map/cond/branch_0_fun/all_to_all | solution.py:34
  159.7 3.5 %copy-start = (bf16[256,512]{1,0:T(8,128)(2,1)S(1)}, bf16[256,512]{1,0:T(8,128)(2,1)}, u32[]{:S(2)}) copy-start(bf16[256,512]{1,0:T(8,128)(2,1)} %get-tuple-element.101) | copy-start | bytes 786436
  159.7 3.7 %copy-start.4 = (bf16[512,256]{1,0:T(8,128)(2,1)S(1)}, bf16[512,256]{1,0:T(8,128)(2,1)}, u32[]{:S(2)}) copy-start(bf16[512,256]{1,0:T(8,128)(2,1)} %get-tuple-element.102) | copy-start | bytes 786436
  169.5 0.7 copy-start.32
  169.5 0.7 copy-start.33
  169.5 0.7 copy-start.38
  169.5 0.7 copy-start.39
  169.5 0.7 copy-start.40
  169.5 0.8 copy-start.101
  169.5 0.9 copy-start.102
  169.6 1.0 copy-start.103
  (3 other events, 1.9 us)
